TPU v7x, 32 devices: a whole 2x2x4 slice. The times are simulated.
32 devices in a mesh: grp: 4 (over z), ctx: 8 (over y, x, core).
Axes of the slice: x: 2, y: 2, z: 4, core: 2. Of those that a mesh axis runs over, the one named last changes fastest.
Arguments:
- inputs: bfloat16 [2, 4, 512, 1152], P(None, 'grp', 'ctx'), may hold values from -6 to 6
- segments: int32 [2, 4, 512], P(None, 'grp', 'ctx'), may hold values from 0 to 16, as said below
- query_weight: bfloat16 [1327104], P(('grp', 'ctx')), may hold values from -0.1875 to 0.1875
- key_weight: bfloat16 [442368], P(('grp', 'ctx')), may hold values from -0.1875 to 0.1875
- value_weight: bfloat16 [442368], P(('grp', 'ctx')), may hold values from -0.1875 to 0.1875
- output_weight: bfloat16 [1327104], P(('grp', 'ctx')), may hold values from -3 to 3
- gate_weight: bfloat16 [3538944], P(('grp', 'ctx')), may hold values from -0.1875 to 0.1875
- up_weight: bfloat16 [3538944], P(('grp', 'ctx')), may hold values from -0.1875 to 0.1875
- down_weight: bfloat16 [3538944], P(('grp', 'ctx')), may hold values from -0.109375 to 0.109375
- norm_gain_pair: bfloat16 [2304], P(('grp', 'ctx')), may hold values from 0.5 to 1.5
- cotangent: bfloat16 [2, 4, 512, 1152], P(None, 'grp', 'ctx'), may hold values from -6 to 6
Outputs:
- outputs: bfloat16 [2, 4, 512, 1152], P(None, 'grp', 'ctx')
- input_grad: bfloat16 [2, 4, 512, 1152], P(None, 'grp', 'ctx')
- grad_query: float32 [1327104], P(('grp', 'ctx'))
- grad_key: float32 [442368], P(('grp', 'ctx'))
- grad_value: float32 [442368], P(('grp', 'ctx'))
- grad_output: float32 [1327104], P(('grp', 'ctx'))
- grad_gate: float32 [3538944], P(('grp', 'ctx'))
- grad_up: float32 [3538944], P(('grp', 'ctx'))
- grad_down: float32 [3538944], P(('grp', 'ctx'))
- grad_gains: float32 [2304], P(('grp', 'ctx'))
Inputs may be any that keep to these rules, and one draw needn't show every extreme that they name: `segments`: segment numbers never fall along a packed sequence.
All inputs are finite; a program needn't handle non-finite values.
Results may differ from a plain program's by a relative error of at most 0.019.
Values may be sent and summed in bfloat16 or wider, within the bound.
No kernel may reach another device: no remote copies, remote signals or barrier semaphores. Data moves between devices by JAX's collectives and lax.ppermute only.
A program may use at most 256 MiB of HBM per device.

v0:
```python
import jax
import jax.numpy as jnp
from jax import lax
from jax.experimental import pallas as pl
from jax.experimental.pallas import tpu as pltpu
from jax.sharding import PartitionSpec as P

MODEL_WIDTH = 1152
QUERY_HEADS = 18
KEY_HEADS = 6
HEAD_SIZE = 64
HIDDEN_UNITS = 3072
MICRO = 2


EPS = 1e-05
THETA = 10000.0
NEGATIVE_LARGE = -1e30


def rope_parts(positions):
    half = HEAD_SIZE // 2
    freq = THETA ** (-jnp.arange(half, dtype=jnp.float32) * 2.0 / HEAD_SIZE)
    angle = positions.astype(jnp.float32)[:, None] * freq[None, :]
    return (jnp.cos(angle)[:, None, :], jnp.sin(angle)[:, None, :])


def rotary_apply(value_rows, cosine_table, sine_table, sign):
    half = value_rows.shape[-1] // 2
    first = value_rows[..., :half]
    second = value_rows[..., half:]
    return jnp.concatenate(
        [
            first * cosine_table - sign * second * sine_table,
            second * cosine_table + sign * first * sine_table,
        ],
        -1,
    )


def shape_weights(full_precision):
    return (
        full_precision[0].reshape(MODEL_WIDTH, QUERY_HEADS * HEAD_SIZE),
        full_precision[1].reshape(MODEL_WIDTH, KEY_HEADS * HEAD_SIZE),
        full_precision[2].reshape(MODEL_WIDTH, KEY_HEADS * HEAD_SIZE),
        full_precision[3].reshape(QUERY_HEADS * HEAD_SIZE, MODEL_WIDTH),
        full_precision[4].reshape(MODEL_WIDTH, HIDDEN_UNITS),
        full_precision[5].reshape(MODEL_WIDTH, HIDDEN_UNITS),
        full_precision[6].reshape(HIDDEN_UNITS, MODEL_WIDTH),
        full_precision[7],
    )


def allowed(key_pos, key_seg, query_pos, query_seg):
    return (key_pos[None, :] <= query_pos[:, None]) & (key_seg[None, :] == query_seg[:, None])


def online_step(
    state, grouped_queries, key_block, value_block, pblock, sblock, query_pos, query_seg
):
    best, total, accum = state
    block_span = key_block.shape[0]
    key_head_rows = key_block.reshape(block_span, KEY_HEADS, HEAD_SIZE)
    value_head_rows = value_block.reshape(block_span, KEY_HEADS, HEAD_SIZE)
    scores = jnp.einsum(
        "tkgd,nkd->kgtn", grouped_queries, key_head_rows, preferred_element_type=jnp.float32
    ) * HEAD_SIZE ** (-0.5)
    mask = allowed(pblock, sblock, query_pos, query_seg)[None, None]
    scores = jnp.where(mask, scores, NEGATIVE_LARGE)
    new_best = jnp.maximum(best, jnp.max(scores, axis=-1))
    factor = jnp.exp(best - new_best)
    expo = jnp.where(mask, jnp.exp(scores - new_best[..., None]), 0.0)
    total = total * factor + jnp.sum(expo, axis=-1)
    accum = accum * factor[..., None] + jnp.einsum(
        "kgtn,nkd->kgtd",
        expo.astype(jnp.bfloat16),
        value_head_rows,
        preferred_element_type=jnp.float32,
    )
    return (new_best, total, accum)


def guarded_step(
    state, grouped_queries, key_block, value_block, pblock, sblock, query_pos, query_seg
):

    def guarded_work(current):
        return online_step(
            current, grouped_queries, key_block, value_block, pblock, sblock, query_pos, query_seg
        )

    def guarded_leave(current):
        return current

    return lax.cond(pblock[0] <= query_pos[-1], guarded_work, guarded_leave, state)


def online_blocks(
    carry, grouped_queries, key_rows, value_rows, key_pos, key_seg, query_pos, query_seg
):
    count = key_rows.shape[0]
    block_size = 512 if count > 512 and count % 512 == 0 else count
    if block_size == count:
        return guarded_step(
            carry, grouped_queries, key_rows, value_rows, key_pos, key_seg, query_pos, query_seg
        )

    def step(state, block_tile):
        return (
            guarded_step(
                state,
                grouped_queries,
                block_tile[0],
                block_tile[1],
                block_tile[2],
                block_tile[3],
                query_pos,
                query_seg,
            ),
            None,
        )

    block_tiles = (
        key_rows.reshape(-1, block_size, key_rows.shape[1]),
        value_rows.reshape(-1, block_size, value_rows.shape[1]),
        key_pos.reshape(-1, block_size),
        key_seg.reshape(-1, block_size),
    )
    carry, _ = lax.scan(step, carry, block_tiles)
    return carry


def forward_rows(xrow, seg_row, query_seg, positions, cosine_table, sine_table, weight_matrices):
    (
        query_weight,
        key_weight,
        value_weight,
        output_weight,
        gate_weight,
        up_weight,
        down_weight,
        gains,
    ) = weight_matrices
    token_rows = xrow.shape[0]
    query_groups = QUERY_HEADS // KEY_HEADS
    gain_one = gains[:MODEL_WIDTH].astype(jnp.float32)
    gain_two = gains[MODEL_WIDTH:].astype(jnp.float32)
    inv_one = lax.rsqrt(jnp.mean(xrow * xrow, axis=-1, keepdims=True) + EPS)
    normed_one = xrow * inv_one
    activated_hidden = (normed_one * gain_one).astype(jnp.bfloat16)
    query_unrotated = jnp.dot(
        activated_hidden, query_weight, preferred_element_type=jnp.float32
    ).reshape(token_rows, QUERY_HEADS, HEAD_SIZE)
    key_unrotated = jnp.dot(
        activated_hidden, key_weight, preferred_element_type=jnp.float32
    ).reshape(token_rows, KEY_HEADS, HEAD_SIZE)
    value_raw = jnp.dot(activated_hidden, value_weight, preferred_element_type=jnp.float32)
    grouped_queries = (
        rotary_apply(query_unrotated, cosine_table, sine_table, 1.0)
        .astype(jnp.bfloat16)
        .reshape(token_rows, KEY_HEADS, query_groups, HEAD_SIZE)
    )
    key_rows = (
        rotary_apply(key_unrotated, cosine_table, sine_table, 1.0)
        .astype(jnp.bfloat16)
        .reshape(token_rows, KEY_HEADS * HEAD_SIZE)
    )
    value_rows = value_raw.astype(jnp.bfloat16)
    start_state = (
        jnp.full((KEY_HEADS, query_groups, token_rows), NEGATIVE_LARGE, jnp.float32),
        jnp.zeros((KEY_HEADS, query_groups, token_rows), jnp.float32),
        jnp.zeros((KEY_HEADS, query_groups, token_rows, HEAD_SIZE), jnp.float32),
    )
    piece = (
        lax.all_gather(key_rows, "ctx", axis=0, tiled=True),
        lax.all_gather(value_rows, "ctx", axis=0, tiled=True),
    )
    count = piece[0].shape[0]
    key_pos = jnp.arange(count, dtype=jnp.int32)
    best, total, accum = online_blocks(
        start_state, grouped_queries, piece[0], piece[1], key_pos, seg_row, positions, query_seg
    )
    attn = accum / total[..., None]
    lse = best + jnp.log(total)
    attn_low = (
        jnp.transpose(attn, (2, 0, 1, 3))
        .reshape(token_rows, QUERY_HEADS * HEAD_SIZE)
        .astype(jnp.bfloat16)
    )
    residual = xrow + jnp.dot(attn_low, output_weight, preferred_element_type=jnp.float32)
    inv_two = lax.rsqrt(jnp.mean(residual * residual, axis=-1, keepdims=True) + EPS)
    normed_two = residual * inv_two
    mixed = (normed_two * gain_two).astype(jnp.bfloat16)
    gate = jnp.dot(mixed, gate_weight, preferred_element_type=jnp.float32)
    upper = jnp.dot(mixed, up_weight, preferred_element_type=jnp.float32)
    hidden = (jax.nn.silu(gate) * upper).astype(jnp.bfloat16)
    result = residual + jnp.dot(hidden, down_weight, preferred_element_type=jnp.float32)
    kept = (
        inv_one,
        normed_one,
        activated_hidden,
        grouped_queries,
        key_rows,
        value_rows,
        attn,
        lse,
        attn_low,
        inv_two,
        normed_two,
        mixed,
        gate,
        upper,
        hidden,
    )
    return (result, kept)


def backward_rows(
    dout, seg_row, query_seg, positions, cosine_table, sine_table, weight_matrices, kept
):
    (
        query_weight,
        key_weight,
        value_weight,
        output_weight,
        gate_weight,
        up_weight,
        down_weight,
        gains,
    ) = weight_matrices
    (
        inv_one,
        normed_one,
        activated_hidden,
        grouped_queries,
        key_rows,
        value_rows,
        attn,
        lse,
        attn_low,
        inv_two,
        normed_two,
        mixed,
        gate,
        upper,
        hidden,
    ) = kept
    token_rows = dout.shape[0]
    query_groups = QUERY_HEADS // KEY_HEADS
    scale = HEAD_SIZE ** (-0.5)
    gain_one = gains[:MODEL_WIDTH].astype(jnp.float32)
    gain_two = gains[MODEL_WIDTH:].astype(jnp.float32)
    dout_low = dout.astype(jnp.bfloat16)
    grad_down = jnp.einsum("tf,td->fd", hidden, dout_low, preferred_element_type=jnp.float32)
    grad_hidden = jnp.einsum("td,fd->tf", dout_low, down_weight, preferred_element_type=jnp.float32)
    sigma = jax.nn.sigmoid(gate)
    grad_gate_act = (grad_hidden * upper * (sigma + gate * sigma * (1.0 - sigma))).astype(
        jnp.bfloat16
    )
    grad_up_act = (grad_hidden * (gate * sigma)).astype(jnp.bfloat16)
    grad_gate = jnp.einsum("te,tf->ef", mixed, grad_gate_act, preferred_element_type=jnp.float32)
    grad_up = jnp.einsum("te,tf->ef", mixed, grad_up_act, preferred_element_type=jnp.float32)
    grad_mixed = jnp.einsum(
        "tf,ef->te", grad_gate_act, gate_weight, preferred_element_type=jnp.float32
    ) + jnp.einsum("tf,ef->te", grad_up_act, up_weight, preferred_element_type=jnp.float32)
    grad_gain_two = jnp.sum(grad_mixed * normed_two, axis=0)
    scaled_two = grad_mixed * gain_two
    grad_res = dout + inv_two * (
        scaled_two - normed_two * jnp.mean(scaled_two * normed_two, axis=-1, keepdims=True)
    )
    grad_branch = grad_res.astype(jnp.bfloat16)
    grad_output = jnp.einsum("te,td->ed", attn_low, grad_branch, preferred_element_type=jnp.float32)
    attention_gradient = jnp.einsum(
        "td,ed->te", grad_branch, output_weight, preferred_element_type=jnp.float32
    )
    attention_gradient_reduced = attention_gradient.astype(jnp.bfloat16).reshape(
        token_rows, KEY_HEADS, query_groups, HEAD_SIZE
    )
    delta = jnp.einsum("tkgd,kgtd->kgt", attention_gradient_reduced.astype(jnp.float32), attn)
    key_rows_total, value_rows_total = (
        lax.all_gather(key_rows, "ctx", axis=0, tiled=True),
        lax.all_gather(value_rows, "ctx", axis=0, tiled=True),
    )
    token_length = key_rows_total.shape[0]
    block_size = min(512, token_length)

    def reverse_block_step(grad_query, block_tile):
        key_block, value_block, pblock, sblock = block_tile

        def reverse_work(current):
            key_head_rows = key_block.reshape(block_size, KEY_HEADS, HEAD_SIZE)
            value_head_rows = value_block.reshape(block_size, KEY_HEADS, HEAD_SIZE)
            scores = (
                jnp.einsum(
                    "tkgd,nkd->kgtn",
                    grouped_queries,
                    key_head_rows,
                    preferred_element_type=jnp.float32,
                )
                * scale
            )
            mask = allowed(pblock, sblock, positions, query_seg)[None, None]
            probs = jnp.where(mask, jnp.exp(scores - lse[..., None]), 0.0)
            grad_probs = jnp.einsum(
                "tkgd,nkd->kgtn",
                attention_gradient_reduced,
                value_head_rows,
                preferred_element_type=jnp.float32,
            )
            grad_scores = (probs * (grad_probs - delta[..., None])).astype(jnp.bfloat16)
            updated_state = current + jnp.einsum(
                "kgtn,nkd->tkgd", grad_scores, key_head_rows, preferred_element_type=jnp.float32
            )
            key_gradient_term = (
                jnp.einsum(
                    "kgtn,tkgd->nkd",
                    grad_scores,
                    grouped_queries,
                    preferred_element_type=jnp.float32,
                )
                * scale
            )
            value_gradient_term = jnp.einsum(
                "kgtn,tkgd->nkd",
                probs.astype(jnp.bfloat16),
                attention_gradient_reduced,
                preferred_element_type=jnp.float32,
            )
            return (
                updated_state,
                (
                    key_gradient_term.reshape(block_size, KEY_HEADS * HEAD_SIZE),
                    value_gradient_term.reshape(block_size, KEY_HEADS * HEAD_SIZE),
                ),
            )

        def reverse_leave(current):
            empty_state = jnp.zeros((block_size, KEY_HEADS * HEAD_SIZE), jnp.float32)
            return (current, (empty_state, empty_state))

        return lax.cond(pblock[0] <= positions[-1], reverse_work, reverse_leave, grad_query)

    places = jnp.arange(token_length, dtype=jnp.int32)
    block_tiles = (
        key_rows_total.reshape(-1, block_size, KEY_HEADS * HEAD_SIZE),
        value_rows_total.reshape(-1, block_size, KEY_HEADS * HEAD_SIZE),
        places.reshape(-1, block_size),
        seg_row.reshape(-1, block_size),
    )
    grad_query_rot, (key_gradient_terms, value_gradient_terms) = lax.scan(
        reverse_block_step,
        jnp.zeros((token_rows, KEY_HEADS, query_groups, HEAD_SIZE), jnp.float32),
        block_tiles,
    )
    key_gradient_rows, grad_values = (
        lax.psum_scatter(
            key_gradient_terms.reshape(token_length, KEY_HEADS * HEAD_SIZE),
            "ctx",
            scatter_dimension=0,
            tiled=True,
        ),
        lax.psum_scatter(
            value_gradient_terms.reshape(token_length, KEY_HEADS * HEAD_SIZE),
            "ctx",
            scatter_dimension=0,
            tiled=True,
        ),
    )
    grad_q_low = (
        rotary_apply(
            (grad_query_rot * scale).reshape(token_rows, QUERY_HEADS, HEAD_SIZE),
            cosine_table,
            sine_table,
            -1.0,
        )
        .astype(jnp.bfloat16)
        .reshape(token_rows, QUERY_HEADS * HEAD_SIZE)
    )
    grad_k_low = (
        rotary_apply(
            key_gradient_rows.reshape(token_rows, KEY_HEADS, HEAD_SIZE),
            cosine_table,
            sine_table,
            -1.0,
        )
        .astype(jnp.bfloat16)
        .reshape(token_rows, KEY_HEADS * HEAD_SIZE)
    )
    grad_v_low = grad_values.astype(jnp.bfloat16)
    grad_wq = jnp.einsum(
        "te,tf->ef", activated_hidden, grad_q_low, preferred_element_type=jnp.float32
    )
    grad_wk = jnp.einsum(
        "te,tf->ef", activated_hidden, grad_k_low, preferred_element_type=jnp.float32
    )
    grad_wv = jnp.einsum(
        "te,tf->ef", activated_hidden, grad_v_low, preferred_element_type=jnp.float32
    )
    grad_acted = jnp.einsum(
        "tf,ef->te", grad_q_low, query_weight, preferred_element_type=jnp.float32
    )
    grad_acted = grad_acted + jnp.einsum(
        "tf,ef->te", grad_k_low, key_weight, preferred_element_type=jnp.float32
    )
    grad_acted = grad_acted + jnp.einsum(
        "tf,ef->te", grad_v_low, value_weight, preferred_element_type=jnp.float32
    )
    grad_gain_one = jnp.sum(grad_acted * normed_one, axis=0)
    scaled_one = grad_acted * gain_one
    grad_input = grad_res + inv_one * (
        scaled_one - normed_one * jnp.mean(scaled_one * normed_one, axis=-1, keepdims=True)
    )
    terms = [
        grad_wq.reshape(-1),
        grad_wk.reshape(-1),
        grad_wv.reshape(-1),
        grad_output.reshape(-1),
        grad_gate.reshape(-1),
        grad_up.reshape(-1),
        grad_down.reshape(-1),
        jnp.concatenate([grad_gain_one, grad_gain_two]),
    ]
    return (grad_input.astype(jnp.bfloat16), terms)


def local(
    inputs,
    segments,
    query_weight,
    key_weight,
    value_weight,
    output_weight,
    gate_weight,
    up_weight,
    down_weight,
    norm_gain_pair,
    cotangent,
):
    shard_rows = inputs.shape[2]
    seg_full = lax.all_gather(segments, "ctx", axis=2, tiled=True)
    positions = lax.axis_index("ctx") * shard_rows + jnp.arange(shard_rows, dtype=jnp.int32)
    cosine_table, sine_table = rope_parts(positions)
    weight_matrices = shape_weights(
        (
            lax.all_gather(query_weight, ("grp", "ctx"), axis=0, tiled=True),
            lax.all_gather(key_weight, ("grp", "ctx"), axis=0, tiled=True),
            lax.all_gather(value_weight, ("grp", "ctx"), axis=0, tiled=True),
            lax.all_gather(output_weight, ("grp", "ctx"), axis=0, tiled=True),
            lax.all_gather(gate_weight, ("grp", "ctx"), axis=0, tiled=True),
            lax.all_gather(up_weight, ("grp", "ctx"), axis=0, tiled=True),
            lax.all_gather(down_weight, ("grp", "ctx"), axis=0, tiled=True),
            lax.all_gather(norm_gain_pair, ("grp", "ctx"), axis=0, tiled=True),
        )
    )
    results = []
    saved = []
    for micro_step in range(MICRO):
        xrow = inputs[micro_step, 0].astype(jnp.float32)
        result, kept = forward_rows(
            xrow,
            seg_full[micro_step, 0],
            segments[micro_step, 0],
            positions,
            cosine_table,
            sine_table,
            weight_matrices,
        )
        results.append(result.astype(jnp.bfloat16))
        saved.append(kept)
    mats_back = shape_weights(
        (
            lax.all_gather(query_weight, ("grp", "ctx"), axis=0, tiled=True),
            lax.all_gather(key_weight, ("grp", "ctx"), axis=0, tiled=True),
            lax.all_gather(value_weight, ("grp", "ctx"), axis=0, tiled=True),
            lax.all_gather(output_weight, ("grp", "ctx"), axis=0, tiled=True),
            lax.all_gather(gate_weight, ("grp", "ctx"), axis=0, tiled=True),
            lax.all_gather(up_weight, ("grp", "ctx"), axis=0, tiled=True),
            lax.all_gather(down_weight, ("grp", "ctx"), axis=0, tiled=True),
            lax.all_gather(norm_gain_pair, ("grp", "ctx"), axis=0, tiled=True),
        )
    )
    input_grads = []
    shares = None
    totals = None
    for micro_step in range(MICRO):
        dout = cotangent[micro_step, 0].astype(jnp.float32)
        grad_input, terms = backward_rows(
            dout,
            seg_full[micro_step, 0],
            segments[micro_step, 0],
            positions,
            cosine_table,
            sine_table,
            mats_back,
            saved[micro_step],
        )
        input_grads.append(grad_input)
        totals = terms if totals is None else [a + b for a, b in zip(totals, terms)]
    shares = list(
        (
            lax.psum_scatter(totals[0], ("grp", "ctx"), scatter_dimension=0, tiled=True),
            lax.psum_scatter(totals[1], ("grp", "ctx"), scatter_dimension=0, tiled=True),
            lax.psum_scatter(totals[2], ("grp", "ctx"), scatter_dimension=0, tiled=True),
            lax.psum_scatter(totals[3], ("grp", "ctx"), scatter_dimension=0, tiled=True),
            lax.psum_scatter(totals[4], ("grp", "ctx"), scatter_dimension=0, tiled=True),
            lax.psum_scatter(totals[5], ("grp", "ctx"), scatter_dimension=0, tiled=True),
            lax.psum_scatter(totals[6], ("grp", "ctx"), scatter_dimension=0, tiled=True),
            lax.psum_scatter(totals[7], ("grp", "ctx"), scatter_dimension=0, tiled=True),
        )
    )
    outputs = jnp.stack(results)[:, None]
    input_grad = jnp.stack(input_grads)[:, None]
    return (
        outputs,
        input_grad,
        shares[0],
        shares[1],
        shares[2],
        shares[3],
        shares[4],
        shares[5],
        shares[6],
        shares[7],
    )


W = MODEL_WIDTH
HG = QUERY_HEADS // KEY_HEADS * HEAD_SIZE
QK = HG + HEAD_SIZE
SLAB = 384
QKV = HG + 2 * HEAD_SIZE
OUT = W // 8
BACK = 512
FEED = 432
EDGE = 304
CHUNK = W // 32
HID = HIDDEN_UNITS // 8
SUB = HIDDEN_UNITS // 32
ROWS = 128
ALL = 8 * ROWS
POS = 64
LEN = 512
RELATIVE = (0, 2, 4, 6, 1, 3, 5, 7)
F32 = jnp.float32
BF16 = jnp.bfloat16
SCALE = HEAD_SIZE ** (-0.5)
NT = (((1,), (1,)), ((), ()))
TN = (((0,), (0,)), ((), ()))
MIB = 1024 * 1024


def pc(value, k):
    return lax.ppermute(value, "ctx", [(s, s ^ k) for s in range(8)])


def pz(value, k):
    return lax.ppermute(value, "grp", [(s, s ^ k) for s in range(4)])


def after(value, *others):
    return lax.optimization_barrier((value,) + others)[0]


def first_ctx(value):
    far = pc(value, 6)
    return [value, pc(value, 2), pc(value, 4), far]


def both_cores(mine):
    return mine + [pc(m, 1) for m in mine]


def gather_ctx(value):
    return both_cores(first_ctx(value))


def gather_grp(value):
    one = pz(value, 1)
    two = pz(value, 2)
    return (value, one, two, pz(two, 1))


def add_low(a, b):
    return (a.astype(F32) + b.astype(F32)).astype(BF16)


class Order:
    def __init__(self):
        self.last = None

    def __call__(self, values):
        return values if self.last is None else after(values, self.last)

    def then(self, result):
        self.last = jax.tree.leaves(result)[-1]
        return result

    def wait(self, values):
        return self.then(self(values))


def scatter_ctx(even, got):
    return [add_low(even[k], got[k]) for k in range(4)]


def send_ctx(sums):
    far = pc(sums[3], 6)
    return sums[0], pc(sums[1], 2), pc(sums[2], 4), far


def pick(blocks, g):
    return [lax.dynamic_index_in_dim(blocks, g ^ k, 0, keepdims=False) for k in range(4)]


def call(body, outs, *args, grid=None, in_specs=None, out_specs=None, scratch=(), name=None):
    kwargs = {}
    if grid is not None:
        kwargs = dict(grid=grid, in_specs=in_specs, out_specs=out_specs)
    else:
        kwargs = dict(
            in_specs=[
                pl.BlockSpec(memory_space=pltpu.SMEM)
                if a.dtype == jnp.int32 and a.ndim == 1
                else pl.BlockSpec(memory_space=pltpu.VMEM)
                for a in args
            ],
            out_specs=out_specs or [pl.BlockSpec(memory_space=pltpu.VMEM) for _ in outs],
        )
    return pl.pallas_call(
        body,
        out_shape=outs,
        scratch_shapes=scratch,
        compiler_params=pltpu.CompilerParams(vmem_limit_bytes=32 * MIB),
        cost_estimate=pl.CostEstimate(flops=0, bytes_accessed=1, transcendentals=0),
        name=name,
        **kwargs,
    )(*args)


def late(values):
    return [pltpu.with_memory_space_constraint(v, pltpu.HBM) for v in values]


def hbm(shape, dtype):
    return pltpu.HBM(shape, dtype)


def hbm(shape, dtype):
    return pltpu.HBM(shape, dtype)


def hbm(shape, dtype):
    return pltpu.HBM(shape, dtype)


def sds(shape, dtype):
    return jax.ShapeDtypeStruct(shape, dtype)


def rows_of(ref, count):
    wide = ref.shape[0] // count
    return jnp.concatenate([ref[pl.ds(n, count, stride=wide), :] for n in range(wide)], 1)


def store_rows(ref, rows):
    count = rows.shape[0]
    wide = ref.shape[0] // count
    for n in range(wide):
        ref[pl.ds(n, count, stride=wide), :] = rows[:, n * 128 : (n + 1) * 128]


def pack_body(q_r, k_r, v_r, gate_r, up_r, gain, out, sq, sk, sv, sg, su):
    for src, dst in ((q_r, sq), (k_r, sk), (v_r, sv), (gate_r, sg), (up_r, su)):
        dst[...] = src[...].astype(F32)
    q, k, v, gate, up = (rows_of(s, CHUNK) for s in (sq, sk, sv, sg, su))
    tail = jnp.concatenate([gain[:, n * SLAB : (n + 1) * SLAB] for n in range(3)], 0).astype(F32)
    tail = jnp.concatenate([tail, jnp.zeros((1, SLAB), F32)], 0)
    for h in range(8):
        if h < KEY_HEADS:
            rows = jnp.concatenate(
                [
                    q[:, h * HG : (h + 1) * HG],
                    k[:, h * HEAD_SIZE : (h + 1) * HEAD_SIZE],
                    v[:, h * HEAD_SIZE : (h + 1) * HEAD_SIZE],
                    jnp.zeros((CHUNK, SLAB - QKV), F32),
                ],
                1,
            )
        else:
            rows = jnp.zeros((CHUNK, SLAB), F32)
        out[h, :, :SLAB] = jnp.concatenate([rows, tail], 0).astype(BF16)
        parts = [
            full[:, z * 768 + h * SUB : z * 768 + (h + 1) * SUB] for full in (gate, up) for z in range(4)
        ]
        rows = jnp.concatenate([jnp.concatenate(parts, 1), jnp.zeros((4, 2 * HID), F32)], 0)
        out[h, :, SLAB:] = rows.astype(BF16)


def unpack_body(src, slab, feed):
    for h in range(8):
        slab[h] = src[h, :, :SLAB]
    feed[...] = jnp.concatenate([src[h, :CHUNK, SLAB:].astype(F32) for h in range(8)], 0).astype(BF16)


def join_body(*refs):
    for n, block in enumerate(refs[:8]):
        refs[8][n * ROWS : (n + 1) * ROWS, :] = block[...]


def join(blocks):
    return call(join_body, [sds((ALL, W), BF16)], *blocks, name="join")[0]


def output_weight_body(sc, b0, b1, b2, b3, b4, b5, b6, b7, out, rows):
    i, g = sc[0], sc[1]
    for j, b in zip(RELATIVE, (b0, b1, b2, b3, b4, b5, b6, b7)):
        for k in range(4):
            rows[i ^ j, g ^ k] = b[k].astype(F32)
    for z in range(4):
        for q in range(2):
            parts = [rows_of(rows.at[c, z], CHUNK) for c in range(4 * q, 4 * q + 4)]
            start = z * 288 + q * 144
            out[start : start + 144, :] = jnp.concatenate(parts, 0).astype(BF16)


def rotate(x, cosine, sine, sign):
    lane = lax.broadcasted_iota(jnp.int32, (1, 128), 1) % HEAD_SIZE
    first = lane < HEAD_SIZE // 2
    halves = []
    for n in range(x.shape[1] // 128):
        part = x[:, n * 128 : (n + 1) * 128]
        swapped = jnp.where(first, pltpu.roll(part, 96, 1), pltpu.roll(part, 32, 1))
        halves.append(part * cosine + sign * (swapped * sine))
    return jnp.concatenate(halves, 1)


def attend_body(
    sc, x0, x1, x2, x3, x4, x5, x6, x7, w0, w1, w2, w3, cosine, sine, pcol, prow,
    att, gains, w_o, qk_h, v_h, acted_h, probs_h, x_h, qk_o, v_o, acted, probs, x_o, segs, held, sems,
):
    xs = (x0, x1, x2, x3, x4, x5, x6, x7)
    g = sc[1]
    copies = []

    def send(src, dst):
        copy = pltpu.make_async_copy(src, dst, sems.at[len(copies)])
        copy.start()
        copies.append(copy)

    sums = [jnp.zeros((3, SLAB), F32), jnp.zeros((3, SLAB), F32)]
    for k, w in enumerate((w0, w1, w2, w3)):
        z = g ^ k
        block = jnp.concatenate([w[h, :CHUNK, :].astype(F32) for h in range(8)], 0)
        w_o[pl.ds(pl.multiple_of(z * 288, 32), 288), :] = block.astype(BF16)
        rows = sum(w[h, CHUNK : CHUNK + 3, :].astype(F32) for h in range(8))
        sums[0] = sums[0] + jnp.where(z < 2, rows, 0.0)
        sums[1] = sums[1] + jnp.where(z < 2, 0.0, rows)
    gain = [jnp.concatenate([s[0:1], s[1:2], s[2:3]], 1) for s in sums]
    gains[...] = jnp.concatenate([gain[0], gain[1], jnp.zeros((6, W), F32)], 0)
    for b in range(8):
        x_o[b * ROWS : (b + 1) * ROWS, :] = xs[b][:, :W]
        segs[b] = xs[b][:, W:]

    @pl.loop(0, 8)
    def _(b):
        at = pl.ds(pl.multiple_of(b * ROWS, ROWS), ROWS)
        x = x_o[at, :].astype(F32)
        inv = lax.rsqrt(jnp.mean(x * x, axis=-1, keepdims=True) + EPS)
        acted[at, :] = (x * inv * gain[0]).astype(BF16)

    send(x_o, x_h)
    send(acted, acted_h)

    @pl.loop(0, MICRO)
    def _(m):
        part = pl.ds(pl.multiple_of(m * POS, POS), POS)
        rows = jnp.concatenate(
            [acted[pl.ds(pl.multiple_of(b * ROWS + m * POS, POS), POS), :] for b in range(8)], 0
        )
        seg = jnp.concatenate([segs[b, part, :].astype(F32) for b in range(8)], 0)
        y = jnp.dot(rows, w_o[...], preferred_element_type=F32)
        qk = rotate(y[:, :QK], cosine[...], sine[...], 1.0).astype(BF16)
        v = y[:, QK:].astype(BF16)
        qk_o[m] = qk
        v_o[m] = v
        seg_row = jnp.transpose(seg)[0:1, :]
        mask = (prow[0:1, :] <= pcol[:, 0:1]) & (seg_row == seg[:, 0:1])
        bias = jnp.where(mask, 0.0, NEGATIVE_LARGE)
        keys = qk[:, HG:]
        for h in range(3):
            s = lax.dot_general(
                qk[:, h * HEAD_SIZE : (h + 1) * HEAD_SIZE], keys, NT, preferred_element_type=F32
            )
            s = s * SCALE + bias
            e = jnp.exp(s - jnp.max(s, axis=-1, keepdims=True))
            p = (e * (1.0 / jnp.sum(e, axis=-1, keepdims=True))).astype(BF16)
            probs[m, h] = p
            held[m, :, h * HEAD_SIZE : (h + 1) * HEAD_SIZE] = jnp.dot(
                p, v[:, :HEAD_SIZE], preferred_element_type=F32
            ).astype(BF16)

    for m in range(MICRO):
        att[:, m * HG : (m + 1) * HG] = held[m]
    send(probs, probs_h)
    send(qk_o, qk_h)
    send(v_o, v_h)
    for copy in copies:
        copy.wait()


def project_body(sc, x, a0, a1, a2, a3, a4, a5, a6, a7, wo, gains, att_o, mixed_o, res_o, heads):
    i = sc[0]
    t = pl.program_id(0)
    for j, a in zip(RELATIVE, (a0, a1, a2, a3, a4, a5, a6, a7)):
        h = i ^ j
        for half in range(2):
            b = 2 * t + half
            q = (2 * (b & 3) + (b >> 2)) ^ j
            start = pl.multiple_of(((q & 1) * 4 + (q >> 1)) * POS, POS)
            rows = a[pl.ds(start, POS), :]
            for m in range(MICRO):
                heads[h, half * ROWS + m * POS : half * ROWS + (m + 1) * POS, :] = rows[:, m * HG : (m + 1) * HG]
    for h in range(KEY_HEADS):
        att_o[:, h * HG : (h + 1) * HG] = heads[h]
    residual = x[...].astype(F32) + jnp.dot(att_o[...], wo[...], preferred_element_type=F32)

    @pl.when(t == 0)
    def _():
        res_o[...] = residual[:ROWS]

    inv = lax.rsqrt(jnp.mean(residual * residual, axis=-1, keepdims=True) + EPS)
    mixed_o[...] = (residual * inv * gains[1:2, :]).astype(BF16)


def feed_body(
    sc, mixed_r, c, g0, g1, g2, g3, d0, d1, d2, d3, hidden_o, dgu_o, pm, pe, dn, sums, gu
):
    g = sc[1]
    t = pl.program_id(0)

    @pl.when(t == 0)
    def _():
        for k, (a, d) in enumerate(((g0, d0), (g1, d1), (g2, d2), (g3, d3))):
            z = g ^ k
            gu[pl.ds(pl.multiple_of(z * 288, 32), 288), :] = a[...]
            dn[pl.ds(pl.multiple_of(z * SUB, 32), SUB), :] = d[...]
        sums[...] = jnp.zeros((8, W), F32)

    mixed = mixed_r[...]
    y = jnp.dot(mixed, gu[...], preferred_element_type=F32)
    gate = y[:, :HID]
    up = y[:, HID:]
    sig = 1.0 / (1.0 + jnp.exp(-gate))
    silu = gate * sig
    hidden_o[...] = (silu * up).astype(BF16)
    dh = lax.dot_general(c[...], dn[...], NT, preferred_element_type=F32)
    dgate = (dh * up * (sig + silu * (1.0 - sig))).astype(BF16)
    dup = (dh * silu).astype(BF16)
    dgu = jnp.concatenate([dgate, dup], 1)
    dgu_o[...] = dgu
    dm = lax.dot_general(dgu, gu[...], NT, preferred_element_type=F32)
    sums[0:1, :] = sums[0:1, :] + jnp.sum(dm * mixed.astype(F32), axis=0, keepdims=True)
    dm = dm.astype(BF16).reshape(2, ROWS, W)

    @pl.when(t < 2)
    def _():
        pm[...] = dm

    @pl.when(t >= 2)
    def _():
        pe[...] = dm


def mid_body(a, b, d, f, c, res, gains, dres, low):
    dm = a[...].astype(F32) + b[...].astype(F32) + d[...].astype(F32) + f[...].astype(F32)
    r = res[...]
    inv = lax.rsqrt(jnp.mean(r * r, axis=-1, keepdims=True) + EPS)
    n = r * inv
    e = dm * gains[1:2, :]
    out = c[...].astype(F32) + inv * (e - n * jnp.mean(e * n, axis=-1, keepdims=True))
    dres[...] = out
    low[...] = out.astype(BF16)


def last_body(a, b, d, f, x, dres, gains, out):
    da = a[...].astype(F32) + b[...].astype(F32) + d[...].astype(F32) + f[...].astype(F32)
    r = x[...].astype(F32)
    inv = lax.rsqrt(jnp.mean(r * r, axis=-1, keepdims=True) + EPS)
    n = r * inv
    e = da * gains[0:1, :]
    out[...] = (dres[...] + inv * (e - n * jnp.mean(e * n, axis=-1, keepdims=True))).astype(BF16)


def back_body(
    sc, l0, l1, l2, l3, l4, l5, l6, l7, wo, qk_r, v_r, probs, cosine, sine, acted_t, att_t, w_slab, gains, sums,
    out, b0, b1, b2, b3, columns, dots, edge,
):
    lows = (l0, l1, l2, l3, l4, l5, l6, l7)
    i, g = sc[0], sc[1]
    place = lax.broadcasted_iota(jnp.int32, (256, W), 1) - lax.broadcasted_iota(jnp.int32, (256, W), 0)
    chosen = jnp.where(place == i * OUT, 1.0, 0.0).astype(BF16)
    @pl.loop(0, MICRO)
    def _(m):
        part = pl.ds(pl.multiple_of(m * POS, POS), POS)
        rows = jnp.concatenate([lows[b][part, :] for b in range(8)], 0)
        datt = lax.dot_general(rows, wo[...], NT, preferred_element_type=F32).astype(BF16)
        chosen_rows = lax.dot_general(rows, chosen, NT, preferred_element_type=F32).astype(BF16)
        qk = qk_r[m]
        keys = qk[:, HG:]
        v = v_r[m][:, :HEAD_SIZE]
        dq = []
        dk = jnp.zeros((HEAD_SIZE, LEN), F32)
        dv = jnp.zeros((HEAD_SIZE, LEN), F32)
        for h in range(3):
            da = datt[:, h * HEAD_SIZE : (h + 1) * HEAD_SIZE]
            q = qk[:, h * HEAD_SIZE : (h + 1) * HEAD_SIZE]
            low = probs[m, h]
            p = low.astype(F32)
            dp = lax.dot_general(da, v, NT, preferred_element_type=F32)
            delta = jnp.sum(p * dp, axis=-1, keepdims=True)
            ds = (p * (dp - delta)).astype(BF16)
            dq.append(jnp.dot(ds, keys, preferred_element_type=F32))
            dk = dk + lax.dot_general(q, ds, TN, preferred_element_type=F32)
            dv = dv + lax.dot_general(da, low, TN, preferred_element_type=F32)
        dqk = jnp.concatenate(dq + [jnp.transpose(dk)], 1) * SCALE
        dqk = rotate(dqk, cosine[...], sine[...], -1.0)
        dvt = jnp.transpose(jnp.concatenate([dv, jnp.zeros((HEAD_SIZE, LEN), F32)], 0))
        full = jnp.concatenate([dqk, dvt], 1).astype(BF16)
        for b in range(8):
            at = pl.ds(pl.multiple_of(b * ROWS + m * POS, POS), POS)
            out[at, :] = full[b * POS : (b + 1) * POS, :]
            columns[at, :] = chosen_rows[b * POS : (b + 1) * POS, :]

    blocks = (b0, b1, b2, b3)
    for k in range(4):
        z = g ^ k
        start = pl.multiple_of(z * 288, 32)
        y = jnp.dot(acted_t[pl.ds(start, 288), :], out[...], preferred_element_type=F32)
        yo = jnp.dot(att_t[pl.ds(start, 288), :], columns[...], preferred_element_type=F32)
        y2 = jnp.concatenate([y[:, :QKV], yo[:, : BACK - QKV]], 1)
        blocks[k][:288, :] = y2.astype(BF16)
        dot = jnp.sum(y * w_slab[pl.ds(start, 288), :].astype(F32), axis=-1, keepdims=True)
        dots[z] = jnp.transpose(jnp.broadcast_to(dot, (288, 128)))[:8, :]
    one = jnp.concatenate([dots[z][0:1, :] for z in range(4)], 1) / gains[0:1, :]
    two = sums[0:1, :] / gains[1:2, :]
    for z in range(4):
        full = one if z < 2 else two
        at = (z % 2) * 576
        rows = jnp.concatenate([full[:, at + 72 * c : at + 72 * (c + 1)] for c in range(8)], 0)
        rows = jnp.concatenate([rows, jnp.zeros((8, BACK - 72), F32)], 1)
        edge[z] = jnp.concatenate([rows, jnp.zeros((EDGE - 288 - 8, BACK), F32)], 0)
    for k in range(4):
        blocks[k][288:, :] = edge[g ^ k].astype(BF16)


def split_back_body(a, b, d, out):
    rows = a[...].astype(F32) + b[...].astype(F32) + d[...].astype(F32)
    for h in range(8):
        block = [rows[h * CHUNK : (h + 1) * CHUNK, :], rows[288 + h : 289 + h, :], jnp.zeros((3, BACK), F32)]
        out[h] = jnp.concatenate(block, 0).astype(BF16)


def grads_body(sc, grad_gu, grad_dn, b0, b1, b2, b3):
    g = sc[1]
    for k, block in enumerate((b0, b1, b2, b3)):
        z = g ^ k
        block[:288, :] = grad_gu[pl.ds(pl.multiple_of(z * 288, 32), 288), :]
        start = pl.multiple_of(z * SUB, 32)
        block[288 : 288 + SUB, :] = grad_dn[pl.ds(start, SUB), :768]
        block[288 + SUB :, :HID] = grad_dn[pl.ds(start, SUB // 2), 768:]
        block[288 + SUB :, HID:] = grad_dn[pl.ds(pl.multiple_of(start + SUB // 2, 16), SUB // 2), 768:]


def transpose_body(src, out):
    for n in range(ALL // 256):
        for m in range(W // 384):
            block = src[n * 256 : (n + 1) * 256, m * 384 : (m + 1) * 384]
            out[m * 384 : (m + 1) * 384, n * 256 : (n + 1) * 256] = jnp.transpose(block)


def transpose(value):
    return call(transpose_body, [sds((W, ALL), BF16)], value, name="transpose")[0]


def onward_body(rows, weight, even, odd):
    dims = NT if weight.shape[0] == W else (((1,), (0,)), ((), ()))
    for n in range(4):
        part = rows[n * 2 * ROWS : (n + 1) * 2 * ROWS, :]
        y = lax.dot_general(part, weight[...], dims, preferred_element_type=F32).astype(BF16)
        out = even if n < 2 else odd
        out[2 * (n % 2)] = y[:ROWS]
        out[2 * (n % 2) + 1] = y[ROWS:]


def onward(rows, weight, name):
    return call(onward_body, [sds((4, ROWS, W), BF16)] * 2, rows, weight, name=name)


def split_feed_body(a, b, d, out, down):
    rows = a[...].astype(F32) + b[...].astype(F32) + d[...].astype(F32)
    for h in range(8):
        out[h] = rows[h * CHUNK : (h + 1) * CHUNK, :].astype(BF16)
    right = jnp.concatenate([rows[288 + SUB :, :HID], rows[288 + SUB :, HID:]], 0)
    store_rows(down, jnp.concatenate([rows[288 : 288 + SUB, :], right], 1))


def split_back_body(a, b, d, out):
    rows = a[...].astype(F32) + b[...].astype(F32) + d[...].astype(F32)
    for h in range(8):
        block = [rows[h * CHUNK : (h + 1) * CHUNK, :], rows[288 + h : 289 + h, :], jnp.zeros((3, BACK), F32)]
        out[h] = jnp.concatenate(block, 0).astype(BF16)


def unpack_back_body(src, q, k, v, o, gains):
    parts = [src[h].astype(F32) for h in range(8)]
    rows = [p[:CHUNK, :] for p in parts]
    store_rows(q, jnp.concatenate([p[:, :HG] for p in rows[:KEY_HEADS]], 1))
    store_rows(k, jnp.concatenate([p[:, HG:QK] for p in rows[:KEY_HEADS]], 1))
    store_rows(v, jnp.concatenate([p[:, QK:QKV] for p in rows[:KEY_HEADS]], 1))
    store_rows(o, jnp.concatenate([p[:, QKV : QKV + OUT] for p in rows], 1))
    gains[...] = jnp.broadcast_to(sum(p[CHUNK : CHUNK + 1, :128] for p in parts), (8, 128))


def unpack_hidden_body(src, gate, up):
    for n, out in enumerate((gate, up)):
        parts = [
            src[h, :, n * HID + z * SUB : n * HID + (z + 1) * SUB].astype(F32)
            for z in range(4)
            for h in range(8)
        ]
        store_rows(out, jnp.concatenate(parts, 1))


def fast_local(inputs, segments, wq, wk, wv, wo, wg, wu, wd, gain_pair, cotangent):
    i = lax.axis_index("ctx").astype(jnp.int32)
    g = lax.axis_index("grp").astype(jnp.int32)
    r = g * 8 + i
    sc = jnp.stack([i, g])
    x_own = inputs.reshape(ROWS, W)
    c_own = cotangent.reshape(ROWS, W)
    order = Order()

    q2, k2, v2, gate2, up2 = (w.reshape(-1, 128) for w in (wq, wk, wv, wg, wu))
    placed = lax.dynamic_update_slice(jnp.zeros((1, W), BF16), gain_pair[None, :], (0, (r % 16) * 72))
    packed = order.then(
        call(
            pack_body,
            [sds((8, 40, SLAB + 2 * HID), BF16)],
            *late([q2, k2, v2, gate2, up2]), placed,
            scratch=[pltpu.VMEM(a.shape, F32) for a in (q2, k2, v2, gate2, up2)], name="pack",
        )
    )[0]
    packed = lax.all_to_all(packed, "ctx", 0, 0, tiled=True)

    x_late, seg_late, wo, wd, i_late, c_late = order((x_own, segments, wo, wd, i, c_own))
    o_own = wo.reshape(-1, 128)
    o_one, o_two = pz(o_own, 1), pz(o_own, 2)
    seg = jnp.broadcast_to(seg_late.reshape(ROWS, 1).astype(BF16), (ROWS, 128))
    x_sent = order.then(jnp.concatenate([x_late, seg], 1))
    d_own = order.then(order(wd).reshape(SUB, W))
    packed, o_one, o_two = order.wait((packed, o_one, o_two))

    slab, feed = order.then(
        call(unpack_body, [sds((8, 40, SLAB), BF16), sds((288, 2 * HID), BF16)], packed, name="unpack")
    )
    s_one, s_two = pz(slab, 1), pz(slab, 2)
    xs = first_ctx(order(x_sent))

    i_late = order(i_late)
    rel = jnp.array(RELATIVE, jnp.int32)
    positions = ((i_late ^ rel)[:, None] * POS + jnp.arange(POS, dtype=jnp.int32)[None, :]).reshape(LEN)
    half = HEAD_SIZE // 2
    freq = THETA ** (-jnp.arange(half, dtype=F32) * 2.0 / HEAD_SIZE)
    angle = positions.astype(F32)[:, None] * freq[None, :]
    cosine = jnp.tile(jnp.cos(angle), (1, 4))
    sine = jnp.sin(angle)
    sine = jnp.concatenate([-sine, sine, -sine, sine], 1)
    pcol = jnp.broadcast_to(positions.astype(F32)[:, None], (LEN, 128))
    prow = jnp.broadcast_to(positions.astype(F32)[None, :], (8, LEN))
    cosine, sine, pcol, prow = order.then((cosine, sine, pcol, prow))

    s_one = order.wait(s_one)
    o_three = pz(order(o_two), 1)
    s_two = order.wait(s_two)
    s_three = pz(s_two, 1)
    o_three = order.wait(o_three)
    g_one = pz(order(feed), 1)
    s_three = order.wait(s_three)
    g_two = pz(order(feed), 2)
    xs = order.wait(both_cores(order.wait(xs)))
    o_sent = order.then(jnp.stack([o_own, o_one, o_two, o_three]))
    os = first_ctx(o_sent)
    xs, slabs = order((xs, (slab, s_one, s_two, s_three)))

    anywhere = pl.BlockSpec(memory_space=pl.ANY)
    vmem = pl.BlockSpec(memory_space=pltpu.VMEM)
    held = [
        sds((MICRO, LEN, QK), BF16),
        sds((MICRO, LEN, 128), BF16),
        sds((ALL, W), BF16),
        sds((MICRO, 3, LEN, LEN), BF16),
        sds((ALL, W), BF16),
    ]
    att, gains, w_slab, qk, v, acted, probs, call_x = order.then(
        call(
            attend_body,
            [sds((LEN, 2 * HG), BF16), sds((8, W), F32), sds((W, SLAB), BF16)]
            + [hbm(o.shape, o.dtype) for o in held],
            sc, *late(xs), *late(slabs), cosine, sine, pcol, prow,
            out_specs=[vmem] * 3 + [anywhere] * 5,
            scratch=[pltpu.VMEM(o.shape, o.dtype) for o in held]
            + [pltpu.VMEM((8, ROWS, 128), BF16), pltpu.VMEM((MICRO, LEN, HG), BF16), pltpu.SemaphoreType.DMA((5,))],
            name="attend",
        )
    )
    att, g_one, g_two = order.wait((att, g_one, g_two))
    heads = first_ctx(att)
    os = order.wait(both_cores(order.wait(os)))
    w_out = order.then(
        call(
            output_weight_body, [sds((W, W), BF16)], sc, *late(os),
            scratch=[pltpu.VMEM((8, 4, wo.size // 128, 128), F32)], name="output_weight",
        )
    )[0]
    g_three = pz(order(g_two), 1)
    d_one, d_two = pz(order(d_own), 1), pz(order(d_own), 2)
    acted_t = order.then(transpose(order(acted)))
    d_one, d_two = order.wait((d_one, d_two))
    d_three = pz(d_two, 1)
    heads[1], heads[2] = order.wait((heads[1], heads[2]))
    heads = order.wait(both_cores(order.wait(heads)))
    cs = first_ctx(order(c_late))
    g_three, d_three = order.wait((g_three, d_three))

    whole = lambda *shape: pl.BlockSpec(shape, lambda t: (0,) * len(shape))
    rowb = lambda n: pl.BlockSpec((256, n), lambda t: (t, 0))
    smem = pl.BlockSpec(memory_space=pltpu.SMEM)
    att_full, mixed, res_own = order.then(
        call(
            project_body,
            [hbm((ALL, W), BF16), sds((ALL, W), BF16), hbm((ROWS, W), F32)],
            sc, call_x, *late(heads), w_out, gains,
            grid=(4,),
            in_specs=[smem, rowb(W)] + [whole(LEN, 2 * HG)] * 8 + [whole(W, W), whole(8, W)],
            out_specs=[rowb(W), rowb(W), whole(ROWS, W)],
            scratch=[pltpu.VMEM((8, 256, HG), BF16)], name="project",
        )
    )
    wo_own = order.then(lax.dynamic_slice(order(w_out), (jnp.minimum(i, KEY_HEADS - 1) * HG, 0), (HG, W)))
    call_c = order.then(join(late(order(both_cores(order.wait(cs))))))
    feeds = order((feed, g_one, g_two, g_three, d_own, d_one, d_two, d_three))
    hidden, dgu, pm, pe, down, dots_two = order.then(
        call(
            feed_body,
            [
                sds((ALL, HID), BF16),
                sds((ALL, 2 * HID), BF16),
                sds((4, ROWS, W), BF16),
                sds((4, ROWS, W), BF16),
                sds((HID, W), BF16),
                sds((8, W), F32),
            ],
            sc, mixed, call_c, *late(feeds),
            grid=(4,),
            in_specs=[smem, rowb(W), rowb(W)] + [whole(288, 2 * HID)] * 4 + [whole(SUB, W)] * 4,
            out_specs=[
                rowb(HID),
                rowb(2 * HID),
                pl.BlockSpec((2, ROWS, W), lambda t: (jnp.minimum(t, 1), 0, 0)),
                pl.BlockSpec((2, ROWS, W), lambda t: (jnp.maximum(t - 2, 0), 0, 0)),
                whole(HID, W),
                whole(8, W),
            ],
            scratch=[pltpu.VMEM((W, 2 * HID), BF16)], name="feed",
        )
    )

    got = pc(pe, 1)
    grad_gu = order.then(lax.dot_general(order(mixed), dgu, TN, preferred_element_type=F32).astype(BF16))
    terms = send_ctx(order.then(scatter_ctx(pm, order(got))))
    grad_dn = order.then(lax.dot_general(order(hidden), call_c, TN, preferred_element_type=F32).astype(BF16))
    feed_blocks = order.then(
        call(grads_body, [hbm((FEED, 2 * HID), BF16)] * 4, sc, grad_gu, grad_dn, name="grads")
    )
    feed_far = pz(feed_blocks[3], 1)
    att_t = order.then(transpose(order(att_full)))
    dres, low = order.then(
        call(
            mid_body, [hbm((ROWS, W), F32), hbm((ROWS, W), BF16)],
            *late([*order(terms), c_own, res_own]), gains, name="mid",
        )
    )
    lows = first_ctx(low)
    feed_mid = order.then(add_low(feed_blocks[2], order(feed_far)))
    feed_terms = (feed_blocks[0], pz(after(feed_blocks[1], feed_mid), 1), pz(feed_mid, 2))

    om_p, oe_p = order.then(onward(order(hidden), down, "outward"))
    out_got = pc(oe_p, 1)
    out_terms = send_ctx(order.then(scatter_ctx(om_p, order(out_got))))
    lows = both_cores(order(lows))

    dqkv, *slab_blocks = order.then(
        call(
            back_body,
            [sds((ALL, SLAB), BF16)] + [sds((EDGE, BACK), BF16)] * 4,
            sc, *late(order(lows)), wo_own, qk, v, probs, cosine, sine, acted_t, att_t, w_slab, gains, dots_two,
            scratch=[
                pltpu.VMEM((ALL, 256), BF16),
                pltpu.VMEM((4, 8, 288), F32),
                pltpu.VMEM((4, EDGE - 288, BACK), F32),
            ],
            name="back",
        )
    )
    slab_far = pz(slab_blocks[3], 1)
    hid_sum, grad_down = order.then(
        call(
            split_feed_body, [sds((8, CHUNK, 2 * HID), BF16), sds((864, 128), F32)],
            *late(order(feed_terms)), name="split_feed",
        )
    )
    hid_sum = lax.all_to_all(hid_sum, "ctx", 0, 0, tiled=True)
    dam, dae = order.then(onward(order(dqkv), w_slab, "inward"))
    in_got = pc(dae, 1)
    slab_mid = order.then(add_low(slab_blocks[2], order(slab_far)))
    slab_terms = (slab_blocks[0], pz(after(slab_blocks[1], slab_mid), 1), pz(slab_mid, 2))
    in_terms = send_ctx(order.then(scatter_ctx(dam, order(in_got))))

    outputs = order.then((res_own + sum(t.astype(F32) for t in order(out_terms))).astype(BF16))
    grad_gate, grad_up = order.then(
        call(unpack_hidden_body, [sds((864, 128), F32), sds((864, 128), F32)], order(hid_sum), name="unpack_hidden")
    )
    slab = order.then(call(split_back_body, [sds((8, 40, BACK), BF16)], *late(order(slab_terms)), name="split_back"))[0]
    slab = lax.all_to_all(slab, "ctx", 0, 0, tiled=True)
    input_grad = order.then(
        call(last_body, [sds((ROWS, W), BF16)], *late([*order(in_terms), x_own, dres]), gains, name="last")
    )[0]
    grad_q, grad_k, grad_v, grad_out, grad_gains = call(
        unpack_back_body,
        [sds((324, 128), F32), sds((108, 128), F32), sds((108, 128), F32), sds((324, 128), F32), sds((8, 128), F32)],
        order(slab), name="unpack_back",
    )
    grad_gains = grad_gains[0, :72]

    shape = (MICRO, 1, POS, W)
    return (
        outputs.reshape(shape),
        input_grad.reshape(shape),
        grad_q.reshape(-1),
        grad_k.reshape(-1),
        grad_v.reshape(-1),
        grad_out.reshape(-1),
        grad_gate.reshape(-1),
        grad_up.reshape(-1),
        grad_down.reshape(-1),
        grad_gains,
    )


def solution(mesh):
    in_specs = (
        P(None, "grp", "ctx", None),
        P(None, "grp", "ctx"),
        P(("grp", "ctx")),
        P(("grp", "ctx")),
        P(("grp", "ctx")),
        P(("grp", "ctx")),
        P(("grp", "ctx")),
        P(("grp", "ctx")),
        P(("grp", "ctx")),
        P(("grp", "ctx")),
        P(None, "grp", "ctx", None),
    )
    out_specs = (
        P(None, "grp", "ctx", None),
        P(None, "grp", "ctx", None),
        P(("grp", "ctx")),
        P(("grp", "ctx")),
        P(("grp", "ctx")),
        P(("grp", "ctx")),
        P(("grp", "ctx")),
        P(("grp", "ctx")),
        P(("grp", "ctx")),
        P(("grp", "ctx")),
    )
    fits = (mesh.shape["ctx"], mesh.shape["grp"]) == (8, 4)
    return jax.shard_map(
        fast_local if fits else local,
        mesh=mesh,
        in_specs=in_specs,
        out_specs=out_specs,
        check_vma=False,
    )
```

profile of v0, /device:TPU:0, one launch (start us, length us, event | category | flops | bytes accessed | tf_op | source)
XLA Modules:
  0.0 244.6 jit_solution(5282551356466406513)
XLA Ops:
  1.5 2.4 pack.1
  3.9 5.4 %all-to-all-start = ((bf16[8,40,1152]{2,1,0:T(8,128)(2,1)}), bf16[8,40,1152]{2,1,0:T(8,128)(2,1)S(1)}, u32[]{:S(2)}, u32[]{:S(2)}) async-start(bf16[8,40,1152]{2,1,0:T(8,128)(2,1)} %pack.1), calls=%async_computation | async-start | bytes 1474560 | tf_op jit(solution)/shard_map/all_to_all | solution.py:1053
  9.4 2.7 %collective-permute-start.1 = (bf16[324,128]{1,0:T(8,128)(2,1)S(1)}, bf16[324,128]{1,0:T(8,128)(2,1)S(1)}, u32[]{:S(2)}, u32[]{:S(2)}) collective-permute-start(bf16[324,128]{1,0:T(8,128)(2,1)S(1)} %bitcast.67), channel_id=1, source_target_pairs={{0,16},{8,24},{16,0},{24,8},{1,17},{9,25},{17,1},{25,9},{2,18},{10... | collective-permute-start | bytes 248840 | tf_op jit(solution)/shard_map/ppermute | solution.py:557
  14.8 2.2 collective-permute-done.1
  17.4 4.1 %all-to-all-done.src = bf16[8,40,1152]{2,1,0:T(8,128)(2,1)S(1)} async-done(((bf16[8,40,1152]{2,1,0:T(8,128)(2,1)}), bf16[8,40,1152]{2,1,0:T(8,128)(2,1)S(1)}, u32[]{:S(2)}, u32[]{:S(2)}) %all-to-all-start) | async-done | bytes 737312 | tf_op jit(solution)/shard_map/all_to_all | solution.py:1053
  23.2 2.6 %collective-permute-start.5 = (bf16[8,40,384]{2,1,0:T(8,128)(2,1)S(1)}, bf16[8,40,384]{2,1,0:T(8,128)(2,1)S(1)}, u32[]{:S(2)}, u32[]{:S(2)}) collective-permute-start(bf16[8,40,384]{2,1,0:T(8,128)(2,1)S(1)} %get-tuple-element.236.w0), channel_id=1, source_target_pairs={{0,16},{8,24},{16,0},{24,8},{1,17},{9,25},{17,1},{25,9},{2,18},{10... | collective-permute-start | bytes 737288 | tf_op jit(solution)/shard_map/ppermute | solution.py:557
  29.4 2.4 collective-permute-done.6.w1
  33.1 2.5 %collective-permute-start.7 = (bf16[8,40,384]{2,1,0:T(8,128)(2,1)S(1)}, bf16[8,40,384]{2,1,0:T(8,128)(2,1)S(1)}, u32[]{:S(2)}, u32[]{:S(2)}) collective-permute-start(bf16[8,40,384]{2,1,0:T(8,128)(2,1)S(1)} %collective-permute-done.5.w2), channel_id=1, source_target_pairs={{0,8},{8,0},{16,24},{24,16},{1,9},{9,1},{17,25},{25,17},{2,10},{10... | collective-permute-start | bytes 737288 | tf_op jit(solution)/shard_map/ppermute | solution.py:557
  35.6 5.0 %collective-permute-done.8 = bf16[324,128]{1,0:T(8,128)(2,1)S(1)} collective-permute-done((bf16[324,128]{1,0:T(8,128)(2,1)S(1)}, bf16[324,128]{1,0:T(8,128)(2,1)S(1)}, u32[]{:S(2)}, u32[]{:S(2)}) %collective-permute-start.8) | collective-permute-done | bytes 82976 | tf_op jit(solution)/shard_map/ppermute | solution.py:557
  42.0 2.0 collective-permute-start.13
  46.6 3.3 %collective-permute-start.19 = (bf16[4,324,128]{2,1,0:T(8,128)(2,1)S(1)}, bf16[4,324,128]{2,1,0:T(8,128)(2,1)}, u32[]{:S(2)}, u32[]{:S(2)}) collective-permute-start(bf16[4,324,128]{2,1,0:T(8,128)(2,1)S(1)} %pad_maximum_fusion.b0), channel_id=1, source_target_pairs={{0,6},{1,7},{2,4},{3,5},{4,2},{5,3},{6,0},{7,1},{8,14},{9,15},{10,... | collective-permute-start | bytes 995336 | tf_op jit(solution)/shard_map/ppermute | solution.py:553
  50.0 3.1 %collective-permute-start.18 = (bf16[4,324,128]{2,1,0:T(8,128)(2,1)S(1)}, bf16[4,324,128]{2,1,0:T(8,128)(2,1)}, u32[]{:S(2)}, u32[]{:S(2)}) collective-permute-start(bf16[4,324,128]{2,1,0:T(8,128)(2,1)S(1)} %pad_maximum_fusion.b0), channel_id=1, source_target_pairs={{0,4},{1,5},{2,6},{3,7},{4,0},{5,1},{6,2},{7,3},{8,12},{9,13},{10,... | collective-permute-start | bytes 995336 | tf_op jit(solution)/shard_map/ppermute | solution.py:553
  55.6 11.0 %attend.1 = (bf16[512,384]{1,0:T(8,128)(2,1)S(1)}, f32[8,1152]{1,0:T(8,128)S(1)}, bf16[1152,384]{1,0:T(8,128)(2,1)S(1)}, bf16[2,512,256]{2,1,0:T(8,128)(2,1)}, b...) custom-call(s32[2]{0:T(128)S(1)} %pad_add_fusion.sc, ...), custom_call_target="tpu_custom_call" | custom-call | bytes 1 | tf_op jit(solution)/shard_map/attend/pallas_call | solution.py:629
  68.9 3.3 %collective-permute-start.15 = (bf16[512,384]{1,0:T(8,128)(2,1)S(1)}, bf16[512,384]{1,0:T(8,128)(2,1)S(1)}, u32[]{:S(2)}, u32[]{:S(2)}) collective-permute-start(bf16[512,384]{1,0:T(8,128)(2,1)S(1)} %get-tuple-element.268.a0), channel_id=1, source_target_pairs={{0,2},{1,3},{2,0},{3,1},{4,6},{5,7},{6,4},{7,5},{8,10},{9,11},{10,... | collective-permute-start | bytes 1179656 | tf_op jit(solution)/shard_map/ppermute | solution.py:553
  74.7 2.5 %output_weight.1.wo = bf16[1152,1152]{1,0:T(8,128)(2,1)S(1)} custom-call(s32[2]{0:T(128)S(1)} %pad_add_fusion.sc, bf16[4,324,128]{2,1,0:T(8,128)(2,1)} %copy-done.23, bf16[4,324,128]{2,1,0:T(8,128)(2,1)} %collective-permute-done.17.b1, bf16[4,324,128]{2,1,0:T(8,128)(2,1)} %collective-permute-done.18.b2, bf16[4,324,128]{2,1,0:T(8,128)(2,1)} %collective-permute-done.19.b3, ...), custom_call_target="tpu_custom_call" | custom-call | bytes 1 | tf_op jit(solution)/shard_map/output_weight/pallas_call | solution.py:629
  77.7 2.9 %collective-permute-start.24 = (bf16[96,1152]{1,0:T(8,128)(2,1)S(1)}, bf16[96,1152]{1,0:T(8,128)(2,1)S(1)}, u32[]{:S(2)}, u32[]{:S(2)}) collective-permute-start(bf16[96,1152]{1,0:T(8,128)(2,1)S(1)} %copy-done.27), channel_id=1, source_target_pairs={{0,8},{8,0},{16,24},{24,16},{1,9},{9,1},{17,25},{25,17},{2,10},{10... | collective-permute-start | bytes 663560 | tf_op jit(solution)/shard_map/ppermute | solution.py:557
  82.6 7.4 %collective-permute-done.25.d2 = bf16[96,1152]{1,0:T(8,128)(2,1)} collective-permute-done((bf16[96,1152]{1,0:T(8,128)(2,1)S(1)}, bf16[96,1152]{1,0:T(8,128)(2,1)}, u32[]{:S(2)}, u32[]{:S(2)}) %collective-permute-start.25) | collective-permute-done | bytes 221216 | tf_op jit(solution)/shard_map/ppermute | solution.py:557
  94.2 2.1 collective-permute-start.33
  97.7 2.0 collective-permute-start.39
  102.2 9.3 %project.1 = (bf16[1024,1152]{1,0:T(8,128)(2,1)}, bf16[1024,1152]{1,0:T(8,128)(2,1)S(1)}, f32[128,1152]{1,0:T(8,128)}) custom-call(s32[2]{0:T(128)S(1)} %pad_add_fusion.sc, bf16[1024,1152]{1,0:T(8,128)(2,1)S(1)} %copy-done.9, bf16[512,384]{1,0:T(8,128)(2,1)} %copy-done.15, bf16[512,384]{1,0:T(8,128)(2,1)} %copy-done.33, bf16[512,384]{1,0:T(8,128)(2,1)} %copy-done.32, ...), custom_call_target="tpu_custom_call" | custom-call | bytes 1 | tf_op jit(solution)/shard_map/project/pallas_call | solution.py:629
  112.2 1.8 collective-permute-done.39.d3
  116.6 1.8 join.1.c
  118.4 9.6 %feed.1 = (bf16[1024,384]{1,0:T(8,128)(2,1)S(1)}, bf16[1024,768]{1,0:T(8,128)(2,1)S(1)}, bf16[4,128,1152]{2,1,0:T(8,128)(2,1)S(1)}, bf16[4,128,1152]{2,1,0:T(8,1...) custom-call(s32[2]{0:T(128)S(1)} %pad_add_fusion.sc, ...), custom_call_target="tpu_custom_call" | custom-call | bytes 1 | tf_op jit(solution)/shard_map/feed/pallas_call | solution.py:629
  128.1 2.1 convolution_convert_fusion.grad_gu
  133.1 2.3 grads.1
  139.9 4.8 %collective-permute-done.43.d = bf16[128,1152]{1,0:T(8,128)(2,1)S(1)} collective-permute-done((bf16[128,1152]{1,0:T(8,128)(2,1)S(1)}, bf16[128,1152]{1,0:T(8,128)(2,1)S(1)}, u32[]{:S(2)}, u32[]{:S(2)}) %collective-permute-start.43) | collective-permute-done | bytes 294944 | tf_op jit(solution)/shard_map/ppermute | solution.py:553
  144.7 2.4 collective-permute-done.42.b
  147.2 4.8 %collective-permute-done.44.f = bf16[128,1152]{1,0:T(8,128)(2,1)S(1)} collective-permute-done((bf16[128,1152]{1,0:T(8,128)(2,1)S(1)}, bf16[128,1152]{1,0:T(8,128)(2,1)S(1)}, u32[]{:S(2)}, u32[]{:S(2)}) %collective-permute-start.44) | collective-permute-done | bytes 294944 | tf_op jit(solution)/shard_map/ppermute | solution.py:553
  152.7 2.9 %mid.1 = (f32[128,1152]{1,0:T(8,128)}, bf16[128,1152]{1,0:T(8,128)(2,1)}) custom-call(bf16[128,1152]{1,0:T(8,128)(2,1)} %get-tuple-element.319.a, bf16[128,1152]{1,0:T(8,128)(2,1)} %copy-done.67, bf16[128,1152]{1,0:T(8,128)(2,1)} %copy-done.66, bf16[128,1152]{1,0:T(8,128)(2,1)} %copy-done.68, bf16[128,1152]{1,0:T(8,128)(2,1)} %bitcast.3.refs_0_.c, ...), custom_call_target="tpu_custom_call" | custom-call | bytes 1 | tf_op jit(solution)/shard_map/mid/pallas_call | solution.py:629
  157.3 2.1 collective-permute-start.51
  160.9 2.9 %collective-permute-start.57 = (bf16[432,768]{1,0:T(8,128)(2,1)S(1)}, bf16[432,768]{1,0:T(8,128)(2,1)S(1)}, u32[]{:S(2)}, u32[]{:S(2)}) collective-permute-start(bf16[432,768]{1,0:T(8,128)(2,1)S(1)} %add_convert_fusion), channel_id=1, source_target_pairs={{0,16},{8,24},{16,0},{24,8},{1,17},{9,25},{17,1},{25,9},{2,18},{10... | collective-permute-start | bytes 1990664 | tf_op jit(solution)/shard_map/ppermute | solution.py:557
  165.3 2.8 %collective-permute-done.51.l3 = bf16[128,1152]{1,0:T(8,128)(2,1)S(1)} collective-permute-done((bf16[128,1152]{1,0:T(8,128)(2,1)S(1)}, bf16[128,1152]{1,0:T(8,128)(2,1)S(1)}, u32[]{:S(2)}, u32[]{:S(2)}) %collective-permute-start.51) | collective-permute-done | bytes 294944 | tf_op jit(solution)/shard_map/ppermute | solution.py:553
  168.2 5.8 %collective-permute-done.50.l2 = bf16[128,1152]{1,0:T(8,128)(2,1)S(1)} collective-permute-done((bf16[128,1152]{1,0:T(8,128)(2,1)S(1)}, bf16[128,1152]{1,0:T(8,128)(2,1)S(1)}, u32[]{:S(2)}, u32[]{:S(2)}) %collective-permute-start.50) | collective-permute-done | bytes 294944 | tf_op jit(solution)/shard_map/ppermute | solution.py:553
  178.0 11.5 %back.1 = (bf16[1024,384]{1,0:T(8,128)(2,1)S(1)}, bf16[304,512]{1,0:T(8,128)(2,1)S(1)}, bf16[304,512]{1,0:T(8,128)(2,1)S(1)}, bf16[304,512]{1,0:T(8,128)(2,1)S(1)}, bf16[304,512]{1,0:T(8,128)(2,1)}) custom-call(s32[2]{0:T(128)S(1)} %pad_add_fusion.sc, bf16[128,1152]{1,0:T(8,128)(2,1)} %get-tuple-element.334.l0, bf16[128,1152]{1,0:T(8,128)(2,1)} %copy-done.54, ...), custom_call_target="tpu_custom_call" | custom-call | bytes 1 | tf_op jit(solution)/shard_map/back/pallas_call | solution.py:629
  189.5 3.7 %collective-permute-done.56.b = bf16[432,768]{1,0:T(8,128)(2,1)S(1)} collective-permute-done((bf16[432,768]{1,0:T(8,128)(2,1)S(1)}, bf16[432,768]{1,0:T(8,128)(2,1)S(1)}, u32[]{:S(2)}, u32[]{:S(2)}) %collective-permute-start.56) | collective-permute-done | bytes 663584 | tf_op jit(solution)/shard_map/ppermute | solution.py:557
  194.3 2.6 %split_feed.1 = (bf16[8,36,768]{2,1,0:T(8,128)(2,1)}, f32[864,128]{1,0:T(8,128)}) custom-call(bf16[432,768]{1,0:T(8,128)(2,1)} %get-tuple-element.351.a, bf16[432,768]{1,0:T(8,128)(2,1)} %copy-done.29, bf16[432,768]{1,0:T(8,128)(2,1)} %copy-done.28), custom_call_target="tpu_custom_call" | custom-call | bytes 1 | tf_op jit(solution)/shard_map/split_feed/pallas_call | solution.py:629
  196.9 2.6 %inward.1 = (bf16[4,128,1152]{2,1,0:T(8,128)(2,1)S(1)}, bf16[4,128,1152]{2,1,0:T(8,128)(2,1)}) custom-call(bf16[1024,384]{1,0:T(8,128)(2,1)S(1)} %get-tuple-element.355.rows, bf16[1152,384]{1,0:T(8,128)(2,1)S(1)} %get-tuple-element.345.w_slab.weight), custom_call_target="tpu_custom_call" | custom-call | bytes 1 | tf_op jit(solution)/shard_map/inward/pallas_call | solution.py:629
  201.0 2.0 collective-permute-start.48
  204.5 3.5 %all-to-all-start.1 = ((bf16[8,36,768]{2,1,0:T(8,128)(2,1)}), bf16[8,36,768]{2,1,0:T(8,128)(2,1)S(1)}, u32[]{:S(2)}, u32[]{:S(2)}) async-start(bf16[8,36,768]{2,1,0:T(8,128)(2,1)} %get-tuple-element.368), calls=%async_computation.1 | async-start | bytes 983040 | tf_op jit(solution)/shard_map/all_to_all | solution.py:1222
  209.6 1.8 add_convert_fusion.1
  214.8 2.9 %collective-permute-done.47 = bf16[128,1152]{1,0:T(8,128)(2,1)} collective-permute-done((bf16[128,1152]{1,0:T(8,128)(2,1)}, bf16[128,1152]{1,0:T(8,128)(2,1)}, u32[]{:S(2)}, u32[]{:S(2)}) %collective-permute-start.47) | collective-permute-done | bytes 294944 | tf_op jit(solution)/shard_map/ppermute | solution.py:553
  217.7 2.7 %collective-permute-start.62 = (bf16[128,1152]{1,0:T(8,128)(2,1)}, bf16[128,1152]{1,0:T(8,128)(2,1)S(1)}, u32[]{:S(2)}, u32[]{:S(2)}) collective-permute-start(bf16[128,1152]{1,0:T(8,128)(2,1)} %get-tuple-element.419), channel_id=1, source_target_pairs={{0,6},{1,7},{2,4},{3,5},{4,2},{5,3},{6,0},{7,1},{8,14},{9,15},{10,... | collective-permute-start | bytes 884744 | tf_op jit(solution)/shard_map/ppermute | solution.py:553
  221.5 2.1 add_convert_fusion.5
  225.8 2.3 collective-permute-done.64.d
  228.9 2.0 split_back.1
  230.9 4.7 %all-to-all-start.2 = ((bf16[8,40,512]{2,1,0:T(8,128)(2,1)}), bf16[8,40,512]{2,1,0:T(8,128)(2,1)S(1)}, u32[]{:S(2)}, u32[]{:S(2)}) async-start(bf16[8,40,512]{2,1,0:T(8,128)(2,1)} %split_back.1), calls=%async_computation.2 | async-start | bytes 655360 | tf_op jit(solution)/shard_map/all_to_all | solution.py:1234
  236.6 2.6 %last.1 = bf16[128,1152]{1,0:T(8,128)(2,1)} custom-call(bf16[128,1152]{1,0:T(8,128)(2,1)} %get-tuple-element.374.a, bf16[128,1152]{1,0:T(8,128)(2,1)} %copy-done.57, bf16[128,1152]{1,0:T(8,128)(2,1)} %copy-done.56, bf16[128,1152]{1,0:T(8,128)(2,1)} %copy-done.55, bf16[128,1152]{1,0:T(8,128)(2,1)} %bitcast.59, f32[128,1152]{1,0:T(8,128)} %get-tuple-element.378.dres, ...), custom_call_target="tpu_custom_call" | custom-call | bytes 1 | tf_op jit(solution)/shard_map/last/pallas_call | solution.py:629
  239.2 4.1 %all-to-all-done.2.src = bf16[8,40,512]{2,1,0:T(8,128)(2,1)S(1)} async-done(((bf16[8,40,512]{2,1,0:T(8,128)(2,1)}), bf16[8,40,512]{2,1,0:T(8,128)(2,1)S(1)}, u32[]{:S(2)}, u32[]{:S(2)}) %all-to-all-start.2) | async-done | bytes 327712 | tf_op jit(solution)/shard_map/all_to_all | solution.py:1234
  (297 shorter events, 67.4 us)
Async XLA Ops:
  3.9 17.5 %all-to-all-start = ((bf16[8,40,1152]{2,1,0:T(8,128)(2,1)}), bf16[8,40,1152]{2,1,0:T(8,128)(2,1)S(1)}, u32[]{:S(2)}, u32[]{:S(2)}) async-start(bf16[8,40,1152]{2,1,0:T(8,128)(2,1)} %pack.1), calls=%async_computation | async-start | bytes 1474560 | tf_op jit(solution)/shard_map/all_to_all | solution.py:1053
  9.4 7.7 %collective-permute-start.1 = (bf16[324,128]{1,0:T(8,128)(2,1)S(1)}, bf16[324,128]{1,0:T(8,128)(2,1)S(1)}, u32[]{:S(2)}, u32[]{:S(2)}) collective-permute-start(bf16[324,128]{1,0:T(8,128)(2,1)S(1)} %bitcast.67), channel_id=1, source_target_pairs={{0,16},{8,24},{16,0},{24,8},{1,17},{9,25},{17,1},{25,9},{2,18},{10... | collective-permute-start | bytes 248840 | tf_op jit(solution)/shard_map/ppermute | solution.py:557
  21.6 10.3 %collective-permute-start.6 = (bf16[8,40,384]{2,1,0:T(8,128)(2,1)S(1)}, bf16[8,40,384]{2,1,0:T(8,128)(2,1)S(1)}, u32[]{:S(2)}, u32[]{:S(2)}) collective-permute-start(bf16[8,40,384]{2,1,0:T(8,128)(2,1)S(1)} %get-tuple-element.236.w0), channel_id=1, source_target_pairs={{0,8},{8,0},{16,24},{24,16},{1,9},{9,1},{17,25},{25,17},{2,10},{10... | collective-permute-start | bytes 737288 | tf_op jit(solution)/shard_map/ppermute | solution.py:557
  23.2 9.9 %collective-permute-start.5 = (bf16[8,40,384]{2,1,0:T(8,128)(2,1)S(1)}, bf16[8,40,384]{2,1,0:T(8,128)(2,1)S(1)}, u32[]{:S(2)}, u32[]{:S(2)}) collective-permute-start(bf16[8,40,384]{2,1,0:T(8,128)(2,1)S(1)} %get-tuple-element.236.w0), channel_id=1, source_target_pairs={{0,16},{8,24},{16,0},{24,8},{1,17},{9,25},{17,1},{25,9},{2,18},{10... | collective-permute-start | bytes 737288 | tf_op jit(solution)/shard_map/ppermute | solution.py:557
  25.8 14.9 %collective-permute-start.4 = (bf16[128,1280]{1,0:T(8,128)(2,1)S(1)}, bf16[128,1280]{1,0:T(8,128)(2,1)S(1)}, u32[]{:S(2)}, u32[]{:S(2)}) collective-permute-start(bf16[128,1280]{1,0:T(8,128)(2,1)S(1)} %pad_maximum_fusion.1.x0), channel_id=1, source_target_pairs={{0,6},{1,7},{2,4},{3,5},{4,2},{5,3},{6,0},{7,1},{8,14},{9,15},{10,... | collective-permute-start | bytes 983048 | tf_op jit(solution)/shard_map/ppermute | solution.py:553
  26.3 14.4 %collective-permute-start.3 = (bf16[128,1280]{1,0:T(8,128)(2,1)S(1)}, bf16[128,1280]{1,0:T(8,128)(2,1)S(1)}, u32[]{:S(2)}, u32[]{:S(2)}) collective-permute-start(bf16[128,1280]{1,0:T(8,128)(2,1)S(1)} %pad_maximum_fusion.1.x0), channel_id=1, source_target_pairs={{0,4},{1,5},{2,6},{3,7},{4,0},{5,1},{6,2},{7,3},{8,12},{9,13},{10,... | collective-permute-start | bytes 983048 | tf_op jit(solution)/shard_map/ppermute | solution.py:553
  27.8 13.0 %collective-permute-start.2 = (bf16[128,1280]{1,0:T(8,128)(2,1)S(1)}, bf16[128,1280]{1,0:T(8,128)(2,1)S(1)}, u32[]{:S(2)}, u32[]{:S(2)}) collective-permute-start(bf16[128,1280]{1,0:T(8,128)(2,1)S(1)} %pad_maximum_fusion.1.x0), channel_id=1, source_target_pairs={{0,2},{1,3},{2,0},{3,1},{4,6},{5,7},{6,4},{7,5},{8,10},{9,11},{10,... | collective-permute-start | bytes 983048 | tf_op jit(solution)/shard_map/ppermute | solution.py:553
  33.1 7.6 %collective-permute-start.7 = (bf16[8,40,384]{2,1,0:T(8,128)(2,1)S(1)}, bf16[8,40,384]{2,1,0:T(8,128)(2,1)S(1)}, u32[]{:S(2)}, u32[]{:S(2)}) collective-permute-start(bf16[8,40,384]{2,1,0:T(8,128)(2,1)S(1)} %collective-permute-done.5.w2), channel_id=1, source_target_pairs={{0,8},{8,0},{16,24},{24,16},{1,9},{9,1},{17,25},{25,17},{2,10},{10... | collective-permute-start | bytes 737288 | tf_op jit(solution)/shard_map/ppermute | solution.py:557
  41.4 8.6 %collective-permute-start.11 = (bf16[128,1280]{1,0:T(8,128)(2,1)S(1)}, bf16[128,1280]{1,0:T(8,128)(2,1)S(1)}, u32[]{:S(2)}, u32[]{:S(2)}) collective-permute-start(bf16[128,1280]{1,0:T(8,128)(2,1)S(1)} %collective-permute-done.3.x2), channel_id=1, source_target_pairs={{0,1},{1,0},{2,3},{3,2},{4,5},{5,4},{6,7},{7,6},{8,9},{9,8},{10,11... | collective-permute-start | bytes 983048 | tf_op jit(solution)/shard_map/ppermute | solution.py:553
  41.4 11.7 %collective-permute-start.12 = (bf16[128,1280]{1,0:T(8,128)(2,1)S(1)}, bf16[128,1280]{1,0:T(8,128)(2,1)S(1)}, u32[]{:S(2)}, u32[]{:S(2)}) collective-permute-start(bf16[128,1280]{1,0:T(8,128)(2,1)S(1)} %collective-permute-done.4.x3), channel_id=1, source_target_pairs={{0,1},{1,0},{2,3},{3,2},{4,5},{5,4},{6,7},{7,6},{8,9},{9,8},{10,11... | collective-permute-start | bytes 983048 | tf_op jit(solution)/shard_map/ppermute | solution.py:553
  42.0 24.7 %collective-permute-start.13 = (bf16[288,768]{1,0:T(8,128)(2,1)S(1)}, bf16[288,768]{1,0:T(8,128)(2,1)}, u32[]{:S(2)}, u32[]{:S(2)}) collective-permute-start(bf16[288,768]{1,0:T(8,128)(2,1)S(1)} %get-tuple-element.299.g0), channel_id=1, source_target_pairs={{0,8},{8,0},{16,24},{24,16},{1,9},{9,1},{17,25},{25,17},{2,10},{10... | collective-permute-start | bytes 1327112 | tf_op jit(solution)/shard_map/ppermute | solution.py:557
  44.0 22.7 %collective-permute-start.14 = (bf16[288,768]{1,0:T(8,128)(2,1)S(1)}, bf16[288,768]{1,0:T(8,128)(2,1)}, u32[]{:S(2)}, u32[]{:S(2)}) collective-permute-start(bf16[288,768]{1,0:T(8,128)(2,1)S(1)} %get-tuple-element.299.g0), channel_id=1, source_target_pairs={{0,16},{8,24},{16,0},{24,8},{1,17},{9,25},{17,1},{25,9},{2,18},{10... | collective-permute-start | bytes 1327112 | tf_op jit(solution)/shard_map/ppermute | solution.py:557
  46.6 20.1 %collective-permute-start.19 = (bf16[4,324,128]{2,1,0:T(8,128)(2,1)S(1)}, bf16[4,324,128]{2,1,0:T(8,128)(2,1)}, u32[]{:S(2)}, u32[]{:S(2)}) collective-permute-start(bf16[4,324,128]{2,1,0:T(8,128)(2,1)S(1)} %pad_maximum_fusion.b0), channel_id=1, source_target_pairs={{0,6},{1,7},{2,4},{3,5},{4,2},{5,3},{6,0},{7,1},{8,14},{9,15},{10,... | collective-permute-start | bytes 995336 | tf_op jit(solution)/shard_map/ppermute | solution.py:553
  50.0 16.7 %collective-permute-start.18 = (bf16[4,324,128]{2,1,0:T(8,128)(2,1)S(1)}, bf16[4,324,128]{2,1,0:T(8,128)(2,1)}, u32[]{:S(2)}, u32[]{:S(2)}) collective-permute-start(bf16[4,324,128]{2,1,0:T(8,128)(2,1)S(1)} %pad_maximum_fusion.b0), channel_id=1, source_target_pairs={{0,4},{1,5},{2,6},{3,7},{4,0},{5,1},{6,2},{7,3},{8,12},{9,13},{10,... | collective-permute-start | bytes 995336 | tf_op jit(solution)/shard_map/ppermute | solution.py:553
  53.1 13.6 %collective-permute-start.17 = (bf16[4,324,128]{2,1,0:T(8,128)(2,1)S(1)}, bf16[4,324,128]{2,1,0:T(8,128)(2,1)}, u32[]{:S(2)}, u32[]{:S(2)}) collective-permute-start(bf16[4,324,128]{2,1,0:T(8,128)(2,1)S(1)} %pad_maximum_fusion.b0), channel_id=1, source_target_pairs={{0,2},{1,3},{2,0},{3,1},{4,6},{5,7},{6,4},{7,5},{8,10},{9,11},{10,... | collective-permute-start | bytes 995336 | tf_op jit(solution)/shard_map/ppermute | solution.py:553
  67.3 5.9 %collective-permute-start.22 = (bf16[4,324,128]{2,1,0:T(8,128)(2,1)}, bf16[4,324,128]{2,1,0:T(8,128)(2,1)S(1)}, u32[]{:S(2)}, u32[]{:S(2)}) collective-permute-start(bf16[4,324,128]{2,1,0:T(8,128)(2,1)} %collective-permute-done.18.b2), channel_id=1, source_target_pairs={{0,1},{1,0},{2,3},{3,2},{4,5},{5,4},{6,7},{7,6},{8,9},{9,8},{10,11... | collective-permute-start | bytes 995336 | tf_op jit(solution)/shard_map/ppermute | solution.py:553
  67.8 22.2 %collective-permute-start.16 = (bf16[512,384]{1,0:T(8,128)(2,1)S(1)}, bf16[512,384]{1,0:T(8,128)(2,1)S(1)}, u32[]{:S(2)}, u32[]{:S(2)}) collective-permute-start(bf16[512,384]{1,0:T(8,128)(2,1)S(1)} %get-tuple-element.268.a0), channel_id=1, source_target_pairs={{0,4},{1,5},{2,6},{3,7},{4,0},{5,1},{6,2},{7,3},{8,12},{9,13},{10,... | collective-permute-start | bytes 1179656 | tf_op jit(solution)/shard_map/ppermute | solution.py:553
  68.9 21.1 %collective-permute-start.15 = (bf16[512,384]{1,0:T(8,128)(2,1)S(1)}, bf16[512,384]{1,0:T(8,128)(2,1)S(1)}, u32[]{:S(2)}, u32[]{:S(2)}) collective-permute-start(bf16[512,384]{1,0:T(8,128)(2,1)S(1)} %get-tuple-element.268.a0), channel_id=1, source_target_pairs={{0,2},{1,3},{2,0},{3,1},{4,6},{5,7},{6,4},{7,5},{8,10},{9,11},{10,... | collective-permute-start | bytes 1179656 | tf_op jit(solution)/shard_map/ppermute | solution.py:553
  72.3 18.3 %collective-permute-start.26 = (bf16[512,384]{1,0:T(8,128)(2,1)S(1)}, bf16[512,384]{1,0:T(8,128)(2,1)S(1)}, u32[]{:S(2)}, u32[]{:S(2)}) collective-permute-start(bf16[512,384]{1,0:T(8,128)(2,1)S(1)} %get-tuple-element.268.a0), channel_id=1, source_target_pairs={{0,6},{1,7},{2,4},{3,5},{4,2},{5,3},{6,0},{7,1},{8,14},{9,15},{10,... | collective-permute-start | bytes 1179656 | tf_op jit(solution)/shard_map/ppermute | solution.py:553
  77.3 12.8 %collective-permute-start.25 = (bf16[96,1152]{1,0:T(8,128)(2,1)S(1)}, bf16[96,1152]{1,0:T(8,128)(2,1)}, u32[]{:S(2)}, u32[]{:S(2)}) collective-permute-start(bf16[96,1152]{1,0:T(8,128)(2,1)S(1)} %copy-done.27), channel_id=1, source_target_pairs={{0,16},{8,24},{16,0},{24,8},{1,17},{9,25},{17,1},{25,9},{2,18},{10... | collective-permute-start | bytes 663560 | tf_op jit(solution)/shard_map/ppermute | solution.py:557
  77.7 12.4 %collective-permute-start.24 = (bf16[96,1152]{1,0:T(8,128)(2,1)S(1)}, bf16[96,1152]{1,0:T(8,128)(2,1)S(1)}, u32[]{:S(2)}, u32[]{:S(2)}) collective-permute-start(bf16[96,1152]{1,0:T(8,128)(2,1)S(1)} %copy-done.27), channel_id=1, source_target_pairs={{0,8},{8,0},{16,24},{24,16},{1,9},{9,1},{17,25},{25,17},{2,10},{10... | collective-permute-start | bytes 663560 | tf_op jit(solution)/shard_map/ppermute | solution.py:557
  94.2 17.4 %collective-permute-start.33 = (bf16[128,1152]{1,0:T(8,128)(2,1)}, bf16[128,1152]{1,0:T(8,128)(2,1)}, u32[]{:S(2)}, u32[]{:S(2)}) collective-permute-start(bf16[128,1152]{1,0:T(8,128)(2,1)} %bitcast.3.refs_0_.c), channel_id=1, source_target_pairs={{0,6},{1,7},{2,4},{3,5},{4,2},{5,3},{6,0},{7,1},{8,14},{9,15},{10,... | collective-permute-start | bytes 884744 | tf_op jit(solution)/shard_map/ppermute | solution.py:553
  96.2 15.3 %collective-permute-start.32 = (bf16[128,1152]{1,0:T(8,128)(2,1)}, bf16[128,1152]{1,0:T(8,128)(2,1)}, u32[]{:S(2)}, u32[]{:S(2)}) collective-permute-start(bf16[128,1152]{1,0:T(8,128)(2,1)} %bitcast.3.refs_0_.c), channel_id=1, source_target_pairs={{0,4},{1,5},{2,6},{3,7},{4,0},{5,1},{6,2},{7,3},{8,12},{9,13},{10,... | collective-permute-start | bytes 884744 | tf_op jit(solution)/shard_map/ppermute | solution.py:553
  97.3 14.3 %collective-permute-start.31 = (bf16[128,1152]{1,0:T(8,128)(2,1)}, bf16[128,1152]{1,0:T(8,128)(2,1)}, u32[]{:S(2)}, u32[]{:S(2)}) collective-permute-start(bf16[128,1152]{1,0:T(8,128)(2,1)} %bitcast.3.refs_0_.c), channel_id=1, source_target_pairs={{0,2},{1,3},{2,0},{3,1},{4,6},{5,7},{6,4},{7,5},{8,10},{9,11},{10,... | collective-permute-start | bytes 884744 | tf_op jit(solution)/shard_map/ppermute | solution.py:553
  97.7 16.3 %collective-permute-start.38 = (bf16[288,768]{1,0:T(8,128)(2,1)}, bf16[288,768]{1,0:T(8,128)(2,1)S(1)}, u32[]{:S(2)}, u32[]{:S(2)}) collective-permute-start(bf16[288,768]{1,0:T(8,128)(2,1)} %collective-permute-done.14.g2), channel_id=1, source_target_pairs={{0,8},{8,0},{16,24},{24,16},{1,9},{9,1},{17,25},{25,17},{2,10},{10... | collective-permute-start | bytes 1327112 | tf_op jit(solution)/shard_map/ppermute | solution.py:557
  97.7 16.3 %collective-permute-start.39 = (bf16[96,1152]{1,0:T(8,128)(2,1)}, bf16[96,1152]{1,0:T(8,128)(2,1)S(1)}, u32[]{:S(2)}, u32[]{:S(2)}) collective-permute-start(bf16[96,1152]{1,0:T(8,128)(2,1)} %collective-permute-done.25.d2), channel_id=1, source_target_pairs={{0,8},{8,0},{16,24},{24,16},{1,9},{9,1},{17,25},{25,17},{2,10},{10... | collective-permute-start | bytes 663560 | tf_op jit(solution)/shard_map/ppermute | solution.py:557
  135.4 20.1 %collective-permute-start.41 = (bf16[432,768]{1,0:T(8,128)(2,1)}, bf16[432,768]{1,0:T(8,128)(2,1)S(1)}, u32[]{:S(2)}, u32[]{:S(2)}) collective-permute-start(bf16[432,768]{1,0:T(8,128)(2,1)} %get-tuple-element.316), channel_id=1, source_target_pairs={{0,8},{8,0},{16,24},{24,16},{1,9},{9,1},{17,25},{25,17},{2,10},{10... | collective-permute-start | bytes 1990664 | tf_op jit(solution)/shard_map/ppermute | solution.py:557
  135.7 9.0 %collective-permute-start.43 = (bf16[128,1152]{1,0:T(8,128)(2,1)S(1)}, bf16[128,1152]{1,0:T(8,128)(2,1)S(1)}, u32[]{:S(2)}, u32[]{:S(2)}) collective-permute-start(bf16[128,1152]{1,0:T(8,128)(2,1)S(1)} %get-tuple-element.424), channel_id=1, source_target_pairs={{0,4},{1,5},{2,6},{3,7},{4,0},{5,1},{6,2},{7,3},{8,12},{9,13},{10,... | collective-permute-start | bytes 884744 | tf_op jit(solution)/shard_map/ppermute | solution.py:553
  137.2 9.9 %collective-permute-start.42 = (bf16[128,1152]{1,0:T(8,128)(2,1)S(1)}, bf16[128,1152]{1,0:T(8,128)(2,1)S(1)}, u32[]{:S(2)}, u32[]{:S(2)}) collective-permute-start(bf16[128,1152]{1,0:T(8,128)(2,1)S(1)} %get-tuple-element.425), channel_id=1, source_target_pairs={{0,2},{1,3},{2,0},{3,1},{4,6},{5,7},{6,4},{7,5},{8,10},{9,11},{10,... | collective-permute-start | bytes 884744 | tf_op jit(solution)/shard_map/ppermute | solution.py:553
  138.3 13.7 %collective-permute-start.44 = (bf16[128,1152]{1,0:T(8,128)(2,1)S(1)}, bf16[128,1152]{1,0:T(8,128)(2,1)S(1)}, u32[]{:S(2)}, u32[]{:S(2)}) collective-permute-start(bf16[128,1152]{1,0:T(8,128)(2,1)S(1)} %get-tuple-element.427), channel_id=1, source_target_pairs={{0,6},{1,7},{2,4},{3,5},{4,2},{5,3},{6,0},{7,1},{8,14},{9,15},{10,... | collective-permute-start | bytes 884744 | tf_op jit(solution)/shard_map/ppermute | solution.py:553
  157.2 6.6 %collective-permute-start.45 = (bf16[4,128,1152]{2,1,0:T(8,128)(2,1)S(1)}, bf16[4,128,1152]{2,1,0:T(8,128)(2,1)S(1)}, u32[]{:S(2)}, u32[]{:S(2)}) collective-permute-start(bf16[4,128,1152]{2,1,0:T(8,128)(2,1)S(1)} %get-tuple-element.328), channel_id=1, source_target_pairs={{0,1},{1,0},{2,3},{3,2},{4,5},{5,4},{6,7},{7,6},{8,9},{9,8},{10,11... | collective-permute-start | bytes 3538952 | tf_op jit(solution)/shard_map/ppermute | solution.py:553
  157.3 10.8 %collective-permute-start.51 = (bf16[128,1152]{1,0:T(8,128)(2,1)S(1)}, bf16[128,1152]{1,0:T(8,128)(2,1)S(1)}, u32[]{:S(2)}, u32[]{:S(2)}) collective-permute-start(bf16[128,1152]{1,0:T(8,128)(2,1)S(1)} %copy-done.51), channel_id=1, source_target_pairs={{0,6},{1,7},{2,4},{3,5},{4,2},{5,3},{6,0},{7,1},{8,14},{9,15},{10,... | collective-permute-start | bytes 884744 | tf_op jit(solution)/shard_map/ppermute | solution.py:553
  159.4 14.5 %collective-permute-start.50 = (bf16[128,1152]{1,0:T(8,128)(2,1)S(1)}, bf16[128,1152]{1,0:T(8,128)(2,1)S(1)}, u32[]{:S(2)}, u32[]{:S(2)}) collective-permute-start(bf16[128,1152]{1,0:T(8,128)(2,1)S(1)} %copy-done.51), channel_id=1, source_target_pairs={{0,4},{1,5},{2,6},{3,7},{4,0},{5,1},{6,2},{7,3},{8,12},{9,13},{10,... | collective-permute-start | bytes 884744 | tf_op jit(solution)/shard_map/ppermute | solution.py:553
  160.5 13.6 %collective-permute-start.49 = (bf16[128,1152]{1,0:T(8,128)(2,1)S(1)}, bf16[128,1152]{1,0:T(8,128)(2,1)S(1)}, u32[]{:S(2)}, u32[]{:S(2)}) collective-permute-start(bf16[128,1152]{1,0:T(8,128)(2,1)S(1)} %copy-done.51), channel_id=1, source_target_pairs={{0,2},{1,3},{2,0},{3,1},{4,6},{5,7},{6,4},{7,5},{8,10},{9,11},{10,... | collective-permute-start | bytes 884744 | tf_op jit(solution)/shard_map/ppermute | solution.py:553
  160.9 32.3 %collective-permute-start.57 = (bf16[432,768]{1,0:T(8,128)(2,1)S(1)}, bf16[432,768]{1,0:T(8,128)(2,1)S(1)}, u32[]{:S(2)}, u32[]{:S(2)}) collective-permute-start(bf16[432,768]{1,0:T(8,128)(2,1)S(1)} %add_convert_fusion), channel_id=1, source_target_pairs={{0,16},{8,24},{16,0},{24,8},{1,17},{9,25},{17,1},{25,9},{2,18},{10... | collective-permute-start | bytes 1990664 | tf_op jit(solution)/shard_map/ppermute | solution.py:557
  163.8 29.4 %collective-permute-start.56 = (bf16[432,768]{1,0:T(8,128)(2,1)S(1)}, bf16[432,768]{1,0:T(8,128)(2,1)S(1)}, u32[]{:S(2)}, u32[]{:S(2)}) collective-permute-start(bf16[432,768]{1,0:T(8,128)(2,1)S(1)} %copy-done.77), channel_id=1, source_target_pairs={{0,8},{8,0},{16,24},{24,16},{1,9},{9,1},{17,25},{25,17},{2,10},{10... | collective-permute-start | bytes 1990664 | tf_op jit(solution)/shard_map/ppermute | solution.py:557
  199.5 12.9 %collective-permute-start.58 = (bf16[4,128,1152]{2,1,0:T(8,128)(2,1)}, bf16[4,128,1152]{2,1,0:T(8,128)(2,1)S(1)}, u32[]{:S(2)}, u32[]{:S(2)}) collective-permute-start(bf16[4,128,1152]{2,1,0:T(8,128)(2,1)} %get-tuple-element.357), channel_id=1, source_target_pairs={{0,1},{1,0},{2,3},{3,2},{4,5},{5,4},{6,7},{7,6},{8,9},{9,8},{10,11... | collective-permute-start | bytes 3538952 | tf_op jit(solution)/shard_map/ppermute | solution.py:553
  199.6 10.0 %collective-permute-start.59 = (bf16[304,512]{1,0:T(8,128)(2,1)}, bf16[304,512]{1,0:T(8,128)(2,1)S(1)}, u32[]{:S(2)}, u32[]{:S(2)}) collective-permute-start(bf16[304,512]{1,0:T(8,128)(2,1)} %get-tuple-element.350), channel_id=1, source_target_pairs={{0,8},{8,0},{16,24},{24,16},{1,9},{9,1},{17,25},{25,17},{2,10},{10... | collective-permute-start | bytes 933896 | tf_op jit(solution)/shard_map/ppermute | solution.py:557
  201.0 19.4 %collective-permute-start.48 = (bf16[128,1152]{1,0:T(8,128)(2,1)}, bf16[128,1152]{1,0:T(8,128)(2,1)}, u32[]{:S(2)}, u32[]{:S(2)}) collective-permute-start(bf16[128,1152]{1,0:T(8,128)(2,1)} %get-tuple-element.420), channel_id=1, source_target_pairs={{0,6},{1,7},{2,4},{3,5},{4,2},{5,3},{6,0},{7,1},{8,14},{9,15},{10,... | collective-permute-start | bytes 884744 | tf_op jit(solution)/shard_map/ppermute | solution.py:553
  203.0 14.7 %collective-permute-start.47 = (bf16[128,1152]{1,0:T(8,128)(2,1)}, bf16[128,1152]{1,0:T(8,128)(2,1)}, u32[]{:S(2)}, u32[]{:S(2)}) collective-permute-start(bf16[128,1152]{1,0:T(8,128)(2,1)} %get-tuple-element.421), channel_id=1, source_target_pairs={{0,4},{1,5},{2,6},{3,7},{4,0},{5,1},{6,2},{7,3},{8,12},{9,13},{10,... | collective-permute-start | bytes 884744 | tf_op jit(solution)/shard_map/ppermute | solution.py:553
  204.1 16.3 %collective-permute-start.46 = (bf16[128,1152]{1,0:T(8,128)(2,1)}, bf16[128,1152]{1,0:T(8,128)(2,1)}, u32[]{:S(2)}, u32[]{:S(2)}) collective-permute-start(bf16[128,1152]{1,0:T(8,128)(2,1)} %get-tuple-element.422), channel_id=1, source_target_pairs={{0,2},{1,3},{2,0},{3,1},{4,6},{5,7},{6,4},{7,5},{8,10},{9,11},{10,... | collective-permute-start | bytes 884744 | tf_op jit(solution)/shard_map/ppermute | solution.py:553
  204.5 19.2 %all-to-all-start.1 = ((bf16[8,36,768]{2,1,0:T(8,128)(2,1)}), bf16[8,36,768]{2,1,0:T(8,128)(2,1)S(1)}, u32[]{:S(2)}, u32[]{:S(2)}) async-start(bf16[8,36,768]{2,1,0:T(8,128)(2,1)} %get-tuple-element.368), calls=%async_computation.1 | async-start | bytes 983040 | tf_op jit(solution)/shard_map/all_to_all | solution.py:1222
  211.4 16.8 %collective-permute-start.64 = (bf16[304,512]{1,0:T(8,128)(2,1)}, bf16[304,512]{1,0:T(8,128)(2,1)S(1)}, u32[]{:S(2)}, u32[]{:S(2)}) collective-permute-start(bf16[304,512]{1,0:T(8,128)(2,1)} %add_convert_fusion.1), channel_id=1, source_target_pairs={{0,16},{8,24},{16,0},{24,8},{1,17},{9,25},{17,1},{25,9},{2,18},{10... | collective-permute-start | bytes 933896 | tf_op jit(solution)/shard_map/ppermute | solution.py:557
  212.4 13.5 %collective-permute-start.63 = (bf16[304,512]{1,0:T(8,128)(2,1)S(1)}, bf16[304,512]{1,0:T(8,128)(2,1)}, u32[]{:S(2)}, u32[]{:S(2)}) collective-permute-start(bf16[304,512]{1,0:T(8,128)(2,1)S(1)} %copy-done.21), channel_id=1, source_target_pairs={{0,8},{8,0},{16,24},{24,16},{1,9},{9,1},{17,25},{25,17},{2,10},{10... | collective-permute-start | bytes 933896 | tf_op jit(solution)/shard_map/ppermute | solution.py:557
  217.7 18.0 %collective-permute-start.62 = (bf16[128,1152]{1,0:T(8,128)(2,1)}, bf16[128,1152]{1,0:T(8,128)(2,1)S(1)}, u32[]{:S(2)}, u32[]{:S(2)}) collective-permute-start(bf16[128,1152]{1,0:T(8,128)(2,1)} %get-tuple-element.419), channel_id=1, source_target_pairs={{0,6},{1,7},{2,4},{3,5},{4,2},{5,3},{6,0},{7,1},{8,14},{9,15},{10,... | collective-permute-start | bytes 884744 | tf_op jit(solution)/shard_map/ppermute | solution.py:553
  220.4 15.2 %collective-permute-start.61 = (bf16[128,1152]{1,0:T(8,128)(2,1)}, bf16[128,1152]{1,0:T(8,128)(2,1)S(1)}, u32[]{:S(2)}, u32[]{:S(2)}) collective-permute-start(bf16[128,1152]{1,0:T(8,128)(2,1)} %get-tuple-element.416), channel_id=1, source_target_pairs={{0,4},{1,5},{2,6},{3,7},{4,0},{5,1},{6,2},{7,3},{8,12},{9,13},{10,... | collective-permute-start | bytes 884744 | tf_op jit(solution)/shard_map/ppermute | solution.py:553
  221.5 14.2 %collective-permute-start.60 = (bf16[128,1152]{1,0:T(8,128)(2,1)}, bf16[128,1152]{1,0:T(8,128)(2,1)S(1)}, u32[]{:S(2)}, u32[]{:S(2)}) collective-permute-start(bf16[128,1152]{1,0:T(8,128)(2,1)} %get-tuple-element.417), channel_id=1, source_target_pairs={{0,2},{1,3},{2,0},{3,1},{4,6},{5,7},{6,4},{7,5},{8,10},{9,11},{10,... | collective-permute-start | bytes 884744 | tf_op jit(solution)/shard_map/ppermute | solution.py:553
  230.9 12.3 %all-to-all-start.2 = ((bf16[8,40,512]{2,1,0:T(8,128)(2,1)}), bf16[8,40,512]{2,1,0:T(8,128)(2,1)S(1)}, u32[]{:S(2)}, u32[]{:S(2)}) async-start(bf16[8,40,512]{2,1,0:T(8,128)(2,1)} %split_back.1), calls=%async_computation.2 | async-start | bytes 655360 | tf_op jit(solution)/shard_map/all_to_all | solution.py:1234
  (100 other events, 745.7 us)
where the time goes:
time: 246 us; the launch traced here: 245 us
  starting transfers between devices  78.7 us (32%)
  waiting for transfers between devices  68.9 us (28%)
  Pallas kernels  68.1 us (28%)
  local copies, waits for them, and re-layouts  14.1 us (6%)
  other arithmetic  9.88 us (4%)
  matrix products  3.33 us (1%)
    pallas_call x19, Pallas kernels, call(): pl.pallas_call(body, out_shape=outs, scratch_shapes=scratch, compiler_par...  68.1 us
    ppermute x47, starting transfers between devices, pc(): return lax.ppermute(value, 'ctx', [(s, s ^ k) for s in range(8)])  38.1 us
    ppermute x47, waiting for transfers between devices, pc(): return lax.ppermute(value, 'ctx', [(s, s ^ k) for s in range(8)])  31.5 us
    ppermute x18, waiting for transfers between devices, pz(): return lax.ppermute(value, 'grp', [(s, s ^ k) for s in range(4)])  29.2 us
    ppermute x18, starting transfers between devices, pz(): return lax.ppermute(value, 'grp', [(s, s ^ k) for s in range(4)])  27 us
    unnamed x160, local copies, waits for them, and re-layouts  11.2 us
    all_to_all x1, starting transfers between devices, fast_local(): packed = lax.all_to_all(packed, 'ctx', 0, 0, tiled=True)  5.42 us
    convert_element_type x5, other arithmetic, add_low(): return (a.astype(F32) + b.astype(F32)).astype(BF16)  5.38 us
  transfers between devices with their start and end apart: 68, of which 33 were waited for; matrix products, arithmetic and copies ran while one was open for 5% of the time, Pallas kernels for 18%

commit v1 on v0

--- a/solution.py
+++ b/solution.py
@@ -541,12 +541,15 @@
 POS = 64
 LEN = 512
 RELATIVE = (0, 2, 4, 6, 1, 3, 5, 7)
+STEP = 512
+STEPS = ALL // STEP
 F32 = jnp.float32
 BF16 = jnp.bfloat16
 SCALE = HEAD_SIZE ** (-0.5)
 NT = (((1,), (1,)), ((), ()))
 TN = (((0,), (0,)), ((), ()))
 MIB = 1024 * 1024
+LARGE = ("attend", "project", "feed", "back")
 
 
 def pc(value, k):
@@ -630,7 +633,7 @@
         body,
         out_shape=outs,
         scratch_shapes=scratch,
-        compiler_params=pltpu.CompilerParams(vmem_limit_bytes=32 * MIB),
+        compiler_params=pltpu.CompilerParams(vmem_limit_bytes=(32 if name in LARGE else 16) * MIB),
         cost_estimate=pl.CostEstimate(flops=0, bytes_accessed=1, transcendentals=0),
         name=name,
         **kwargs,
@@ -813,8 +816,8 @@
     t = pl.program_id(0)
     for j, a in zip(RELATIVE, (a0, a1, a2, a3, a4, a5, a6, a7)):
         h = i ^ j
-        for half in range(2):
-            b = 2 * t + half
+        for half in range(STEP // ROWS):
+            b = STEP // ROWS * t + half
             q = (2 * (b & 3) + (b >> 2)) ^ j
             start = pl.multiple_of(((q & 1) * 4 + (q >> 1)) * POS, POS)
             rows = a[pl.ds(start, POS), :]
@@ -860,15 +863,65 @@
     dgu_o[...] = dgu
     dm = lax.dot_general(dgu, gu[...], NT, preferred_element_type=F32)
     sums[0:1, :] = sums[0:1, :] + jnp.sum(dm * mixed.astype(F32), axis=0, keepdims=True)
-    dm = dm.astype(BF16).reshape(2, ROWS, W)
-
-    @pl.when(t < 2)
+    dm = dm.astype(BF16).reshape(4, ROWS, W)
+
+    @pl.when(t == 0)
     def _():
         pm[...] = dm
 
-    @pl.when(t >= 2)
+    @pl.when(t == 1)
     def _():
         pe[...] = dm
+
+
+def whole(*shape):
+    return pl.BlockSpec(shape, lambda t: (0,) * len(shape))
+
+
+def rows_at(rows, columns):
+    return pl.BlockSpec((rows, columns), lambda t: (t, 0))
+
+
+def run_project(sc, x, heads, w_out, gains):
+    return call(
+        project_body,
+        [hbm((ALL, W), BF16), sds((ALL, W), BF16), hbm((ROWS, W), F32)],
+        sc, x, *heads, w_out, gains,
+        grid=(STEPS,),
+        in_specs=[pl.BlockSpec(memory_space=pltpu.SMEM), rows_at(STEP, W)]
+        + [whole(LEN, 2 * HG)] * 8
+        + [whole(W, W), whole(8, W)],
+        out_specs=[rows_at(STEP, W), rows_at(STEP, W), whole(ROWS, W)],
+        scratch=[pltpu.VMEM((8, STEP, HG), BF16)], name="project",
+    )
+
+
+def run_feed(sc, mixed, c, feeds):
+    return call(
+        feed_body,
+        [
+            sds((ALL, HID), BF16),
+            sds((ALL, 2 * HID), BF16),
+            sds((4, ROWS, W), BF16),
+            sds((4, ROWS, W), BF16),
+            sds((HID, W), BF16),
+            sds((8, W), F32),
+        ],
+        sc, mixed, c, *feeds,
+        grid=(STEPS,),
+        in_specs=[pl.BlockSpec(memory_space=pltpu.SMEM), rows_at(STEP, W), rows_at(STEP, W)]
+        + [whole(288, 2 * HID)] * 4
+        + [whole(SUB, W)] * 4,
+        out_specs=[
+            rows_at(STEP, HID),
+            rows_at(STEP, 2 * HID),
+            whole(4, ROWS, W),
+            whole(4, ROWS, W),
+            whole(HID, W),
+            whole(8, W),
+        ],
+        scratch=[pltpu.VMEM((W, 2 * HID), BF16)], name="feed",
+    )
 
 
 def mid_body(a, b, d, f, c, res, gains, dres, low):
@@ -1055,6 +1108,7 @@
     x_late, seg_late, wo, wd, i_late, c_late = order((x_own, segments, wo, wd, i, c_own))
     o_own = wo.reshape(-1, 128)
     o_one, o_two = pz(o_own, 1), pz(o_own, 2)
+    c_near = pc(c_late, 2), pc(c_late, 4)
     seg = jnp.broadcast_to(seg_late.reshape(ROWS, 1).astype(BF16), (ROWS, 128))
     x_sent = order.then(jnp.concatenate([x_late, seg], 1))
     d_own = order.then(order(wd).reshape(SUB, W))
@@ -1079,17 +1133,17 @@
     prow = jnp.broadcast_to(positions.astype(F32)[None, :], (8, LEN))
     cosine, sine, pcol, prow = order.then((cosine, sine, pcol, prow))
 
+    c_near = order.wait(c_near)
     s_one = order.wait(s_one)
     o_three = pz(order(o_two), 1)
     s_two = order.wait(s_two)
     s_three = pz(s_two, 1)
     o_three = order.wait(o_three)
-    g_one = pz(order(feed), 1)
+    o_sent = order.then(jnp.stack([o_own, o_one, o_two, o_three]))
+    g_one, g_two = pz(order(feed), 1), pz(order(feed), 2)
     s_three = order.wait(s_three)
-    g_two = pz(order(feed), 2)
+    os = first_ctx(order(o_sent))
     xs = order.wait(both_cores(order.wait(xs)))
-    o_sent = order.then(jnp.stack([o_own, o_one, o_two, o_three]))
-    os = first_ctx(o_sent)
     xs, slabs = order((xs, (slab, s_one, s_two, s_three)))
 
     anywhere = pl.BlockSpec(memory_space=pl.ANY)
@@ -1129,51 +1183,14 @@
     d_three = pz(d_two, 1)
     heads[1], heads[2] = order.wait((heads[1], heads[2]))
     heads = order.wait(both_cores(order.wait(heads)))
-    cs = first_ctx(order(c_late))
+    cs = [c_late, *c_near, pc(order(c_late), 6)]
     g_three, d_three = order.wait((g_three, d_three))
 
-    whole = lambda *shape: pl.BlockSpec(shape, lambda t: (0,) * len(shape))
-    rowb = lambda n: pl.BlockSpec((256, n), lambda t: (t, 0))
-    smem = pl.BlockSpec(memory_space=pltpu.SMEM)
-    att_full, mixed, res_own = order.then(
-        call(
-            project_body,
-            [hbm((ALL, W), BF16), sds((ALL, W), BF16), hbm((ROWS, W), F32)],
-            sc, call_x, *late(heads), w_out, gains,
-            grid=(4,),
-            in_specs=[smem, rowb(W)] + [whole(LEN, 2 * HG)] * 8 + [whole(W, W), whole(8, W)],
-            out_specs=[rowb(W), rowb(W), whole(ROWS, W)],
-            scratch=[pltpu.VMEM((8, 256, HG), BF16)], name="project",
-        )
-    )
+    att_full, mixed, res_own = order.then(run_project(sc, call_x, late(heads), w_out, gains))
     wo_own = order.then(lax.dynamic_slice(order(w_out), (jnp.minimum(i, KEY_HEADS - 1) * HG, 0), (HG, W)))
     call_c = order.then(join(late(order(both_cores(order.wait(cs))))))
     feeds = order((feed, g_one, g_two, g_three, d_own, d_one, d_two, d_three))
-    hidden, dgu, pm, pe, down, dots_two = order.then(
-        call(
-            feed_body,
-            [
-                sds((ALL, HID), BF16),
-                sds((ALL, 2 * HID), BF16),
-                sds((4, ROWS, W), BF16),
-                sds((4, ROWS, W), BF16),
-                sds((HID, W), BF16),
-                sds((8, W), F32),
-            ],
-            sc, mixed, call_c, *late(feeds),
-            grid=(4,),
-            in_specs=[smem, rowb(W), rowb(W)] + [whole(288, 2 * HID)] * 4 + [whole(SUB, W)] * 4,
-            out_specs=[
-                rowb(HID),
-                rowb(2 * HID),
-                pl.BlockSpec((2, ROWS, W), lambda t: (jnp.minimum(t, 1), 0, 0)),
-                pl.BlockSpec((2, ROWS, W), lambda t: (jnp.maximum(t - 2, 0), 0, 0)),
-                whole(HID, W),
-                whole(8, W),
-            ],
-            scratch=[pltpu.VMEM((W, 2 * HID), BF16)], name="feed",
-        )
-    )
+    hidden, dgu, pm, pe, down, dots_two = order.then(run_feed(sc, mixed, call_c, late(feeds)))
 
     got = pc(pe, 1)
     grad_gu = order.then(lax.dot_general(order(mixed), dgu, TN, preferred_element_type=F32).astype(BF16))

time: 246 us -> 241 us (0.980)
  Pallas kernels: 68.1 us -> 65.6 us
    ppermute x47, waiting for transfers between devices: 31.5 us -> 34.4 us  [pc(): return lax.ppermute(value, 'ctx', [(s, s ^ k) for s in range(8)])]
    unnamed x160 -> x158, local copies, waits for them, and re-layouts: 11.2 us -> 11.9 us
  transfers between devices with their start and end apart: 68 -> 68, of which waited for: 33 -> 32; matrix products, arithmetic and copies ran while one was open for 5% -> 5% of each run, Pallas kernels for 18% -> 18%
where the time goes in v1:
time: 241 us; the launch traced here: 240 us
  starting transfers between devices  76.3 us (32%)
  waiting for transfers between devices  69.8 us (29%)
  Pallas kernels  65.6 us (27%)
  local copies, waits for them, and re-layouts  14.9 us (6%)
  other arithmetic  8.41 us (3%)
  matrix products  3.32 us (1%)
    pallas_call x19, Pallas kernels, call(): pl.pallas_call(body, out_shape=outs, scratch_shapes=scratch, compiler_par...  65.6 us
    ppermute x47, starting transfers between devices, pc(): return lax.ppermute(value, 'ctx', [(s, s ^ k) for s in range(8)])  37.4 us
    ppermute x47, waiting for transfers between devices, pc(): return lax.ppermute(value, 'ctx', [(s, s ^ k) for s in range(8)])  34.4 us
    ppermute x18, waiting for transfers between devices, pz(): return lax.ppermute(value, 'grp', [(s, s ^ k) for s in range(4)])  29.3 us
    ppermute x18, starting transfers between devices, pz(): return lax.ppermute(value, 'grp', [(s, s ^ k) for s in range(4)])  26.6 us
    unnamed x158, local copies, waits for them, and re-layouts  11.9 us
    all_to_all x1, starting transfers between devices, fast_local(): packed = lax.all_to_all(packed, 'ctx', 0, 0, tiled=True)  5.42 us
    convert_element_type x5, other arithmetic, add_low(): return (a.astype(F32) + b.astype(F32)).astype(BF16)  4.86 us
  transfers between devices with their start and end apart: 68, of which 32 were waited for; matrix products, arithmetic and copies ran while one was open for 5% of the time, Pallas kernels for 18%

profile of v1, /device:TPU:0, one launch (start us, length us, event | category | flops | bytes accessed | tf_op | source)
XLA Modules:
  0.0 239.9 jit_solution(11125125985784253625)
XLA Ops:
  1.5 2.4 %pack.1 = bf16[8,40,1152]{2,1,0:T(8,128)(2,1)} custom-call(bf16[324,128]{1,0:T(8,128)(2,1)} %bitcast.66, bf16[108,128]{1,0:T(8,128)(2,1)} %bitcast.73, bf16[108,128]{1,0:T(8,128)(2,1)} %bitcast.74, bf16[864,128]{1,0:T(8,128)(2,1)} %bitcast.64, bf16[864,128]{1,0:T(8,128)(2,1)} %bitcast.65, bf16[1,1152]{1,0:T(2,128)(2,1)S(1)} %dynamic_update_slice.3.gain), custom_call_target="tpu_custom_call" | custom-call | bytes 1 | tf_op jit(solution)/shard_map/pack/pallas_call | solution.py:632
  4.0 5.4 %all-to-all-start = ((bf16[8,40,1152]{2,1,0:T(8,128)(2,1)}), bf16[8,40,1152]{2,1,0:T(8,128)(2,1)S(1)}, u32[]{:S(2)}, u32[]{:S(2)}) async-start(bf16[8,40,1152]{2,1,0:T(8,128)(2,1)} %pack.1), calls=%async_computation | async-start | bytes 1474560 | tf_op jit(solution)/shard_map/all_to_all | solution.py:1106
  9.4 2.7 %collective-permute-start.1 = (bf16[324,128]{1,0:T(8,128)(2,1)S(1)}, bf16[324,128]{1,0:T(8,128)(2,1)S(1)}, u32[]{:S(2)}, u32[]{:S(2)}) collective-permute-start(bf16[324,128]{1,0:T(8,128)(2,1)S(1)} %bitcast.67), channel_id=1, source_target_pairs={{0,16},{8,24},{16,0},{24,8},{1,17},{9,25},{17,1},{25,9},{2,18},{10... | collective-permute-start | bytes 248840 | tf_op jit(solution)/shard_map/ppermute | solution.py:560
  13.6 2.0 collective-permute-start.8
  18.3 3.7 %all-to-all-done.src = bf16[8,40,1152]{2,1,0:T(8,128)(2,1)S(1)} async-done(((bf16[8,40,1152]{2,1,0:T(8,128)(2,1)}), bf16[8,40,1152]{2,1,0:T(8,128)(2,1)S(1)}, u32[]{:S(2)}, u32[]{:S(2)}) %all-to-all-start) | async-done | bytes 737312 | tf_op jit(solution)/shard_map/all_to_all | solution.py:1106
  23.7 2.6 %collective-permute-start.5 = (bf16[8,40,384]{2,1,0:T(8,128)(2,1)S(1)}, bf16[8,40,384]{2,1,0:T(8,128)(2,1)S(1)}, u32[]{:S(2)}, u32[]{:S(2)}) collective-permute-start(bf16[8,40,384]{2,1,0:T(8,128)(2,1)S(1)} %get-tuple-element.240.w0), channel_id=1, source_target_pairs={{0,16},{8,24},{16,0},{24,8},{1,17},{9,25},{17,1},{25,9},{2,18},{10... | collective-permute-start | bytes 737288 | tf_op jit(solution)/shard_map/ppermute | solution.py:560
  27.9 2.0 collective-permute-start.2
  30.0 1.8 collective-permute-done.6.w1
  31.8 2.1 collective-permute-done.5.w2
  36.0 5.1 %collective-permute-done.10 = bf16[324,128]{1,0:T(8,128)(2,1)S(1)} collective-permute-done((bf16[324,128]{1,0:T(8,128)(2,1)S(1)}, bf16[324,128]{1,0:T(8,128)(2,1)S(1)}, u32[]{:S(2)}, u32[]{:S(2)}) %collective-permute-start.10) | collective-permute-done | bytes 82976 | tf_op jit(solution)/shard_map/ppermute | solution.py:560
  42.9 2.7 %collective-permute-start.16 = (bf16[288,768]{1,0:T(8,128)(2,1)S(1)}, bf16[288,768]{1,0:T(8,128)(2,1)S(1)}, u32[]{:S(2)}, u32[]{:S(2)}) collective-permute-start(bf16[288,768]{1,0:T(8,128)(2,1)S(1)} %get-tuple-element.303.g0), channel_id=1, source_target_pairs={{0,16},{8,24},{16,0},{24,8},{1,17},{9,25},{17,1},{25,9},{2,18},{10... | collective-permute-start | bytes 1327112 | tf_op jit(solution)/shard_map/ppermute | solution.py:560
  47.2 1.8 collective-permute-start.21
  49.0 3.0 %collective-permute-start.20 = (bf16[4,324,128]{2,1,0:T(8,128)(2,1)S(1)}, bf16[4,324,128]{2,1,0:T(8,128)(2,1)}, u32[]{:S(2)}, u32[]{:S(2)}) collective-permute-start(bf16[4,324,128]{2,1,0:T(8,128)(2,1)S(1)} %pad_maximum_fusion.b0), channel_id=1, source_target_pairs={{0,4},{1,5},{2,6},{3,7},{4,0},{5,1},{6,2},{7,3},{8,12},{9,13},{10,... | collective-permute-start | bytes 995336 | tf_op jit(solution)/shard_map/ppermute | solution.py:556
  53.9 11.1 %attend.1 = (bf16[512,384]{1,0:T(8,128)(2,1)S(1)}, f32[8,1152]{1,0:T(8,128)S(1)}, bf16[1152,384]{1,0:T(8,128)(2,1)S(1)}, bf16[2,512,256]{2,1,0:T(8,128)(2,1)}, b...) custom-call(s32[2]{0:T(128)S(1)} %pad_add_fusion.sc, ...), custom_call_target="tpu_custom_call" | custom-call | bytes 1 | tf_op jit(solution)/shard_map/attend/pallas_call | solution.py:632
  67.9 2.7 %collective-permute-start.17 = (bf16[512,384]{1,0:T(8,128)(2,1)S(1)}, bf16[512,384]{1,0:T(8,128)(2,1)S(1)}, u32[]{:S(2)}, u32[]{:S(2)}) collective-permute-start(bf16[512,384]{1,0:T(8,128)(2,1)S(1)} %get-tuple-element.272.a0), channel_id=1, source_target_pairs={{0,2},{1,3},{2,0},{3,1},{4,6},{5,7},{6,4},{7,5},{8,10},{9,11},{10,... | collective-permute-start | bytes 1179656 | tf_op jit(solution)/shard_map/ppermute | solution.py:556
  73.1 2.5 %output_weight.1.wo = bf16[1152,1152]{1,0:T(8,128)(2,1)S(1)} custom-call(s32[2]{0:T(128)S(1)} %pad_add_fusion.sc, bf16[4,324,128]{2,1,0:T(8,128)(2,1)} %copy-done.20, bf16[4,324,128]{2,1,0:T(8,128)(2,1)} %collective-permute-done.19.b1, bf16[4,324,128]{2,1,0:T(8,128)(2,1)} %collective-permute-done.20.b2, bf16[4,324,128]{2,1,0:T(8,128)(2,1)} %collective-permute-done.21.b3, ...), custom_call_target="tpu_custom_call" | custom-call | bytes 1 | tf_op jit(solution)/shard_map/output_weight/pallas_call | solution.py:632
  75.7 1.8 collective-permute-start.27
  77.5 2.1 collective-permute-start.26
  81.7 6.7 %collective-permute-done.27.d2 = bf16[96,1152]{1,0:T(8,128)(2,1)} collective-permute-done((bf16[96,1152]{1,0:T(8,128)(2,1)S(1)}, bf16[96,1152]{1,0:T(8,128)(2,1)}, u32[]{:S(2)}, u32[]{:S(2)}) %collective-permute-start.27) | collective-permute-done | bytes 221216 | tf_op jit(solution)/shard_map/ppermute | solution.py:560
  93.5 2.1 collective-permute-start.33
  100.0 8.6 %project.1 = (bf16[1024,1152]{1,0:T(8,128)(2,1)}, bf16[1024,1152]{1,0:T(8,128)(2,1)S(1)}, f32[128,1152]{1,0:T(8,128)}) custom-call(s32[2]{0:T(128)S(1)} %pad_add_fusion.sc, bf16[1024,1152]{1,0:T(8,128)(2,1)S(1)} %copy-done.9, bf16[512,384]{1,0:T(8,128)(2,1)} %copy-done.15, bf16[512,384]{1,0:T(8,128)(2,1)} %copy-done.31, bf16[512,384]{1,0:T(8,128)(2,1)} %copy-done.30, ...), custom_call_target="tpu_custom_call" | custom-call | bytes 1 | tf_op jit(solution)/shard_map/project/pallas_call | solution.py:632
  109.3 3.1 %collective-permute-done.39.d3 = bf16[96,1152]{1,0:T(8,128)(2,1)S(1)} collective-permute-done((bf16[96,1152]{1,0:T(8,128)(2,1)}, bf16[96,1152]{1,0:T(8,128)(2,1)S(1)}, u32[]{:S(2)}, u32[]{:S(2)}) %collective-permute-start.39) | collective-permute-done | bytes 221216 | tf_op jit(solution)/shard_map/ppermute | solution.py:560
  116.7 8.7 %feed.1 = (bf16[1024,384]{1,0:T(8,128)(2,1)S(1)}, bf16[1024,768]{1,0:T(8,128)(2,1)S(1)}, bf16[4,128,1152]{2,1,0:T(8,128)(2,1)S(1)}, bf16[4,128,1152]{2,1,0:T(8,1...) custom-call(s32[2]{0:T(128)S(1)} %pad_add_fusion.sc, ...), custom_call_target="tpu_custom_call" | custom-call | bytes 1 | tf_op jit(solution)/shard_map/feed/pallas_call | solution.py:632
  125.6 2.1 convolution_convert_fusion.grad_gu
  130.6 2.3 grads.1
  135.7 2.1 collective-permute-start.44
  138.5 4.8 %collective-permute-done.43.d = bf16[128,1152]{1,0:T(8,128)(2,1)S(1)} collective-permute-done((bf16[128,1152]{1,0:T(8,128)(2,1)S(1)}, bf16[128,1152]{1,0:T(8,128)(2,1)S(1)}, u32[]{:S(2)}, u32[]{:S(2)}) %collective-permute-start.43) | collective-permute-done | bytes 294944 | tf_op jit(solution)/shard_map/ppermute | solution.py:556
  143.3 2.0 collective-permute-done.42.b
  145.3 5.3 %collective-permute-done.44.f = bf16[128,1152]{1,0:T(8,128)(2,1)S(1)} collective-permute-done((bf16[128,1152]{1,0:T(8,128)(2,1)S(1)}, bf16[128,1152]{1,0:T(8,128)(2,1)S(1)}, u32[]{:S(2)}, u32[]{:S(2)}) %collective-permute-start.44) | collective-permute-done | bytes 294944 | tf_op jit(solution)/shard_map/ppermute | solution.py:556
  151.3 2.9 %mid.1 = (f32[128,1152]{1,0:T(8,128)}, bf16[128,1152]{1,0:T(8,128)(2,1)}) custom-call(bf16[128,1152]{1,0:T(8,128)(2,1)} %get-tuple-element.323.a, bf16[128,1152]{1,0:T(8,128)(2,1)} %copy-done.67, bf16[128,1152]{1,0:T(8,128)(2,1)} %copy-done.66, bf16[128,1152]{1,0:T(8,128)(2,1)} %copy-done.68, bf16[128,1152]{1,0:T(8,128)(2,1)} %bitcast.3.refs_0_.c, ...), custom_call_target="tpu_custom_call" | custom-call | bytes 1 | tf_op jit(solution)/shard_map/mid/pallas_call | solution.py:632
  159.5 2.3 collective-permute-start.57
  163.2 3.5 %collective-permute-done.51.l3 = bf16[128,1152]{1,0:T(8,128)(2,1)S(1)} collective-permute-done((bf16[128,1152]{1,0:T(8,128)(2,1)S(1)}, bf16[128,1152]{1,0:T(8,128)(2,1)S(1)}, u32[]{:S(2)}, u32[]{:S(2)}) %collective-permute-start.51) | collective-permute-done | bytes 294944 | tf_op jit(solution)/shard_map/ppermute | solution.py:556
  166.7 5.4 %collective-permute-done.50.l2 = bf16[128,1152]{1,0:T(8,128)(2,1)S(1)} collective-permute-done((bf16[128,1152]{1,0:T(8,128)(2,1)S(1)}, bf16[128,1152]{1,0:T(8,128)(2,1)S(1)}, u32[]{:S(2)}, u32[]{:S(2)}) %collective-permute-start.50) | collective-permute-done | bytes 294944 | tf_op jit(solution)/shard_map/ppermute | solution.py:556
  176.2 10.7 %back.1 = (bf16[1024,384]{1,0:T(8,128)(2,1)S(1)}, bf16[304,512]{1,0:T(8,128)(2,1)S(1)}, bf16[304,512]{1,0:T(8,128)(2,1)S(1)}, bf16[304,512]{1,0:T(8,128)(2,1)S(1)}, bf16[304,512]{1,0:T(8,128)(2,1)S(1)}) custom-call(s32[2]{0:T(128)S(1)} %pad_add_fusion.sc, bf16[128,1152]{1,0:T(8,128)(2,1)} %get-tuple-element.338.l0, bf16[128,1152]{1,0:T(8,128)(2,1)} %copy-done.54, ...), custom_call_target="tpu_custom_call" | custom-call | bytes 1 | tf_op jit(solution)/shard_map/back/pallas_call | solution.py:632
  186.8 5.2 %collective-permute-done.56.b = bf16[432,768]{1,0:T(8,128)(2,1)S(1)} collective-permute-done((bf16[432,768]{1,0:T(8,128)(2,1)S(1)}, bf16[432,768]{1,0:T(8,128)(2,1)S(1)}, u32[]{:S(2)}, u32[]{:S(2)}) %collective-permute-start.56) | collective-permute-done | bytes 663584 | tf_op jit(solution)/shard_map/ppermute | solution.py:560
  193.1 2.6 %split_feed.1 = (bf16[8,36,768]{2,1,0:T(8,128)(2,1)}, f32[864,128]{1,0:T(8,128)}) custom-call(bf16[432,768]{1,0:T(8,128)(2,1)} %get-tuple-element.355.a, bf16[432,768]{1,0:T(8,128)(2,1)} %copy-done.25, bf16[432,768]{1,0:T(8,128)(2,1)} %copy-done.24), custom_call_target="tpu_custom_call" | custom-call | bytes 1 | tf_op jit(solution)/shard_map/split_feed/pallas_call | solution.py:632
  195.7 2.6 %inward.1 = (bf16[4,128,1152]{2,1,0:T(8,128)(2,1)S(1)}, bf16[4,128,1152]{2,1,0:T(8,128)(2,1)}) custom-call(bf16[1024,384]{1,0:T(8,128)(2,1)S(1)} %get-tuple-element.359.rows, bf16[1152,384]{1,0:T(8,128)(2,1)S(1)} %get-tuple-element.349.w_slab.weight), custom_call_target="tpu_custom_call" | custom-call | bytes 1 | tf_op jit(solution)/shard_map/inward/pallas_call | solution.py:632
  202.3 3.5 %all-to-all-start.1 = ((bf16[8,36,768]{2,1,0:T(8,128)(2,1)}), bf16[8,36,768]{2,1,0:T(8,128)(2,1)S(1)}, u32[]{:S(2)}, u32[]{:S(2)}) async-start(bf16[8,36,768]{2,1,0:T(8,128)(2,1)} %get-tuple-element.372), calls=%async_computation.1 | async-start | bytes 983040 | tf_op jit(solution)/shard_map/all_to_all | solution.py:1239
  205.8 2.4 collective-permute-done.59
  209.7 2.5 %fusion.11 = (bf16[128,1152]{1,0:T(8,128)(2,1)}, bf16[128,1152]{1,0:T(8,128)(2,1)}, bf16[128,1152]{1,0:T(8,128)(2,1)}, bf16[128,1152]{1,0:T(8,128)(2,1)}) fusion(bf16[4,128,1152]{2,1,0:T(8,128)(2,1)} %collective-permute-done.58, bf16[4,128,1152]{2,1,0:T(8,128)(2,1)S(1)} %get-tuple-element.360), kind=kLoop, calls=%fused_computation.32 | loop fusion | flops 2359296 | bytes 3538944 | tf_op jit(solution)/shard_map/convert_element_type | solution.py:587
  212.2 3.4 %collective-permute-done.47 = bf16[128,1152]{1,0:T(8,128)(2,1)} collective-permute-done((bf16[128,1152]{1,0:T(8,128)(2,1)}, bf16[128,1152]{1,0:T(8,128)(2,1)}, u32[]{:S(2)}, u32[]{:S(2)}) %collective-permute-start.47) | collective-permute-done | bytes 294944 | tf_op jit(solution)/shard_map/ppermute | solution.py:556
  219.0 2.0 add_convert_fusion.5
  222.5 2.3 collective-permute-done.64.d
  225.5 2.0 split_back.1
  227.6 3.4 %all-to-all-start.2 = ((bf16[8,40,512]{2,1,0:T(8,128)(2,1)}), bf16[8,40,512]{2,1,0:T(8,128)(2,1)S(1)}, u32[]{:S(2)}, u32[]{:S(2)}) async-start(bf16[8,40,512]{2,1,0:T(8,128)(2,1)} %split_back.1), calls=%async_computation.2 | async-start | bytes 655360 | tf_op jit(solution)/shard_map/all_to_all | solution.py:1251
  231.0 2.0 collective-permute-done.61.d
  233.9 2.6 %last.1 = bf16[128,1152]{1,0:T(8,128)(2,1)} custom-call(bf16[128,1152]{1,0:T(8,128)(2,1)} %get-tuple-element.378.a, bf16[128,1152]{1,0:T(8,128)(2,1)} %copy-done.57, bf16[128,1152]{1,0:T(8,128)(2,1)} %copy-done.56, bf16[128,1152]{1,0:T(8,128)(2,1)} %copy-done.55, bf16[128,1152]{1,0:T(8,128)(2,1)} %bitcast.59, f32[128,1152]{1,0:T(8,128)} %get-tuple-element.382.dres, ...), custom_call_target="tpu_custom_call" | custom-call | bytes 1 | tf_op jit(solution)/shard_map/last/pallas_call | solution.py:632
  236.5 2.0 all-to-all-done.2.src
  (295 shorter events, 69.9 us)
Async XLA Ops:
  4.0 18.0 %all-to-all-start = ((bf16[8,40,1152]{2,1,0:T(8,128)(2,1)}), bf16[8,40,1152]{2,1,0:T(8,128)(2,1)S(1)}, u32[]{:S(2)}, u32[]{:S(2)}) async-start(bf16[8,40,1152]{2,1,0:T(8,128)(2,1)} %pack.1), calls=%async_computation | async-start | bytes 1474560 | tf_op jit(solution)/shard_map/all_to_all | solution.py:1106
  9.4 8.9 %collective-permute-start.1 = (bf16[324,128]{1,0:T(8,128)(2,1)S(1)}, bf16[324,128]{1,0:T(8,128)(2,1)S(1)}, u32[]{:S(2)}, u32[]{:S(2)}) collective-permute-start(bf16[324,128]{1,0:T(8,128)(2,1)S(1)} %bitcast.67), channel_id=1, source_target_pairs={{0,16},{8,24},{16,0},{24,8},{1,17},{9,25},{17,1},{25,9},{2,18},{10... | collective-permute-start | bytes 248840 | tf_op jit(solution)/shard_map/ppermute | solution.py:560
  12.0 6.2 %collective-permute-start = (bf16[324,128]{1,0:T(8,128)(2,1)S(1)}, bf16[324,128]{1,0:T(8,128)(2,1)S(1)}, u32[]{:S(2)}, u32[]{:S(2)}) collective-permute-start(bf16[324,128]{1,0:T(8,128)(2,1)S(1)} %bitcast.68), channel_id=1, source_target_pairs={{0,8},{8,0},{16,24},{24,16},{1,9},{9,1},{17,25},{25,17},{2,10},{10... | collective-permute-start | bytes 248840 | tf_op jit(solution)/shard_map/ppermute | solution.py:560
  13.6 13.3 %collective-permute-start.8 = (bf16[128,1152]{1,0:T(8,128)(2,1)}, bf16[128,1152]{1,0:T(8,128)(2,1)}, u32[]{:S(2)}, u32[]{:S(2)}) collective-permute-start(bf16[128,1152]{1,0:T(8,128)(2,1)} %bitcast.3.refs_0_.c), channel_id=1, source_target_pairs={{0,4},{1,5},{2,6},{3,7},{4,0},{5,1},{6,2},{7,3},{8,12},{9,13},{10,... | collective-permute-start | bytes 884744 | tf_op jit(solution)/shard_map/ppermute | solution.py:556
  15.6 12.3 %collective-permute-start.7 = (bf16[128,1152]{1,0:T(8,128)(2,1)}, bf16[128,1152]{1,0:T(8,128)(2,1)S(1)}, u32[]{:S(2)}, u32[]{:S(2)}) collective-permute-start(bf16[128,1152]{1,0:T(8,128)(2,1)} %bitcast.3.refs_0_.c), channel_id=1, source_target_pairs={{0,2},{1,3},{2,0},{3,1},{4,6},{5,7},{6,4},{7,5},{8,10},{9,11},{10,... | collective-permute-start | bytes 884744 | tf_op jit(solution)/shard_map/ppermute | solution.py:556
  22.1 9.8 %collective-permute-start.6 = (bf16[8,40,384]{2,1,0:T(8,128)(2,1)S(1)}, bf16[8,40,384]{2,1,0:T(8,128)(2,1)S(1)}, u32[]{:S(2)}, u32[]{:S(2)}) collective-permute-start(bf16[8,40,384]{2,1,0:T(8,128)(2,1)S(1)} %get-tuple-element.240.w0), channel_id=1, source_target_pairs={{0,8},{8,0},{16,24},{24,16},{1,9},{9,1},{17,25},{25,17},{2,10},{10... | collective-permute-start | bytes 737288 | tf_op jit(solution)/shard_map/ppermute | solution.py:560
  23.7 10.2 %collective-permute-start.5 = (bf16[8,40,384]{2,1,0:T(8,128)(2,1)S(1)}, bf16[8,40,384]{2,1,0:T(8,128)(2,1)S(1)}, u32[]{:S(2)}, u32[]{:S(2)}) collective-permute-start(bf16[8,40,384]{2,1,0:T(8,128)(2,1)S(1)} %get-tuple-element.240.w0), channel_id=1, source_target_pairs={{0,16},{8,24},{16,0},{24,8},{1,17},{9,25},{17,1},{25,9},{2,18},{10... | collective-permute-start | bytes 737288 | tf_op jit(solution)/shard_map/ppermute | solution.py:560
  26.3 14.8 %collective-permute-start.4 = (bf16[128,1280]{1,0:T(8,128)(2,1)S(1)}, bf16[128,1280]{1,0:T(8,128)(2,1)S(1)}, u32[]{:S(2)}, u32[]{:S(2)}) collective-permute-start(bf16[128,1280]{1,0:T(8,128)(2,1)S(1)} %pad_maximum_fusion.1.x0), channel_id=1, source_target_pairs={{0,6},{1,7},{2,4},{3,5},{4,2},{5,3},{6,0},{7,1},{8,14},{9,15},{10,... | collective-permute-start | bytes 983048 | tf_op jit(solution)/shard_map/ppermute | solution.py:556
  26.9 14.9 %collective-permute-start.3 = (bf16[128,1280]{1,0:T(8,128)(2,1)S(1)}, bf16[128,1280]{1,0:T(8,128)(2,1)S(1)}, u32[]{:S(2)}, u32[]{:S(2)}) collective-permute-start(bf16[128,1280]{1,0:T(8,128)(2,1)S(1)} %pad_maximum_fusion.1.x0), channel_id=1, source_target_pairs={{0,4},{1,5},{2,6},{3,7},{4,0},{5,1},{6,2},{7,3},{8,12},{9,13},{10,... | collective-permute-start | bytes 983048 | tf_op jit(solution)/shard_map/ppermute | solution.py:556
  27.9 14.0 %collective-permute-start.2 = (bf16[128,1280]{1,0:T(8,128)(2,1)S(1)}, bf16[128,1280]{1,0:T(8,128)(2,1)}, u32[]{:S(2)}, u32[]{:S(2)}) collective-permute-start(bf16[128,1280]{1,0:T(8,128)(2,1)S(1)} %pad_maximum_fusion.1.x0), channel_id=1, source_target_pairs={{0,2},{1,3},{2,0},{3,1},{4,6},{5,7},{6,4},{7,5},{8,10},{9,11},{10,... | collective-permute-start | bytes 983048 | tf_op jit(solution)/shard_map/ppermute | solution.py:556
  33.9 7.2 %collective-permute-start.9 = (bf16[8,40,384]{2,1,0:T(8,128)(2,1)S(1)}, bf16[8,40,384]{2,1,0:T(8,128)(2,1)S(1)}, u32[]{:S(2)}, u32[]{:S(2)}) collective-permute-start(bf16[8,40,384]{2,1,0:T(8,128)(2,1)S(1)} %collective-permute-done.5.w2), channel_id=1, source_target_pairs={{0,8},{8,0},{16,24},{24,16},{1,9},{9,1},{17,25},{25,17},{2,10},{10... | collective-permute-start | bytes 737288 | tf_op jit(solution)/shard_map/ppermute | solution.py:560
  34.8 6.3 %collective-permute-start.10 = (bf16[324,128]{1,0:T(8,128)(2,1)S(1)}, bf16[324,128]{1,0:T(8,128)(2,1)S(1)}, u32[]{:S(2)}, u32[]{:S(2)}) collective-permute-start(bf16[324,128]{1,0:T(8,128)(2,1)S(1)} %collective-permute-done.1), channel_id=1, source_target_pairs={{0,8},{8,0},{16,24},{24,16},{1,9},{9,1},{17,25},{25,17},{2,10},{10... | collective-permute-start | bytes 248840 | tf_op jit(solution)/shard_map/ppermute | solution.py:560
  42.4 6.6 %collective-permute-start.13 = (bf16[128,1280]{1,0:T(8,128)(2,1)S(1)}, bf16[128,1280]{1,0:T(8,128)(2,1)S(1)}, u32[]{:S(2)}, u32[]{:S(2)}) collective-permute-start(bf16[128,1280]{1,0:T(8,128)(2,1)S(1)} %collective-permute-done.3.x2), channel_id=1, source_target_pairs={{0,1},{1,0},{2,3},{3,2},{4,5},{5,4},{6,7},{7,6},{8,9},{9,8},{10,11... | collective-permute-start | bytes 983048 | tf_op jit(solution)/shard_map/ppermute | solution.py:556
  42.4 9.6 %collective-permute-start.14 = (bf16[128,1280]{1,0:T(8,128)(2,1)S(1)}, bf16[128,1280]{1,0:T(8,128)(2,1)S(1)}, u32[]{:S(2)}, u32[]{:S(2)}) collective-permute-start(bf16[128,1280]{1,0:T(8,128)(2,1)S(1)} %collective-permute-done.4.x3), channel_id=1, source_target_pairs={{0,1},{1,0},{2,3},{3,2},{4,5},{5,4},{6,7},{7,6},{8,9},{9,8},{10,11... | collective-permute-start | bytes 983048 | tf_op jit(solution)/shard_map/ppermute | solution.py:556
  42.9 22.7 %collective-permute-start.16 = (bf16[288,768]{1,0:T(8,128)(2,1)S(1)}, bf16[288,768]{1,0:T(8,128)(2,1)S(1)}, u32[]{:S(2)}, u32[]{:S(2)}) collective-permute-start(bf16[288,768]{1,0:T(8,128)(2,1)S(1)} %get-tuple-element.303.g0), channel_id=1, source_target_pairs={{0,16},{8,24},{16,0},{24,8},{1,17},{9,25},{17,1},{25,9},{2,18},{10... | collective-permute-start | bytes 1327112 | tf_op jit(solution)/shard_map/ppermute | solution.py:560
  45.6 20.2 %collective-permute-start.15 = (bf16[288,768]{1,0:T(8,128)(2,1)S(1)}, bf16[288,768]{1,0:T(8,128)(2,1)S(1)}, u32[]{:S(2)}, u32[]{:S(2)}) collective-permute-start(bf16[288,768]{1,0:T(8,128)(2,1)S(1)} %get-tuple-element.303.g0), channel_id=1, source_target_pairs={{0,8},{8,0},{16,24},{24,16},{1,9},{9,1},{17,25},{25,17},{2,10},{10... | collective-permute-start | bytes 1327112 | tf_op jit(solution)/shard_map/ppermute | solution.py:560
  47.2 18.6 %collective-permute-start.21 = (bf16[4,324,128]{2,1,0:T(8,128)(2,1)S(1)}, bf16[4,324,128]{2,1,0:T(8,128)(2,1)}, u32[]{:S(2)}, u32[]{:S(2)}) collective-permute-start(bf16[4,324,128]{2,1,0:T(8,128)(2,1)S(1)} %pad_maximum_fusion.b0), channel_id=1, source_target_pairs={{0,6},{1,7},{2,4},{3,5},{4,2},{5,3},{6,0},{7,1},{8,14},{9,15},{10,... | collective-permute-start | bytes 995336 | tf_op jit(solution)/shard_map/ppermute | solution.py:556
  49.0 16.8 %collective-permute-start.20 = (bf16[4,324,128]{2,1,0:T(8,128)(2,1)S(1)}, bf16[4,324,128]{2,1,0:T(8,128)(2,1)}, u32[]{:S(2)}, u32[]{:S(2)}) collective-permute-start(bf16[4,324,128]{2,1,0:T(8,128)(2,1)S(1)} %pad_maximum_fusion.b0), channel_id=1, source_target_pairs={{0,4},{1,5},{2,6},{3,7},{4,0},{5,1},{6,2},{7,3},{8,12},{9,13},{10,... | collective-permute-start | bytes 995336 | tf_op jit(solution)/shard_map/ppermute | solution.py:556
  52.1 13.7 %collective-permute-start.19 = (bf16[4,324,128]{2,1,0:T(8,128)(2,1)S(1)}, bf16[4,324,128]{2,1,0:T(8,128)(2,1)}, u32[]{:S(2)}, u32[]{:S(2)}) collective-permute-start(bf16[4,324,128]{2,1,0:T(8,128)(2,1)S(1)} %pad_maximum_fusion.b0), channel_id=1, source_target_pairs={{0,2},{1,3},{2,0},{3,1},{4,6},{5,7},{6,4},{7,5},{8,10},{9,11},{10,... | collective-permute-start | bytes 995336 | tf_op jit(solution)/shard_map/ppermute | solution.py:556
  66.9 21.4 %collective-permute-start.18 = (bf16[512,384]{1,0:T(8,128)(2,1)S(1)}, bf16[512,384]{1,0:T(8,128)(2,1)S(1)}, u32[]{:S(2)}, u32[]{:S(2)}) collective-permute-start(bf16[512,384]{1,0:T(8,128)(2,1)S(1)} %get-tuple-element.272.a0), channel_id=1, source_target_pairs={{0,4},{1,5},{2,6},{3,7},{4,0},{5,1},{6,2},{7,3},{8,12},{9,13},{10,... | collective-permute-start | bytes 1179656 | tf_op jit(solution)/shard_map/ppermute | solution.py:556
  67.9 20.4 %collective-permute-start.17 = (bf16[512,384]{1,0:T(8,128)(2,1)S(1)}, bf16[512,384]{1,0:T(8,128)(2,1)S(1)}, u32[]{:S(2)}, u32[]{:S(2)}) collective-permute-start(bf16[512,384]{1,0:T(8,128)(2,1)S(1)} %get-tuple-element.272.a0), channel_id=1, source_target_pairs={{0,2},{1,3},{2,0},{3,1},{4,6},{5,7},{6,4},{7,5},{8,10},{9,11},{10,... | collective-permute-start | bytes 1179656 | tf_op jit(solution)/shard_map/ppermute | solution.py:556
  70.7 18.4 %collective-permute-start.28 = (bf16[512,384]{1,0:T(8,128)(2,1)S(1)}, bf16[512,384]{1,0:T(8,128)(2,1)S(1)}, u32[]{:S(2)}, u32[]{:S(2)}) collective-permute-start(bf16[512,384]{1,0:T(8,128)(2,1)S(1)} %get-tuple-element.272.a0), channel_id=1, source_target_pairs={{0,6},{1,7},{2,4},{3,5},{4,2},{5,3},{6,0},{7,1},{8,14},{9,15},{10,... | collective-permute-start | bytes 1179656 | tf_op jit(solution)/shard_map/ppermute | solution.py:556
  75.7 12.7 %collective-permute-start.27 = (bf16[96,1152]{1,0:T(8,128)(2,1)S(1)}, bf16[96,1152]{1,0:T(8,128)(2,1)}, u32[]{:S(2)}, u32[]{:S(2)}) collective-permute-start(bf16[96,1152]{1,0:T(8,128)(2,1)S(1)} %copy-done.23), channel_id=1, source_target_pairs={{0,16},{8,24},{16,0},{24,8},{1,17},{9,25},{17,1},{25,9},{2,18},{10... | collective-permute-start | bytes 663560 | tf_op jit(solution)/shard_map/ppermute | solution.py:560
  77.5 10.8 %collective-permute-start.26 = (bf16[96,1152]{1,0:T(8,128)(2,1)S(1)}, bf16[96,1152]{1,0:T(8,128)(2,1)S(1)}, u32[]{:S(2)}, u32[]{:S(2)}) collective-permute-start(bf16[96,1152]{1,0:T(8,128)(2,1)S(1)} %copy-done.23), channel_id=1, source_target_pairs={{0,8},{8,0},{16,24},{24,16},{1,9},{9,1},{17,25},{25,17},{2,10},{10... | collective-permute-start | bytes 663560 | tf_op jit(solution)/shard_map/ppermute | solution.py:560
  93.5 15.2 %collective-permute-start.33 = (bf16[128,1152]{1,0:T(8,128)(2,1)}, bf16[128,1152]{1,0:T(8,128)(2,1)}, u32[]{:S(2)}, u32[]{:S(2)}) collective-permute-start(bf16[128,1152]{1,0:T(8,128)(2,1)} %bitcast.3.refs_0_.c), channel_id=1, source_target_pairs={{0,6},{1,7},{2,4},{3,5},{4,2},{5,3},{6,0},{7,1},{8,14},{9,15},{10,... | collective-permute-start | bytes 884744 | tf_op jit(solution)/shard_map/ppermute | solution.py:556
  95.5 16.9 %collective-permute-start.38 = (bf16[288,768]{1,0:T(8,128)(2,1)}, bf16[288,768]{1,0:T(8,128)(2,1)S(1)}, u32[]{:S(2)}, u32[]{:S(2)}) collective-permute-start(bf16[288,768]{1,0:T(8,128)(2,1)} %copy-done.27), channel_id=1, source_target_pairs={{0,8},{8,0},{16,24},{24,16},{1,9},{9,1},{17,25},{25,17},{2,10},{10... | collective-permute-start | bytes 1327112 | tf_op jit(solution)/shard_map/ppermute | solution.py:560
  97.0 15.4 %collective-permute-start.39 = (bf16[96,1152]{1,0:T(8,128)(2,1)}, bf16[96,1152]{1,0:T(8,128)(2,1)S(1)}, u32[]{:S(2)}, u32[]{:S(2)}) collective-permute-start(bf16[96,1152]{1,0:T(8,128)(2,1)} %collective-permute-done.27.d2), channel_id=1, source_target_pairs={{0,8},{8,0},{16,24},{24,16},{1,9},{9,1},{17,25},{25,17},{2,10},{10... | collective-permute-start | bytes 663560 | tf_op jit(solution)/shard_map/ppermute | solution.py:560
  132.8 21.3 %collective-permute-start.41 = (bf16[432,768]{1,0:T(8,128)(2,1)}, bf16[432,768]{1,0:T(8,128)(2,1)S(1)}, u32[]{:S(2)}, u32[]{:S(2)}) collective-permute-start(bf16[432,768]{1,0:T(8,128)(2,1)} %get-tuple-element.320), channel_id=1, source_target_pairs={{0,8},{8,0},{16,24},{24,16},{1,9},{9,1},{17,25},{25,17},{2,10},{10... | collective-permute-start | bytes 1990664 | tf_op jit(solution)/shard_map/ppermute | solution.py:560
  134.3 9.0 %collective-permute-start.43 = (bf16[128,1152]{1,0:T(8,128)(2,1)S(1)}, bf16[128,1152]{1,0:T(8,128)(2,1)S(1)}, u32[]{:S(2)}, u32[]{:S(2)}) collective-permute-start(bf16[128,1152]{1,0:T(8,128)(2,1)S(1)} %get-tuple-element.428), channel_id=1, source_target_pairs={{0,4},{1,5},{2,6},{3,7},{4,0},{5,1},{6,2},{7,3},{8,12},{9,13},{10,... | collective-permute-start | bytes 884744 | tf_op jit(solution)/shard_map/ppermute | solution.py:556
  135.4 9.9 %collective-permute-start.42 = (bf16[128,1152]{1,0:T(8,128)(2,1)S(1)}, bf16[128,1152]{1,0:T(8,128)(2,1)S(1)}, u32[]{:S(2)}, u32[]{:S(2)}) collective-permute-start(bf16[128,1152]{1,0:T(8,128)(2,1)S(1)} %get-tuple-element.429), channel_id=1, source_target_pairs={{0,2},{1,3},{2,0},{3,1},{4,6},{5,7},{6,4},{7,5},{8,10},{9,11},{10,... | collective-permute-start | bytes 884744 | tf_op jit(solution)/shard_map/ppermute | solution.py:556
  135.7 14.9 %collective-permute-start.44 = (bf16[128,1152]{1,0:T(8,128)(2,1)S(1)}, bf16[128,1152]{1,0:T(8,128)(2,1)S(1)}, u32[]{:S(2)}, u32[]{:S(2)}) collective-permute-start(bf16[128,1152]{1,0:T(8,128)(2,1)S(1)} %get-tuple-element.431), channel_id=1, source_target_pairs={{0,6},{1,7},{2,4},{3,5},{4,2},{5,3},{6,0},{7,1},{8,14},{9,15},{10,... | collective-permute-start | bytes 884744 | tf_op jit(solution)/shard_map/ppermute | solution.py:556
  155.9 10.8 %collective-permute-start.51 = (bf16[128,1152]{1,0:T(8,128)(2,1)S(1)}, bf16[128,1152]{1,0:T(8,128)(2,1)S(1)}, u32[]{:S(2)}, u32[]{:S(2)}) collective-permute-start(bf16[128,1152]{1,0:T(8,128)(2,1)S(1)} %copy-done.51), channel_id=1, source_target_pairs={{0,6},{1,7},{2,4},{3,5},{4,2},{5,3},{6,0},{7,1},{8,14},{9,15},{10,... | collective-permute-start | bytes 884744 | tf_op jit(solution)/shard_map/ppermute | solution.py:556
  156.8 15.4 %collective-permute-start.50 = (bf16[128,1152]{1,0:T(8,128)(2,1)S(1)}, bf16[128,1152]{1,0:T(8,128)(2,1)S(1)}, u32[]{:S(2)}, u32[]{:S(2)}) collective-permute-start(bf16[128,1152]{1,0:T(8,128)(2,1)S(1)} %copy-done.51), channel_id=1, source_target_pairs={{0,4},{1,5},{2,6},{3,7},{4,0},{5,1},{6,2},{7,3},{8,12},{9,13},{10,... | collective-permute-start | bytes 884744 | tf_op jit(solution)/shard_map/ppermute | solution.py:556
  157.7 14.5 %collective-permute-start.49 = (bf16[128,1152]{1,0:T(8,128)(2,1)S(1)}, bf16[128,1152]{1,0:T(8,128)(2,1)S(1)}, u32[]{:S(2)}, u32[]{:S(2)}) collective-permute-start(bf16[128,1152]{1,0:T(8,128)(2,1)S(1)} %copy-done.51), channel_id=1, source_target_pairs={{0,2},{1,3},{2,0},{3,1},{4,6},{5,7},{6,4},{7,5},{8,10},{9,11},{10,... | collective-permute-start | bytes 884744 | tf_op jit(solution)/shard_map/ppermute | solution.py:556
  159.5 32.6 %collective-permute-start.57 = (bf16[432,768]{1,0:T(8,128)(2,1)S(1)}, bf16[432,768]{1,0:T(8,128)(2,1)S(1)}, u32[]{:S(2)}, u32[]{:S(2)}) collective-permute-start(bf16[432,768]{1,0:T(8,128)(2,1)S(1)} %add_convert_fusion), channel_id=1, source_target_pairs={{0,16},{8,24},{16,0},{24,8},{1,17},{9,25},{17,1},{25,9},{2,18},{10... | collective-permute-start | bytes 1990664 | tf_op jit(solution)/shard_map/ppermute | solution.py:560
  161.8 30.3 %collective-permute-start.56 = (bf16[432,768]{1,0:T(8,128)(2,1)S(1)}, bf16[432,768]{1,0:T(8,128)(2,1)S(1)}, u32[]{:S(2)}, u32[]{:S(2)}) collective-permute-start(bf16[432,768]{1,0:T(8,128)(2,1)S(1)} %copy-done.76), channel_id=1, source_target_pairs={{0,8},{8,0},{16,24},{24,16},{1,9},{9,1},{17,25},{25,17},{2,10},{10... | collective-permute-start | bytes 1990664 | tf_op jit(solution)/shard_map/ppermute | solution.py:560
  198.3 10.0 %collective-permute-start.58 = (bf16[4,128,1152]{2,1,0:T(8,128)(2,1)}, bf16[4,128,1152]{2,1,0:T(8,128)(2,1)}, u32[]{:S(2)}, u32[]{:S(2)}) collective-permute-start(bf16[4,128,1152]{2,1,0:T(8,128)(2,1)} %get-tuple-element.361), channel_id=1, source_target_pairs={{0,1},{1,0},{2,3},{3,2},{4,5},{5,4},{6,7},{7,6},{8,9},{9,8},{10,11... | collective-permute-start | bytes 3538952 | tf_op jit(solution)/shard_map/ppermute | solution.py:556
  198.4 9.8 %collective-permute-start.59 = (bf16[304,512]{1,0:T(8,128)(2,1)S(1)}, bf16[304,512]{1,0:T(8,128)(2,1)S(1)}, u32[]{:S(2)}, u32[]{:S(2)}) collective-permute-start(bf16[304,512]{1,0:T(8,128)(2,1)S(1)} %get-tuple-element.354), channel_id=1, source_target_pairs={{0,8},{8,0},{16,24},{24,16},{1,9},{9,1},{17,25},{25,17},{2,10},{10... | collective-permute-start | bytes 933896 | tf_op jit(solution)/shard_map/ppermute | solution.py:560
  198.8 18.2 %collective-permute-start.48 = (bf16[128,1152]{1,0:T(8,128)(2,1)}, bf16[128,1152]{1,0:T(8,128)(2,1)}, u32[]{:S(2)}, u32[]{:S(2)}) collective-permute-start(bf16[128,1152]{1,0:T(8,128)(2,1)} %get-tuple-element.424), channel_id=1, source_target_pairs={{0,6},{1,7},{2,4},{3,5},{4,2},{5,3},{6,0},{7,1},{8,14},{9,15},{10,... | collective-permute-start | bytes 884744 | tf_op jit(solution)/shard_map/ppermute | solution.py:556
  199.6 16.0 %collective-permute-start.47 = (bf16[128,1152]{1,0:T(8,128)(2,1)}, bf16[128,1152]{1,0:T(8,128)(2,1)}, u32[]{:S(2)}, u32[]{:S(2)}) collective-permute-start(bf16[128,1152]{1,0:T(8,128)(2,1)} %get-tuple-element.425), channel_id=1, source_target_pairs={{0,4},{1,5},{2,6},{3,7},{4,0},{5,1},{6,2},{7,3},{8,12},{9,13},{10,... | collective-permute-start | bytes 884744 | tf_op jit(solution)/shard_map/ppermute | solution.py:556
  200.6 16.4 %collective-permute-start.46 = (bf16[128,1152]{1,0:T(8,128)(2,1)}, bf16[128,1152]{1,0:T(8,128)(2,1)}, u32[]{:S(2)}, u32[]{:S(2)}) collective-permute-start(bf16[128,1152]{1,0:T(8,128)(2,1)} %get-tuple-element.426), channel_id=1, source_target_pairs={{0,2},{1,3},{2,0},{3,1},{4,6},{5,7},{6,4},{7,5},{8,10},{9,11},{10,... | collective-permute-start | bytes 884744 | tf_op jit(solution)/shard_map/ppermute | solution.py:556
  202.3 19.1 %all-to-all-start.1 = ((bf16[8,36,768]{2,1,0:T(8,128)(2,1)}), bf16[8,36,768]{2,1,0:T(8,128)(2,1)S(1)}, u32[]{:S(2)}, u32[]{:S(2)}) async-start(bf16[8,36,768]{2,1,0:T(8,128)(2,1)} %get-tuple-element.372), calls=%async_computation.1 | async-start | bytes 983040 | tf_op jit(solution)/shard_map/all_to_all | solution.py:1239
  208.2 16.6 %collective-permute-start.64 = (bf16[304,512]{1,0:T(8,128)(2,1)S(1)}, bf16[304,512]{1,0:T(8,128)(2,1)S(1)}, u32[]{:S(2)}, u32[]{:S(2)}) collective-permute-start(bf16[304,512]{1,0:T(8,128)(2,1)S(1)} %add_convert_fusion.1), channel_id=1, source_target_pairs={{0,16},{8,24},{16,0},{24,8},{1,17},{9,25},{17,1},{25,9},{2,18},{10... | collective-permute-start | bytes 933896 | tf_op jit(solution)/shard_map/ppermute | solution.py:560
  208.3 14.2 %collective-permute-start.63 = (bf16[304,512]{1,0:T(8,128)(2,1)S(1)}, bf16[304,512]{1,0:T(8,128)(2,1)S(1)}, u32[]{:S(2)}, u32[]{:S(2)}) collective-permute-start(bf16[304,512]{1,0:T(8,128)(2,1)S(1)} %get-tuple-element.371), channel_id=1, source_target_pairs={{0,8},{8,0},{16,24},{24,16},{1,9},{9,1},{17,25},{25,17},{2,10},{10... | collective-permute-start | bytes 933896 | tf_op jit(solution)/shard_map/ppermute | solution.py:560
  215.5 17.4 %collective-permute-start.62 = (bf16[128,1152]{1,0:T(8,128)(2,1)}, bf16[128,1152]{1,0:T(8,128)(2,1)S(1)}, u32[]{:S(2)}, u32[]{:S(2)}) collective-permute-start(bf16[128,1152]{1,0:T(8,128)(2,1)} %get-tuple-element.423), channel_id=1, source_target_pairs={{0,6},{1,7},{2,4},{3,5},{4,2},{5,3},{6,0},{7,1},{8,14},{9,15},{10,... | collective-permute-start | bytes 884744 | tf_op jit(solution)/shard_map/ppermute | solution.py:556
  217.0 15.9 %collective-permute-start.61 = (bf16[128,1152]{1,0:T(8,128)(2,1)}, bf16[128,1152]{1,0:T(8,128)(2,1)S(1)}, u32[]{:S(2)}, u32[]{:S(2)}) collective-permute-start(bf16[128,1152]{1,0:T(8,128)(2,1)} %get-tuple-element.420), channel_id=1, source_target_pairs={{0,4},{1,5},{2,6},{3,7},{4,0},{5,1},{6,2},{7,3},{8,12},{9,13},{10,... | collective-permute-start | bytes 884744 | tf_op jit(solution)/shard_map/ppermute | solution.py:556
  218.0 14.9 %collective-permute-start.60 = (bf16[128,1152]{1,0:T(8,128)(2,1)}, bf16[128,1152]{1,0:T(8,128)(2,1)S(1)}, u32[]{:S(2)}, u32[]{:S(2)}) collective-permute-start(bf16[128,1152]{1,0:T(8,128)(2,1)} %get-tuple-element.421), channel_id=1, source_target_pairs={{0,2},{1,3},{2,0},{3,1},{4,6},{5,7},{6,4},{7,5},{8,10},{9,11},{10,... | collective-permute-start | bytes 884744 | tf_op jit(solution)/shard_map/ppermute | solution.py:556
  227.6 11.0 %all-to-all-start.2 = ((bf16[8,40,512]{2,1,0:T(8,128)(2,1)}), bf16[8,40,512]{2,1,0:T(8,128)(2,1)S(1)}, u32[]{:S(2)}, u32[]{:S(2)}) async-start(bf16[8,40,512]{2,1,0:T(8,128)(2,1)} %split_back.1), calls=%async_computation.2 | async-start | bytes 655360 | tf_op jit(solution)/shard_map/all_to_all | solution.py:1251
  (99 other events, 713.9 us)

commit v2 on v1

--- a/solution.py
+++ b/solution.py
@@ -1140,7 +1140,7 @@
     s_three = pz(s_two, 1)
     o_three = order.wait(o_three)
     o_sent = order.then(jnp.stack([o_own, o_one, o_two, o_three]))
-    g_one, g_two = pz(order(feed), 1), pz(order(feed), 2)
+    d_one, d_two = pz(order(d_own), 1), pz(order(d_own), 2)
     s_three = order.wait(s_three)
     os = first_ctx(order(o_sent))
     xs = order.wait(both_cores(order.wait(xs)))
@@ -1167,26 +1167,27 @@
             name="attend",
         )
     )
-    att, g_one, g_two = order.wait((att, g_one, g_two))
+    att, d_one, d_two = order.wait((att, d_one, d_two))
     heads = first_ctx(att)
-    os = order.wait(both_cores(order.wait(os)))
+    os = order.wait(os)
+    g_one, g_two = pz(order(feed), 1), pz(order(feed), 2)
+    os = order.wait(both_cores(os))
     w_out = order.then(
         call(
             output_weight_body, [sds((W, W), BF16)], sc, *late(os),
             scratch=[pltpu.VMEM((8, 4, wo.size // 128, 128), F32)], name="output_weight",
         )
     )[0]
-    g_three = pz(order(g_two), 1)
-    d_one, d_two = pz(order(d_own), 1), pz(order(d_own), 2)
+    d_three = order.wait(pz(d_two, 1))
     acted_t = order.then(transpose(order(acted)))
-    d_one, d_two = order.wait((d_one, d_two))
-    d_three = pz(d_two, 1)
     heads[1], heads[2] = order.wait((heads[1], heads[2]))
     heads = order.wait(both_cores(order.wait(heads)))
+    g_two = order.wait(g_two)
+    g_three = pz(g_two, 1)
     cs = [c_late, *c_near, pc(order(c_late), 6)]
     g_three, d_three = order.wait((g_three, d_three))
 
-    att_full, mixed, res_own = order.then(run_project(sc, call_x, late(heads), w_out, gains))
+    att_full, mixed, res_own = order.then(run_project(sc, *late([call_x]), late(heads), w_out, gains))
     wo_own = order.then(lax.dynamic_slice(order(w_out), (jnp.minimum(i, KEY_HEADS - 1) * HG, 0), (HG, W)))
     call_c = order.then(join(late(order(both_cores(order.wait(cs))))))
     feeds = order((feed, g_one, g_two, g_three, d_own, d_one, d_two, d_three))
@@ -1201,15 +1202,15 @@
     )
     feed_far = pz(feed_blocks[3], 1)
     att_t = order.then(transpose(order(att_full)))
+    feed_mid = order.then(add_low(feed_blocks[2], order(feed_far)))
+    feed_terms = (feed_blocks[0], pz(after(feed_blocks[1], feed_mid), 1), pz(feed_mid, 2))
     dres, low = order.then(
         call(
             mid_body, [hbm((ROWS, W), F32), hbm((ROWS, W), BF16)],
-            *late([*order(terms), c_own, res_own]), gains, name="mid",
+            *order(terms), *late([c_own, res_own]), gains, name="mid",
         )
     )
     lows = first_ctx(low)
-    feed_mid = order.then(add_low(feed_blocks[2], order(feed_far)))
-    feed_terms = (feed_blocks[0], pz(after(feed_blocks[1], feed_mid), 1), pz(feed_mid, 2))
 
     om_p, oe_p = order.then(onward(order(hidden), down, "outward"))
     out_got = pc(oe_p, 1)
@@ -1233,7 +1234,7 @@
     hid_sum, grad_down = order.then(
         call(
             split_feed_body, [sds((8, CHUNK, 2 * HID), BF16), sds((864, 128), F32)],
-            *late(order(feed_terms)), name="split_feed",
+            *order(feed_terms), name="split_feed",
         )
     )
     hid_sum = lax.all_to_all(hid_sum, "ctx", 0, 0, tiled=True)
@@ -1247,7 +1248,7 @@
     grad_gate, grad_up = order.then(
         call(unpack_hidden_body, [sds((864, 128), F32), sds((864, 128), F32)], order(hid_sum), name="unpack_hidden")
     )
-    slab = order.then(call(split_back_body, [sds((8, 40, BACK), BF16)], *late(order(slab_terms)), name="split_back"))[0]
+    slab = order.then(call(split_back_body, [sds((8, 40, BACK), BF16)], *order(slab_terms), name="split_back"))[0]
     slab = lax.all_to_all(slab, "ctx", 0, 0, tiled=True)
     input_grad = order.then(
         call(last_body, [sds((ROWS, W), BF16)], *late([*order(in_terms), x_own, dres]), gains, name="last")

time: 241 us -> 234 us (0.971)
  local copies, waits for them, and re-layouts: 14.9 us -> 8.94 us
  waiting for transfers between devices: 69.8 us -> 74.2 us
  starting transfers between devices: 76.3 us -> 73.1 us
    ppermute x18, waiting for transfers between devices: 29.3 us -> 39.8 us  [pz(): return lax.ppermute(value, 'grp', [(s, s ^ k) for s in range(4)])]
    unnamed x158 -> x144, local copies, waits for them, and re-layouts: 11.9 us -> 6.69 us
    ppermute x47, waiting for transfers between devices: 34.4 us -> 29.8 us  [pc(): return lax.ppermute(value, 'ctx', [(s, s ^ k) for s in range(8)])]
    ppermute x18, starting transfers between devices: 26.6 us -> 22.5 us  [pz(): return lax.ppermute(value, 'grp', [(s, s ^ k) for s in range(4)])]
  transfers between devices with their start and end apart: 68 -> 68, of which waited for: 32 -> 35; matrix products, arithmetic and copies ran while one was open for 5% -> 5% of each run, Pallas kernels for 18% -> 18%
where the time goes in v2:
time: 234 us; the launch traced here: 233 us
  waiting for transfers between devices  74.2 us (32%)
  starting transfers between devices  73.1 us (31%)
  Pallas kernels  63.9 us (27%)
  local copies, waits for them, and re-layouts  8.94 us (4%)
  other arithmetic  7.82 us (3%)
  matrix products  3.3 us (1%)
    pallas_call x19, Pallas kernels, call(): pl.pallas_call(body, out_shape=outs, scratch_shapes=scratch, compiler_par...  63.9 us
    ppermute x18, waiting for transfers between devices, pz(): return lax.ppermute(value, 'grp', [(s, s ^ k) for s in range(4)])  39.8 us
    ppermute x47, starting transfers between devices, pc(): return lax.ppermute(value, 'ctx', [(s, s ^ k) for s in range(8)])  37.8 us
    ppermute x47, waiting for transfers between devices, pc(): return lax.ppermute(value, 'ctx', [(s, s ^ k) for s in range(8)])  29.8 us
    ppermute x18, starting transfers between devices, pz(): return lax.ppermute(value, 'grp', [(s, s ^ k) for s in range(4)])  22.5 us
    unnamed x144, local copies, waits for them, and re-layouts  6.69 us
    all_to_all x1, starting transfers between devices, fast_local(): packed = lax.all_to_all(packed, 'ctx', 0, 0, tiled=True)  5.42 us
  transfers between devices with their start and end apart: 68, of which 35 were waited for; matrix products, arithmetic and copies ran while one was open for 5% of the time, Pallas kernels for 18%

profile of v2, /device:TPU:0, one launch (start us, length us, event | category | flops | bytes accessed | tf_op | source)
XLA Modules:
  0.0 232.8 jit_solution(14548490546852441503)
XLA Ops:
  1.5 2.4 %pack.1 = bf16[8,40,1152]{2,1,0:T(8,128)(2,1)} custom-call(bf16[324,128]{1,0:T(8,128)(2,1)} %bitcast.66, bf16[108,128]{1,0:T(8,128)(2,1)} %bitcast.73, bf16[108,128]{1,0:T(8,128)(2,1)} %bitcast.74, bf16[864,128]{1,0:T(8,128)(2,1)} %bitcast.64, bf16[864,128]{1,0:T(8,128)(2,1)} %bitcast.65, bf16[1,1152]{1,0:T(2,128)(2,1)S(1)} %dynamic_update_slice.3.gain), custom_call_target="tpu_custom_call" | custom-call | bytes 1 | tf_op jit(solution)/shard_map/pack/pallas_call | solution.py:632
  3.9 5.4 %all-to-all-start = ((bf16[8,40,1152]{2,1,0:T(8,128)(2,1)}), bf16[8,40,1152]{2,1,0:T(8,128)(2,1)S(1)}, u32[]{:S(2)}, u32[]{:S(2)}) async-start(bf16[8,40,1152]{2,1,0:T(8,128)(2,1)} %pack.1), calls=%async_computation | async-start | bytes 1474560 | tf_op jit(solution)/shard_map/all_to_all | solution.py:1106
  9.4 2.7 %collective-permute-start.1 = (bf16[324,128]{1,0:T(8,128)(2,1)S(1)}, bf16[324,128]{1,0:T(8,128)(2,1)S(1)}, u32[]{:S(2)}, u32[]{:S(2)}) collective-permute-start(bf16[324,128]{1,0:T(8,128)(2,1)S(1)} %bitcast.67), channel_id=1, source_target_pairs={{0,16},{8,24},{16,0},{24,8},{1,17},{9,25},{17,1},{25,9},{2,18},{10... | collective-permute-start | bytes 248840 | tf_op jit(solution)/shard_map/ppermute | solution.py:560
  12.0 1.6 collective-permute-start
  13.6 2.0 collective-permute-start.8
  17.6 4.4 %all-to-all-done.src = bf16[8,40,1152]{2,1,0:T(8,128)(2,1)S(1)} async-done(((bf16[8,40,1152]{2,1,0:T(8,128)(2,1)}), bf16[8,40,1152]{2,1,0:T(8,128)(2,1)S(1)}, u32[]{:S(2)}, u32[]{:S(2)}) %all-to-all-start) | async-done | bytes 737312 | tf_op jit(solution)/shard_map/all_to_all | solution.py:1106
  24.4 2.6 %collective-permute-start.5 = (bf16[8,40,384]{2,1,0:T(8,128)(2,1)S(1)}, bf16[8,40,384]{2,1,0:T(8,128)(2,1)S(1)}, u32[]{:S(2)}, u32[]{:S(2)}) collective-permute-start(bf16[8,40,384]{2,1,0:T(8,128)(2,1)S(1)} %get-tuple-element.239.w0), channel_id=1, source_target_pairs={{0,16},{8,24},{16,0},{24,8},{1,17},{9,25},{17,1},{25,9},{2,18},{10... | collective-permute-start | bytes 737288 | tf_op jit(solution)/shard_map/ppermute | solution.py:560
  28.6 2.0 collective-permute-start.2
  30.7 1.8 collective-permute-done.6.w1
  33.8 2.4 %collective-permute-start.9 = (bf16[8,40,384]{2,1,0:T(8,128)(2,1)S(1)}, bf16[8,40,384]{2,1,0:T(8,128)(2,1)S(1)}, u32[]{:S(2)}, u32[]{:S(2)}) collective-permute-start(bf16[8,40,384]{2,1,0:T(8,128)(2,1)S(1)} %collective-permute-done.5.w2), channel_id=1, source_target_pairs={{0,8},{8,0},{16,24},{24,16},{1,9},{9,1},{17,25},{25,17},{2,10},{10... | collective-permute-start | bytes 737288 | tf_op jit(solution)/shard_map/ppermute | solution.py:560
  36.2 5.0 %collective-permute-done.10 = bf16[324,128]{1,0:T(8,128)(2,1)S(1)} collective-permute-done((bf16[324,128]{1,0:T(8,128)(2,1)S(1)}, bf16[324,128]{1,0:T(8,128)(2,1)S(1)}, u32[]{:S(2)}, u32[]{:S(2)}) %collective-permute-start.10) | collective-permute-done | bytes 82976 | tf_op jit(solution)/shard_map/ppermute | solution.py:560
  43.0 2.6 %collective-permute-start.16 = (bf16[96,1152]{1,0:T(8,128)(2,1)S(1)}, bf16[96,1152]{1,0:T(8,128)(2,1)}, u32[]{:S(2)}, u32[]{:S(2)}) collective-permute-start(bf16[96,1152]{1,0:T(8,128)(2,1)S(1)} %reshape.202.d0), channel_id=1, source_target_pairs={{0,16},{8,24},{16,0},{24,8},{1,17},{9,25},{17,1},{25,9},{2,18},{10... | collective-permute-start | bytes 663560 | tf_op jit(solution)/shard_map/ppermute | solution.py:560
  45.6 1.6 collective-permute-start.15
  47.2 2.4 %collective-permute-start.22 = (bf16[4,324,128]{2,1,0:T(8,128)(2,1)S(1)}, bf16[4,324,128]{2,1,0:T(8,128)(2,1)S(1)}, u32[]{:S(2)}, u32[]{:S(2)}) collective-permute-start(bf16[4,324,128]{2,1,0:T(8,128)(2,1)S(1)} %pad_maximum_fusion.b0), channel_id=1, source_target_pairs={{0,6},{1,7},{2,4},{3,5},{4,2},{5,3},{6,0},{7,1},{8,14},{9,15},{10,... | collective-permute-start | bytes 995336 | tf_op jit(solution)/shard_map/ppermute | solution.py:556
  49.7 3.3 %collective-permute-start.21 = (bf16[4,324,128]{2,1,0:T(8,128)(2,1)S(1)}, bf16[4,324,128]{2,1,0:T(8,128)(2,1)S(1)}, u32[]{:S(2)}, u32[]{:S(2)}) collective-permute-start(bf16[4,324,128]{2,1,0:T(8,128)(2,1)S(1)} %pad_maximum_fusion.b0), channel_id=1, source_target_pairs={{0,4},{1,5},{2,6},{3,7},{4,0},{5,1},{6,2},{7,3},{8,12},{9,13},{10,... | collective-permute-start | bytes 995336 | tf_op jit(solution)/shard_map/ppermute | solution.py:556
  54.9 11.1 %attend.1 = (bf16[512,384]{1,0:T(8,128)(2,1)S(1)}, f32[8,1152]{1,0:T(8,128)S(1)}, bf16[1152,384]{1,0:T(8,128)(2,1)S(1)}, bf16[2,512,256]{2,1,0:T(8,128)(2,1)}, b...) custom-call(s32[2]{0:T(128)S(1)} %pad_add_fusion.sc, ...), custom_call_target="tpu_custom_call" | custom-call | bytes 1 | tf_op jit(solution)/shard_map/attend/pallas_call | solution.py:632
  68.4 1.7 collective-permute-start.17
  73.1 2.6 %output_weight.1.wo = bf16[1152,1152]{1,0:T(8,128)(2,1)S(1)} custom-call(s32[2]{0:T(128)S(1)} %pad_add_fusion.sc, bf16[4,324,128]{2,1,0:T(8,128)(2,1)} %copy-done.18, bf16[4,324,128]{2,1,0:T(8,128)(2,1)} %copy-done.34, bf16[4,324,128]{2,1,0:T(8,128)(2,1)} %copy-done.33, bf16[4,324,128]{2,1,0:T(8,128)(2,1)} %copy-done.32, bf16[4,324,128]{2,1,0:T(8,128)(2,1)} %copy-done.35, ...), custom_call_target="tpu_custom_call" | custom-call | bytes 1 | tf_op jit(solution)/shard_map/output_weight/pallas_call | solution.py:632
  75.7 5.8 %collective-permute-done.19.d3 = bf16[96,1152]{1,0:T(8,128)(2,1)S(1)} collective-permute-done((bf16[96,1152]{1,0:T(8,128)(2,1)}, bf16[96,1152]{1,0:T(8,128)(2,1)S(1)}, u32[]{:S(2)}, u32[]{:S(2)}) %collective-permute-start.19) | collective-permute-done | bytes 221216 | tf_op jit(solution)/shard_map/ppermute | solution.py:560
  84.3 3.8 %collective-permute-done.27.a3 = bf16[512,384]{1,0:T(8,128)(2,1)S(1)} collective-permute-done((bf16[512,384]{1,0:T(8,128)(2,1)S(1)}, bf16[512,384]{1,0:T(8,128)(2,1)S(1)}, u32[]{:S(2)}, u32[]{:S(2)}) %collective-permute-start.27) | collective-permute-done | bytes 393248 | tf_op jit(solution)/shard_map/ppermute | solution.py:556
  91.5 3.7 %collective-permute-done.32.g2 = bf16[288,768]{1,0:T(8,128)(2,1)} collective-permute-done((bf16[288,768]{1,0:T(8,128)(2,1)}, bf16[288,768]{1,0:T(8,128)(2,1)}, u32[]{:S(2)}, u32[]{:S(2)}) %collective-permute-start.32) | collective-permute-done | bytes 442400 | tf_op jit(solution)/shard_map/ppermute | solution.py:560
  95.3 2.5 %collective-permute-start.33 = (bf16[128,1152]{1,0:T(8,128)(2,1)}, bf16[128,1152]{1,0:T(8,128)(2,1)}, u32[]{:S(2)}, u32[]{:S(2)}) collective-permute-start(bf16[128,1152]{1,0:T(8,128)(2,1)} %bitcast.3.refs_0_.c), channel_id=1, source_target_pairs={{0,6},{1,7},{2,4},{3,5},{4,2},{5,3},{6,0},{7,1},{8,14},{9,15},{10,... | collective-permute-start | bytes 884744 | tf_op jit(solution)/shard_map/ppermute | solution.py:556
  97.8 2.0 collective-permute-start.38
  100.5 9.1 %project.1 = (bf16[1024,1152]{1,0:T(8,128)(2,1)}, bf16[1024,1152]{1,0:T(8,128)(2,1)S(1)}, f32[128,1152]{1,0:T(8,128)}) custom-call(s32[2]{0:T(128)S(1)} %pad_add_fusion.sc, bf16[1024,1152]{1,0:T(8,128)(2,1)} %get-tuple-element.243.x, bf16[512,384]{1,0:T(8,128)(2,1)} %copy-done.14, bf16[512,384]{1,0:T(8,128)(2,1)} %copy-done.26, bf16[512,384]{1,0:T(8,128)(2,1)} %copy-done.25, ...), custom_call_target="tpu_custom_call" | custom-call | bytes 1 | tf_op jit(solution)/shard_map/project/pallas_call | solution.py:632
  114.0 1.8 join.1.c
  117.0 8.6 %feed.1 = (bf16[1024,384]{1,0:T(8,128)(2,1)S(1)}, bf16[1024,768]{1,0:T(8,128)(2,1)S(1)}, bf16[4,128,1152]{2,1,0:T(8,128)(2,1)S(1)}, bf16[4,128,1152]{2,1,0:T(8,1...) custom-call(s32[2]{0:T(128)S(1)} %pad_add_fusion.sc, ...), custom_call_target="tpu_custom_call" | custom-call | bytes 1 | tf_op jit(solution)/shard_map/feed/pallas_call | solution.py:632
  125.8 2.1 convolution_convert_fusion.grad_gu
  130.1 2.2 grads.1
  133.9 1.7 collective-permute-start.41
  136.8 12.7 %collective-permute-done.44 = bf16[432,768]{1,0:T(8,128)(2,1)S(1)} collective-permute-done((bf16[432,768]{1,0:T(8,128)(2,1)}, bf16[432,768]{1,0:T(8,128)(2,1)S(1)}, u32[]{:S(2)}, u32[]{:S(2)}) %collective-permute-start.44) | collective-permute-done | bytes 663584 | tf_op jit(solution)/shard_map/ppermute | solution.py:560
  149.7 2.6 %mid.1 = (f32[128,1152]{1,0:T(8,128)}, bf16[128,1152]{1,0:T(8,128)(2,1)}) custom-call(bf16[128,1152]{1,0:T(8,128)(2,1)S(1)} %get-tuple-element.322.a, bf16[128,1152]{1,0:T(8,128)(2,1)S(1)} %collective-permute-done.41.b, bf16[128,1152]{1,0:T(8,128)(2,1)S(1)} %collective-permute-done.42.d, bf16[128,1152]{1,0:T(8,128)(2,1)S(1)} %collective-permute-done.43.f, ...), custom_call_target="tpu_custom_call" | custom-call | bytes 1 | tf_op jit(solution)/shard_map/mid/pallas_call | solution.py:632
  153.9 2.5 %collective-permute-start.51 = (bf16[128,1152]{1,0:T(8,128)(2,1)S(1)}, bf16[128,1152]{1,0:T(8,128)(2,1)S(1)}, u32[]{:S(2)}, u32[]{:S(2)}) collective-permute-start(bf16[128,1152]{1,0:T(8,128)(2,1)S(1)} %copy-done.48), channel_id=1, source_target_pairs={{0,6},{1,7},{2,4},{3,5},{4,2},{5,3},{6,0},{7,1},{8,14},{9,15},{10,... | collective-permute-start | bytes 884744 | tf_op jit(solution)/shard_map/ppermute | solution.py:556
  160.3 4.4 %collective-permute-done.51.l3 = bf16[128,1152]{1,0:T(8,128)(2,1)S(1)} collective-permute-done((bf16[128,1152]{1,0:T(8,128)(2,1)S(1)}, bf16[128,1152]{1,0:T(8,128)(2,1)S(1)}, u32[]{:S(2)}, u32[]{:S(2)}) %collective-permute-start.51) | collective-permute-done | bytes 294944 | tf_op jit(solution)/shard_map/ppermute | solution.py:556
  164.7 5.8 %collective-permute-done.50.l2 = bf16[128,1152]{1,0:T(8,128)(2,1)S(1)} collective-permute-done((bf16[128,1152]{1,0:T(8,128)(2,1)S(1)}, bf16[128,1152]{1,0:T(8,128)(2,1)S(1)}, u32[]{:S(2)}, u32[]{:S(2)}) %collective-permute-start.50) | collective-permute-done | bytes 294944 | tf_op jit(solution)/shard_map/ppermute | solution.py:556
  174.5 10.8 %back.1 = (bf16[1024,384]{1,0:T(8,128)(2,1)S(1)}, bf16[304,512]{1,0:T(8,128)(2,1)S(1)}, bf16[304,512]{1,0:T(8,128)(2,1)S(1)}, bf16[304,512]{1,0:T(8,128)(2,1)S(1)}, bf16[304,512]{1,0:T(8,128)(2,1)S(1)}) custom-call(s32[2]{0:T(128)S(1)} %pad_add_fusion.sc, bf16[128,1152]{1,0:T(8,128)(2,1)} %get-tuple-element.336.l0, bf16[128,1152]{1,0:T(8,128)(2,1)} %copy-done.51, ...), custom_call_target="tpu_custom_call" | custom-call | bytes 1 | tf_op jit(solution)/shard_map/back/pallas_call | solution.py:632
  186.3 2.6 %collective-permute-done.57.d = bf16[432,768]{1,0:T(8,128)(2,1)S(1)} collective-permute-done((bf16[432,768]{1,0:T(8,128)(2,1)S(1)}, bf16[432,768]{1,0:T(8,128)(2,1)S(1)}, u32[]{:S(2)}, u32[]{:S(2)}) %collective-permute-start.57) | collective-permute-done | bytes 663584 | tf_op jit(solution)/shard_map/ppermute | solution.py:560
  190.1 2.6 %inward.1 = (bf16[4,128,1152]{2,1,0:T(8,128)(2,1)S(1)}, bf16[4,128,1152]{2,1,0:T(8,128)(2,1)}) custom-call(bf16[1024,384]{1,0:T(8,128)(2,1)S(1)} %get-tuple-element.357.rows, bf16[1152,384]{1,0:T(8,128)(2,1)S(1)} %get-tuple-element.347.w_slab.weight), custom_call_target="tpu_custom_call" | custom-call | bytes 1 | tf_op jit(solution)/shard_map/inward/pallas_call | solution.py:632
  192.7 2.4 %collective-permute-start.48 = (bf16[128,1152]{1,0:T(8,128)(2,1)}, bf16[128,1152]{1,0:T(8,128)(2,1)}, u32[]{:S(2)}, u32[]{:S(2)}) collective-permute-start(bf16[128,1152]{1,0:T(8,128)(2,1)} %get-tuple-element.422), channel_id=1, source_target_pairs={{0,6},{1,7},{2,4},{3,5},{4,2},{5,3},{6,0},{7,1},{8,14},{9,15},{10,... | collective-permute-start | bytes 884744 | tf_op jit(solution)/shard_map/ppermute | solution.py:556
  196.2 3.7 %all-to-all-start.1 = ((bf16[8,36,768]{2,1,0:T(8,128)(2,1)}), bf16[8,36,768]{2,1,0:T(8,128)(2,1)S(1)}, u32[]{:S(2)}, u32[]{:S(2)}) async-start(bf16[8,36,768]{2,1,0:T(8,128)(2,1)} %get-tuple-element.370), calls=%async_computation.1 | async-start | bytes 983040 | tf_op jit(solution)/shard_map/all_to_all | solution.py:1240
  199.9 2.6 %collective-permute-done.59 = bf16[304,512]{1,0:T(8,128)(2,1)S(1)} collective-permute-done((bf16[304,512]{1,0:T(8,128)(2,1)S(1)}, bf16[304,512]{1,0:T(8,128)(2,1)S(1)}, u32[]{:S(2)}, u32[]{:S(2)}) %collective-permute-start.59) | collective-permute-done | bytes 311328 | tf_op jit(solution)/shard_map/ppermute | solution.py:560
  204.8 2.5 %fusion.11 = (bf16[128,1152]{1,0:T(8,128)(2,1)}, bf16[128,1152]{1,0:T(8,128)(2,1)}, bf16[128,1152]{1,0:T(8,128)(2,1)}, bf16[128,1152]{1,0:T(8,128)(2,1)}) fusion(bf16[4,128,1152]{2,1,0:T(8,128)(2,1)} %collective-permute-done.58, bf16[4,128,1152]{2,1,0:T(8,128)(2,1)S(1)} %get-tuple-element.358), kind=kLoop, calls=%fused_computation.32 | loop fusion | flops 2359296 | bytes 3538944 | tf_op jit(solution)/shard_map/convert_element_type | solution.py:587
  207.4 2.4 %collective-permute-done.47 = bf16[128,1152]{1,0:T(8,128)(2,1)} collective-permute-done((bf16[128,1152]{1,0:T(8,128)(2,1)}, bf16[128,1152]{1,0:T(8,128)(2,1)}, u32[]{:S(2)}, u32[]{:S(2)}) %collective-permute-start.47) | collective-permute-done | bytes 294944 | tf_op jit(solution)/shard_map/ppermute | solution.py:556
  209.7 2.7 %collective-permute-start.62 = (bf16[128,1152]{1,0:T(8,128)(2,1)}, bf16[128,1152]{1,0:T(8,128)(2,1)S(1)}, u32[]{:S(2)}, u32[]{:S(2)}) collective-permute-start(bf16[128,1152]{1,0:T(8,128)(2,1)} %get-tuple-element.421), channel_id=1, source_target_pairs={{0,6},{1,7},{2,4},{3,5},{4,2},{5,3},{6,0},{7,1},{8,14},{9,15},{10,... | collective-permute-start | bytes 884744 | tf_op jit(solution)/shard_map/ppermute | solution.py:556
  213.3 2.1 add_convert_fusion.5
  216.9 2.3 collective-permute-done.64.d
  220.1 3.7 %all-to-all-start.2 = ((bf16[8,40,512]{2,1,0:T(8,128)(2,1)}), bf16[8,40,512]{2,1,0:T(8,128)(2,1)S(1)}, u32[]{:S(2)}, u32[]{:S(2)}) async-start(bf16[8,40,512]{2,1,0:T(8,128)(2,1)} %split_back.1), calls=%async_computation.2 | async-start | bytes 655360 | tf_op jit(solution)/shard_map/all_to_all | solution.py:1252
  223.8 3.9 %collective-permute-done.61.d = bf16[128,1152]{1,0:T(8,128)(2,1)S(1)} collective-permute-done((bf16[128,1152]{1,0:T(8,128)(2,1)}, bf16[128,1152]{1,0:T(8,128)(2,1)S(1)}, u32[]{:S(2)}, u32[]{:S(2)}) %collective-permute-start.61) | collective-permute-done | bytes 294944 | tf_op jit(solution)/shard_map/ppermute | solution.py:556
  228.6 2.6 %last.1 = bf16[128,1152]{1,0:T(8,128)(2,1)} custom-call(bf16[128,1152]{1,0:T(8,128)(2,1)} %get-tuple-element.376.a, bf16[128,1152]{1,0:T(8,128)(2,1)} %copy-done.54, bf16[128,1152]{1,0:T(8,128)(2,1)} %copy-done.53, bf16[128,1152]{1,0:T(8,128)(2,1)} %copy-done.52, bf16[128,1152]{1,0:T(8,128)(2,1)} %bitcast.59, f32[128,1152]{1,0:T(8,128)} %get-tuple-element.380.dres, ...), custom_call_target="tpu_custom_call" | custom-call | bytes 1 | tf_op jit(solution)/shard_map/last/pallas_call | solution.py:632
  (281 shorter events, 55.9 us)
Async XLA Ops:
  3.9 18.0 %all-to-all-start = ((bf16[8,40,1152]{2,1,0:T(8,128)(2,1)}), bf16[8,40,1152]{2,1,0:T(8,128)(2,1)S(1)}, u32[]{:S(2)}, u32[]{:S(2)}) async-start(bf16[8,40,1152]{2,1,0:T(8,128)(2,1)} %pack.1), calls=%async_computation | async-start | bytes 1474560 | tf_op jit(solution)/shard_map/all_to_all | solution.py:1106
  9.4 8.2 %collective-permute-start.1 = (bf16[324,128]{1,0:T(8,128)(2,1)S(1)}, bf16[324,128]{1,0:T(8,128)(2,1)S(1)}, u32[]{:S(2)}, u32[]{:S(2)}) collective-permute-start(bf16[324,128]{1,0:T(8,128)(2,1)S(1)} %bitcast.67), channel_id=1, source_target_pairs={{0,16},{8,24},{16,0},{24,8},{1,17},{9,25},{17,1},{25,9},{2,18},{10... | collective-permute-start | bytes 248840 | tf_op jit(solution)/shard_map/ppermute | solution.py:560
  12.0 5.6 %collective-permute-start = (bf16[324,128]{1,0:T(8,128)(2,1)S(1)}, bf16[324,128]{1,0:T(8,128)(2,1)S(1)}, u32[]{:S(2)}, u32[]{:S(2)}) collective-permute-start(bf16[324,128]{1,0:T(8,128)(2,1)S(1)} %bitcast.68), channel_id=1, source_target_pairs={{0,8},{8,0},{16,24},{24,16},{1,9},{9,1},{17,25},{25,17},{2,10},{10... | collective-permute-start | bytes 248840 | tf_op jit(solution)/shard_map/ppermute | solution.py:560
  13.6 13.9 %collective-permute-start.8 = (bf16[128,1152]{1,0:T(8,128)(2,1)}, bf16[128,1152]{1,0:T(8,128)(2,1)S(1)}, u32[]{:S(2)}, u32[]{:S(2)}) collective-permute-start(bf16[128,1152]{1,0:T(8,128)(2,1)} %bitcast.3.refs_0_.c), channel_id=1, source_target_pairs={{0,4},{1,5},{2,6},{3,7},{4,0},{5,1},{6,2},{7,3},{8,12},{9,13},{10,... | collective-permute-start | bytes 884744 | tf_op jit(solution)/shard_map/ppermute | solution.py:556
  15.6 13.0 %collective-permute-start.7 = (bf16[128,1152]{1,0:T(8,128)(2,1)}, bf16[128,1152]{1,0:T(8,128)(2,1)}, u32[]{:S(2)}, u32[]{:S(2)}) collective-permute-start(bf16[128,1152]{1,0:T(8,128)(2,1)} %bitcast.3.refs_0_.c), channel_id=1, source_target_pairs={{0,2},{1,3},{2,0},{3,1},{4,6},{5,7},{6,4},{7,5},{8,10},{9,11},{10,... | collective-permute-start | bytes 884744 | tf_op jit(solution)/shard_map/ppermute | solution.py:556
  22.8 9.7 %collective-permute-start.6 = (bf16[8,40,384]{2,1,0:T(8,128)(2,1)S(1)}, bf16[8,40,384]{2,1,0:T(8,128)(2,1)S(1)}, u32[]{:S(2)}, u32[]{:S(2)}) collective-permute-start(bf16[8,40,384]{2,1,0:T(8,128)(2,1)S(1)} %get-tuple-element.239.w0), channel_id=1, source_target_pairs={{0,8},{8,0},{16,24},{24,16},{1,9},{9,1},{17,25},{25,17},{2,10},{10... | collective-permute-start | bytes 737288 | tf_op jit(solution)/shard_map/ppermute | solution.py:560
  24.4 9.5 %collective-permute-start.5 = (bf16[8,40,384]{2,1,0:T(8,128)(2,1)S(1)}, bf16[8,40,384]{2,1,0:T(8,128)(2,1)S(1)}, u32[]{:S(2)}, u32[]{:S(2)}) collective-permute-start(bf16[8,40,384]{2,1,0:T(8,128)(2,1)S(1)} %get-tuple-element.239.w0), channel_id=1, source_target_pairs={{0,16},{8,24},{16,0},{24,8},{1,17},{9,25},{17,1},{25,9},{2,18},{10... | collective-permute-start | bytes 737288 | tf_op jit(solution)/shard_map/ppermute | solution.py:560
  27.0 14.4 %collective-permute-start.4 = (bf16[128,1280]{1,0:T(8,128)(2,1)S(1)}, bf16[128,1280]{1,0:T(8,128)(2,1)S(1)}, u32[]{:S(2)}, u32[]{:S(2)}) collective-permute-start(bf16[128,1280]{1,0:T(8,128)(2,1)S(1)} %pad_maximum_fusion.1.x0), channel_id=1, source_target_pairs={{0,6},{1,7},{2,4},{3,5},{4,2},{5,3},{6,0},{7,1},{8,14},{9,15},{10,... | collective-permute-start | bytes 983048 | tf_op jit(solution)/shard_map/ppermute | solution.py:556
  27.5 14.3 %collective-permute-start.3 = (bf16[128,1280]{1,0:T(8,128)(2,1)S(1)}, bf16[128,1280]{1,0:T(8,128)(2,1)S(1)}, u32[]{:S(2)}, u32[]{:S(2)}) collective-permute-start(bf16[128,1280]{1,0:T(8,128)(2,1)S(1)} %pad_maximum_fusion.1.x0), channel_id=1, source_target_pairs={{0,4},{1,5},{2,6},{3,7},{4,0},{5,1},{6,2},{7,3},{8,12},{9,13},{10,... | collective-permute-start | bytes 983048 | tf_op jit(solution)/shard_map/ppermute | solution.py:556
  28.6 13.3 %collective-permute-start.2 = (bf16[128,1280]{1,0:T(8,128)(2,1)S(1)}, bf16[128,1280]{1,0:T(8,128)(2,1)S(1)}, u32[]{:S(2)}, u32[]{:S(2)}) collective-permute-start(bf16[128,1280]{1,0:T(8,128)(2,1)S(1)} %pad_maximum_fusion.1.x0), channel_id=1, source_target_pairs={{0,2},{1,3},{2,0},{3,1},{4,6},{5,7},{6,4},{7,5},{8,10},{9,11},{10,... | collective-permute-start | bytes 983048 | tf_op jit(solution)/shard_map/ppermute | solution.py:556
  33.8 7.5 %collective-permute-start.9 = (bf16[8,40,384]{2,1,0:T(8,128)(2,1)S(1)}, bf16[8,40,384]{2,1,0:T(8,128)(2,1)S(1)}, u32[]{:S(2)}, u32[]{:S(2)}) collective-permute-start(bf16[8,40,384]{2,1,0:T(8,128)(2,1)S(1)} %collective-permute-done.5.w2), channel_id=1, source_target_pairs={{0,8},{8,0},{16,24},{24,16},{1,9},{9,1},{17,25},{25,17},{2,10},{10... | collective-permute-start | bytes 737288 | tf_op jit(solution)/shard_map/ppermute | solution.py:560
  41.9 5.3 %collective-permute-start.12 = (bf16[128,1280]{1,0:T(8,128)(2,1)S(1)}, bf16[128,1280]{1,0:T(8,128)(2,1)S(1)}, u32[]{:S(2)}, u32[]{:S(2)}) collective-permute-start(bf16[128,1280]{1,0:T(8,128)(2,1)S(1)} %collective-permute-done.2.x1), channel_id=1, source_target_pairs={{0,1},{1,0},{2,3},{3,2},{4,5},{5,4},{6,7},{7,6},{8,9},{9,8},{10,11... | collective-permute-start | bytes 983048 | tf_op jit(solution)/shard_map/ppermute | solution.py:556
  42.4 7.2 %collective-permute-start.13 = (bf16[128,1280]{1,0:T(8,128)(2,1)S(1)}, bf16[128,1280]{1,0:T(8,128)(2,1)S(1)}, u32[]{:S(2)}, u32[]{:S(2)}) collective-permute-start(bf16[128,1280]{1,0:T(8,128)(2,1)S(1)} %collective-permute-done.3.x2), channel_id=1, source_target_pairs={{0,1},{1,0},{2,3},{3,2},{4,5},{5,4},{6,7},{7,6},{8,9},{9,8},{10,11... | collective-permute-start | bytes 983048 | tf_op jit(solution)/shard_map/ppermute | solution.py:556
  42.5 10.5 %collective-permute-start.14 = (bf16[128,1280]{1,0:T(8,128)(2,1)S(1)}, bf16[128,1280]{1,0:T(8,128)(2,1)S(1)}, u32[]{:S(2)}, u32[]{:S(2)}) collective-permute-start(bf16[128,1280]{1,0:T(8,128)(2,1)S(1)} %collective-permute-done.4.x3), channel_id=1, source_target_pairs={{0,1},{1,0},{2,3},{3,2},{4,5},{5,4},{6,7},{7,6},{8,9},{9,8},{10,11... | collective-permute-start | bytes 983048 | tf_op jit(solution)/shard_map/ppermute | solution.py:556
  43.0 23.0 %collective-permute-start.16 = (bf16[96,1152]{1,0:T(8,128)(2,1)S(1)}, bf16[96,1152]{1,0:T(8,128)(2,1)}, u32[]{:S(2)}, u32[]{:S(2)}) collective-permute-start(bf16[96,1152]{1,0:T(8,128)(2,1)S(1)} %reshape.202.d0), channel_id=1, source_target_pairs={{0,16},{8,24},{16,0},{24,8},{1,17},{9,25},{17,1},{25,9},{2,18},{10... | collective-permute-start | bytes 663560 | tf_op jit(solution)/shard_map/ppermute | solution.py:560
  45.6 20.4 %collective-permute-start.15 = (bf16[96,1152]{1,0:T(8,128)(2,1)S(1)}, bf16[96,1152]{1,0:T(8,128)(2,1)}, u32[]{:S(2)}, u32[]{:S(2)}) collective-permute-start(bf16[96,1152]{1,0:T(8,128)(2,1)S(1)} %reshape.202.d0), channel_id=1, source_target_pairs={{0,8},{8,0},{16,24},{24,16},{1,9},{9,1},{17,25},{25,17},{2,10},{10... | collective-permute-start | bytes 663560 | tf_op jit(solution)/shard_map/ppermute | solution.py:560
  47.2 18.8 %collective-permute-start.22 = (bf16[4,324,128]{2,1,0:T(8,128)(2,1)S(1)}, bf16[4,324,128]{2,1,0:T(8,128)(2,1)S(1)}, u32[]{:S(2)}, u32[]{:S(2)}) collective-permute-start(bf16[4,324,128]{2,1,0:T(8,128)(2,1)S(1)} %pad_maximum_fusion.b0), channel_id=1, source_target_pairs={{0,6},{1,7},{2,4},{3,5},{4,2},{5,3},{6,0},{7,1},{8,14},{9,15},{10,... | collective-permute-start | bytes 995336 | tf_op jit(solution)/shard_map/ppermute | solution.py:556
  49.7 16.4 %collective-permute-start.21 = (bf16[4,324,128]{2,1,0:T(8,128)(2,1)S(1)}, bf16[4,324,128]{2,1,0:T(8,128)(2,1)S(1)}, u32[]{:S(2)}, u32[]{:S(2)}) collective-permute-start(bf16[4,324,128]{2,1,0:T(8,128)(2,1)S(1)} %pad_maximum_fusion.b0), channel_id=1, source_target_pairs={{0,4},{1,5},{2,6},{3,7},{4,0},{5,1},{6,2},{7,3},{8,12},{9,13},{10,... | collective-permute-start | bytes 995336 | tf_op jit(solution)/shard_map/ppermute | solution.py:556
  53.0 13.2 %collective-permute-start.20 = (bf16[4,324,128]{2,1,0:T(8,128)(2,1)S(1)}, bf16[4,324,128]{2,1,0:T(8,128)(2,1)S(1)}, u32[]{:S(2)}, u32[]{:S(2)}) collective-permute-start(bf16[4,324,128]{2,1,0:T(8,128)(2,1)S(1)} %pad_maximum_fusion.b0), channel_id=1, source_target_pairs={{0,2},{1,3},{2,0},{3,1},{4,6},{5,7},{6,4},{7,5},{8,10},{9,11},{10,... | collective-permute-start | bytes 995336 | tf_op jit(solution)/shard_map/ppermute | solution.py:556
  66.8 17.5 %collective-permute-start.18 = (bf16[512,384]{1,0:T(8,128)(2,1)S(1)}, bf16[512,384]{1,0:T(8,128)(2,1)S(1)}, u32[]{:S(2)}, u32[]{:S(2)}) collective-permute-start(bf16[512,384]{1,0:T(8,128)(2,1)S(1)} %get-tuple-element.270.a0), channel_id=1, source_target_pairs={{0,4},{1,5},{2,6},{3,7},{4,0},{5,1},{6,2},{7,3},{8,12},{9,13},{10,... | collective-permute-start | bytes 1179656 | tf_op jit(solution)/shard_map/ppermute | solution.py:556
  68.4 15.9 %collective-permute-start.17 = (bf16[512,384]{1,0:T(8,128)(2,1)S(1)}, bf16[512,384]{1,0:T(8,128)(2,1)S(1)}, u32[]{:S(2)}, u32[]{:S(2)}) collective-permute-start(bf16[512,384]{1,0:T(8,128)(2,1)S(1)} %get-tuple-element.270.a0), channel_id=1, source_target_pairs={{0,2},{1,3},{2,0},{3,1},{4,6},{5,7},{6,4},{7,5},{8,10},{9,11},{10,... | collective-permute-start | bytes 1179656 | tf_op jit(solution)/shard_map/ppermute | solution.py:556
  70.1 18.0 %collective-permute-start.27 = (bf16[512,384]{1,0:T(8,128)(2,1)S(1)}, bf16[512,384]{1,0:T(8,128)(2,1)S(1)}, u32[]{:S(2)}, u32[]{:S(2)}) collective-permute-start(bf16[512,384]{1,0:T(8,128)(2,1)S(1)} %get-tuple-element.270.a0), channel_id=1, source_target_pairs={{0,6},{1,7},{2,4},{3,5},{4,2},{5,3},{6,0},{7,1},{8,14},{9,15},{10,... | collective-permute-start | bytes 1179656 | tf_op jit(solution)/shard_map/ppermute | solution.py:556
  70.6 10.9 %collective-permute-start.19 = (bf16[96,1152]{1,0:T(8,128)(2,1)}, bf16[96,1152]{1,0:T(8,128)(2,1)S(1)}, u32[]{:S(2)}, u32[]{:S(2)}) collective-permute-start(bf16[96,1152]{1,0:T(8,128)(2,1)} %collective-permute-done.16.d2), channel_id=1, source_target_pairs={{0,8},{8,0},{16,24},{24,16},{1,9},{9,1},{17,25},{25,17},{2,10},{10... | collective-permute-start | bytes 663560 | tf_op jit(solution)/shard_map/ppermute | solution.py:560
  72.2 23.0 %collective-permute-start.32 = (bf16[288,768]{1,0:T(8,128)(2,1)}, bf16[288,768]{1,0:T(8,128)(2,1)}, u32[]{:S(2)}, u32[]{:S(2)}) collective-permute-start(bf16[288,768]{1,0:T(8,128)(2,1)} %get-tuple-element.301.g0), channel_id=1, source_target_pairs={{0,16},{8,24},{16,0},{24,8},{1,17},{9,25},{17,1},{25,9},{2,18},{10... | collective-permute-start | bytes 1327112 | tf_op jit(solution)/shard_map/ppermute | solution.py:560
  95.2 15.1 %collective-permute-start.39 = (bf16[288,768]{1,0:T(8,128)(2,1)}, bf16[288,768]{1,0:T(8,128)(2,1)}, u32[]{:S(2)}, u32[]{:S(2)}) collective-permute-start(bf16[288,768]{1,0:T(8,128)(2,1)} %collective-permute-done.32.g2), channel_id=1, source_target_pairs={{0,8},{8,0},{16,24},{24,16},{1,9},{9,1},{17,25},{25,17},{2,10},{10... | collective-permute-start | bytes 1327112 | tf_op jit(solution)/shard_map/ppermute | solution.py:560
  95.3 14.4 %collective-permute-start.33 = (bf16[128,1152]{1,0:T(8,128)(2,1)}, bf16[128,1152]{1,0:T(8,128)(2,1)}, u32[]{:S(2)}, u32[]{:S(2)}) collective-permute-start(bf16[128,1152]{1,0:T(8,128)(2,1)} %bitcast.3.refs_0_.c), channel_id=1, source_target_pairs={{0,6},{1,7},{2,4},{3,5},{4,2},{5,3},{6,0},{7,1},{8,14},{9,15},{10,... | collective-permute-start | bytes 884744 | tf_op jit(solution)/shard_map/ppermute | solution.py:556
  97.8 18.5 %collective-permute-start.38 = (bf16[288,768]{1,0:T(8,128)(2,1)}, bf16[288,768]{1,0:T(8,128)(2,1)S(1)}, u32[]{:S(2)}, u32[]{:S(2)}) collective-permute-start(bf16[288,768]{1,0:T(8,128)(2,1)} %get-tuple-element.301.g0), channel_id=1, source_target_pairs={{0,8},{8,0},{16,24},{24,16},{1,9},{9,1},{17,25},{25,17},{2,10},{10... | collective-permute-start | bytes 1327112 | tf_op jit(solution)/shard_map/ppermute | solution.py:560
  132.3 17.2 %collective-permute-start.44 = (bf16[432,768]{1,0:T(8,128)(2,1)}, bf16[432,768]{1,0:T(8,128)(2,1)S(1)}, u32[]{:S(2)}, u32[]{:S(2)}) collective-permute-start(bf16[432,768]{1,0:T(8,128)(2,1)} %get-tuple-element.318), channel_id=1, source_target_pairs={{0,8},{8,0},{16,24},{24,16},{1,9},{9,1},{17,25},{25,17},{2,10},{10... | collective-permute-start | bytes 1990664 | tf_op jit(solution)/shard_map/ppermute | solution.py:560
  132.6 17.1 %collective-permute-start.42 = (bf16[128,1152]{1,0:T(8,128)(2,1)S(1)}, bf16[128,1152]{1,0:T(8,128)(2,1)S(1)}, u32[]{:S(2)}, u32[]{:S(2)}) collective-permute-start(bf16[128,1152]{1,0:T(8,128)(2,1)S(1)} %get-tuple-element.427), channel_id=1, source_target_pairs={{0,4},{1,5},{2,6},{3,7},{4,0},{5,1},{6,2},{7,3},{8,12},{9,13},{10,... | collective-permute-start | bytes 884744 | tf_op jit(solution)/shard_map/ppermute | solution.py:556
  133.9 15.8 %collective-permute-start.41 = (bf16[128,1152]{1,0:T(8,128)(2,1)S(1)}, bf16[128,1152]{1,0:T(8,128)(2,1)S(1)}, u32[]{:S(2)}, u32[]{:S(2)}) collective-permute-start(bf16[128,1152]{1,0:T(8,128)(2,1)S(1)} %get-tuple-element.428), channel_id=1, source_target_pairs={{0,2},{1,3},{2,0},{3,1},{4,6},{5,7},{6,4},{7,5},{8,10},{9,11},{10,... | collective-permute-start | bytes 884744 | tf_op jit(solution)/shard_map/ppermute | solution.py:556
  135.6 14.1 %collective-permute-start.43 = (bf16[128,1152]{1,0:T(8,128)(2,1)S(1)}, bf16[128,1152]{1,0:T(8,128)(2,1)S(1)}, u32[]{:S(2)}, u32[]{:S(2)}) collective-permute-start(bf16[128,1152]{1,0:T(8,128)(2,1)S(1)} %get-tuple-element.426), channel_id=1, source_target_pairs={{0,6},{1,7},{2,4},{3,5},{4,2},{5,3},{6,0},{7,1},{8,14},{9,15},{10,... | collective-permute-start | bytes 884744 | tf_op jit(solution)/shard_map/ppermute | solution.py:556
  153.9 10.8 %collective-permute-start.51 = (bf16[128,1152]{1,0:T(8,128)(2,1)S(1)}, bf16[128,1152]{1,0:T(8,128)(2,1)S(1)}, u32[]{:S(2)}, u32[]{:S(2)}) collective-permute-start(bf16[128,1152]{1,0:T(8,128)(2,1)S(1)} %copy-done.48), channel_id=1, source_target_pairs={{0,6},{1,7},{2,4},{3,5},{4,2},{5,3},{6,0},{7,1},{8,14},{9,15},{10,... | collective-permute-start | bytes 884744 | tf_op jit(solution)/shard_map/ppermute | solution.py:556
  156.4 14.1 %collective-permute-start.50 = (bf16[128,1152]{1,0:T(8,128)(2,1)S(1)}, bf16[128,1152]{1,0:T(8,128)(2,1)S(1)}, u32[]{:S(2)}, u32[]{:S(2)}) collective-permute-start(bf16[128,1152]{1,0:T(8,128)(2,1)S(1)} %copy-done.48), channel_id=1, source_target_pairs={{0,4},{1,5},{2,6},{3,7},{4,0},{5,1},{6,2},{7,3},{8,12},{9,13},{10,... | collective-permute-start | bytes 884744 | tf_op jit(solution)/shard_map/ppermute | solution.py:556
  157.1 13.4 %collective-permute-start.49 = (bf16[128,1152]{1,0:T(8,128)(2,1)S(1)}, bf16[128,1152]{1,0:T(8,128)(2,1)S(1)}, u32[]{:S(2)}, u32[]{:S(2)}) collective-permute-start(bf16[128,1152]{1,0:T(8,128)(2,1)S(1)} %copy-done.48), channel_id=1, source_target_pairs={{0,2},{1,3},{2,0},{3,1},{4,6},{5,7},{6,4},{7,5},{8,10},{9,11},{10,... | collective-permute-start | bytes 884744 | tf_op jit(solution)/shard_map/ppermute | solution.py:556
  157.4 31.5 %collective-permute-start.57 = (bf16[432,768]{1,0:T(8,128)(2,1)S(1)}, bf16[432,768]{1,0:T(8,128)(2,1)S(1)}, u32[]{:S(2)}, u32[]{:S(2)}) collective-permute-start(bf16[432,768]{1,0:T(8,128)(2,1)S(1)} %add_convert_fusion), channel_id=1, source_target_pairs={{0,16},{8,24},{16,0},{24,8},{1,17},{9,25},{17,1},{25,9},{2,18},{10... | collective-permute-start | bytes 1990664 | tf_op jit(solution)/shard_map/ppermute | solution.py:560
  158.2 28.2 %collective-permute-start.56 = (bf16[432,768]{1,0:T(8,128)(2,1)S(1)}, bf16[432,768]{1,0:T(8,128)(2,1)S(1)}, u32[]{:S(2)}, u32[]{:S(2)}) collective-permute-start(bf16[432,768]{1,0:T(8,128)(2,1)S(1)} %copy-done.69), channel_id=1, source_target_pairs={{0,8},{8,0},{16,24},{24,16},{1,9},{9,1},{17,25},{25,17},{2,10},{10... | collective-permute-start | bytes 1990664 | tf_op jit(solution)/shard_map/ppermute | solution.py:560
  192.7 10.9 %collective-permute-start.58 = (bf16[4,128,1152]{2,1,0:T(8,128)(2,1)}, bf16[4,128,1152]{2,1,0:T(8,128)(2,1)}, u32[]{:S(2)}, u32[]{:S(2)}) collective-permute-start(bf16[4,128,1152]{2,1,0:T(8,128)(2,1)} %get-tuple-element.359), channel_id=1, source_target_pairs={{0,1},{1,0},{2,3},{3,2},{4,5},{5,4},{6,7},{7,6},{8,9},{9,8},{10,11... | collective-permute-start | bytes 3538952 | tf_op jit(solution)/shard_map/ppermute | solution.py:556
  192.7 9.8 %collective-permute-start.59 = (bf16[304,512]{1,0:T(8,128)(2,1)S(1)}, bf16[304,512]{1,0:T(8,128)(2,1)S(1)}, u32[]{:S(2)}, u32[]{:S(2)}) collective-permute-start(bf16[304,512]{1,0:T(8,128)(2,1)S(1)} %get-tuple-element.352), channel_id=1, source_target_pairs={{0,8},{8,0},{16,24},{24,16},{1,9},{9,1},{17,25},{25,17},{2,10},{10... | collective-permute-start | bytes 933896 | tf_op jit(solution)/shard_map/ppermute | solution.py:560
  192.7 19.7 %collective-permute-start.48 = (bf16[128,1152]{1,0:T(8,128)(2,1)}, bf16[128,1152]{1,0:T(8,128)(2,1)}, u32[]{:S(2)}, u32[]{:S(2)}) collective-permute-start(bf16[128,1152]{1,0:T(8,128)(2,1)} %get-tuple-element.422), channel_id=1, source_target_pairs={{0,6},{1,7},{2,4},{3,5},{4,2},{5,3},{6,0},{7,1},{8,14},{9,15},{10,... | collective-permute-start | bytes 884744 | tf_op jit(solution)/shard_map/ppermute | solution.py:556
  195.1 14.6 %collective-permute-start.47 = (bf16[128,1152]{1,0:T(8,128)(2,1)}, bf16[128,1152]{1,0:T(8,128)(2,1)}, u32[]{:S(2)}, u32[]{:S(2)}) collective-permute-start(bf16[128,1152]{1,0:T(8,128)(2,1)} %get-tuple-element.423), channel_id=1, source_target_pairs={{0,4},{1,5},{2,6},{3,7},{4,0},{5,1},{6,2},{7,3},{8,12},{9,13},{10,... | collective-permute-start | bytes 884744 | tf_op jit(solution)/shard_map/ppermute | solution.py:556
  195.9 16.6 %collective-permute-start.46 = (bf16[128,1152]{1,0:T(8,128)(2,1)}, bf16[128,1152]{1,0:T(8,128)(2,1)}, u32[]{:S(2)}, u32[]{:S(2)}) collective-permute-start(bf16[128,1152]{1,0:T(8,128)(2,1)} %get-tuple-element.424), channel_id=1, source_target_pairs={{0,2},{1,3},{2,0},{3,1},{4,6},{5,7},{6,4},{7,5},{8,10},{9,11},{10,... | collective-permute-start | bytes 884744 | tf_op jit(solution)/shard_map/ppermute | solution.py:556
  196.2 19.2 %all-to-all-start.1 = ((bf16[8,36,768]{2,1,0:T(8,128)(2,1)}), bf16[8,36,768]{2,1,0:T(8,128)(2,1)S(1)}, u32[]{:S(2)}, u32[]{:S(2)}) async-start(bf16[8,36,768]{2,1,0:T(8,128)(2,1)} %get-tuple-element.370), calls=%async_computation.1 | async-start | bytes 983040 | tf_op jit(solution)/shard_map/all_to_all | solution.py:1240
  202.6 16.7 %collective-permute-start.64 = (bf16[304,512]{1,0:T(8,128)(2,1)S(1)}, bf16[304,512]{1,0:T(8,128)(2,1)S(1)}, u32[]{:S(2)}, u32[]{:S(2)}) collective-permute-start(bf16[304,512]{1,0:T(8,128)(2,1)S(1)} %add_convert_fusion.1), channel_id=1, source_target_pairs={{0,16},{8,24},{16,0},{24,8},{1,17},{9,25},{17,1},{25,9},{2,18},{10... | collective-permute-start | bytes 933896 | tf_op jit(solution)/shard_map/ppermute | solution.py:560
  203.6 13.3 %collective-permute-start.63 = (bf16[304,512]{1,0:T(8,128)(2,1)S(1)}, bf16[304,512]{1,0:T(8,128)(2,1)S(1)}, u32[]{:S(2)}, u32[]{:S(2)}) collective-permute-start(bf16[304,512]{1,0:T(8,128)(2,1)S(1)} %get-tuple-element.369), channel_id=1, source_target_pairs={{0,8},{8,0},{16,24},{24,16},{1,9},{9,1},{17,25},{25,17},{2,10},{10... | collective-permute-start | bytes 933896 | tf_op jit(solution)/shard_map/ppermute | solution.py:560
  209.7 18.0 %collective-permute-start.62 = (bf16[128,1152]{1,0:T(8,128)(2,1)}, bf16[128,1152]{1,0:T(8,128)(2,1)S(1)}, u32[]{:S(2)}, u32[]{:S(2)}) collective-permute-start(bf16[128,1152]{1,0:T(8,128)(2,1)} %get-tuple-element.421), channel_id=1, source_target_pairs={{0,6},{1,7},{2,4},{3,5},{4,2},{5,3},{6,0},{7,1},{8,14},{9,15},{10,... | collective-permute-start | bytes 884744 | tf_op jit(solution)/shard_map/ppermute | solution.py:556
  212.4 15.2 %collective-permute-start.61 = (bf16[128,1152]{1,0:T(8,128)(2,1)}, bf16[128,1152]{1,0:T(8,128)(2,1)S(1)}, u32[]{:S(2)}, u32[]{:S(2)}) collective-permute-start(bf16[128,1152]{1,0:T(8,128)(2,1)} %get-tuple-element.418), channel_id=1, source_target_pairs={{0,4},{1,5},{2,6},{3,7},{4,0},{5,1},{6,2},{7,3},{8,12},{9,13},{10,... | collective-permute-start | bytes 884744 | tf_op jit(solution)/shard_map/ppermute | solution.py:556
  213.3 14.4 %collective-permute-start.60 = (bf16[128,1152]{1,0:T(8,128)(2,1)}, bf16[128,1152]{1,0:T(8,128)(2,1)S(1)}, u32[]{:S(2)}, u32[]{:S(2)}) collective-permute-start(bf16[128,1152]{1,0:T(8,128)(2,1)} %get-tuple-element.419), channel_id=1, source_target_pairs={{0,2},{1,3},{2,0},{3,1},{4,6},{5,7},{6,4},{7,5},{8,10},{9,11},{10,... | collective-permute-start | bytes 884744 | tf_op jit(solution)/shard_map/ppermute | solution.py:556
  220.1 11.4 %all-to-all-start.2 = ((bf16[8,40,512]{2,1,0:T(8,128)(2,1)}), bf16[8,40,512]{2,1,0:T(8,128)(2,1)S(1)}, u32[]{:S(2)}, u32[]{:S(2)}) async-start(bf16[8,40,512]{2,1,0:T(8,128)(2,1)} %split_back.1), calls=%async_computation.2 | async-start | bytes 655360 | tf_op jit(solution)/shard_map/all_to_all | solution.py:1252
  (92 other events, 720.8 us)

commit v3 on v2

--- a/solution.py
+++ b/solution.py
@@ -1191,7 +1191,7 @@
     wo_own = order.then(lax.dynamic_slice(order(w_out), (jnp.minimum(i, KEY_HEADS - 1) * HG, 0), (HG, W)))
     call_c = order.then(join(late(order(both_cores(order.wait(cs))))))
     feeds = order((feed, g_one, g_two, g_three, d_own, d_one, d_two, d_three))
-    hidden, dgu, pm, pe, down, dots_two = order.then(run_feed(sc, mixed, call_c, late(feeds)))
+    hidden, dgu, pm, pe, down, dots_two = order.then(run_feed(sc, mixed, call_c, feeds))
 
     got = pc(pe, 1)
     grad_gu = order.then(lax.dot_general(order(mixed), dgu, TN, preferred_element_type=F32).astype(BF16))

time: 234 us -> 233 us (level)
    unnamed x144 -> x148, local copies, waits for them, and re-layouts: 6.69 us -> 6.01 us
  transfers between devices with their start and end apart: 68 -> 68, of which waited for: 35 -> 33; matrix products, arithmetic and copies ran while one was open for 5% -> 5% of each run, Pallas kernels for 18% -> 18%
where the time goes in v3:
time: 233 us; the launch traced here: 232 us
  waiting for transfers between devices  74.5 us (32%)
  starting transfers between devices  72.4 us (31%)
  Pallas kernels  64.4 us (28%)
  local copies, waits for them, and re-layouts  8.27 us (4%)
  other arithmetic  7.89 us (3%)
  matrix products  3.31 us (1%)
    pallas_call x19, Pallas kernels, call(): pl.pallas_call(body, out_shape=outs, scratch_shapes=scratch, compiler_par...  64.4 us
    ppermute x18, waiting for transfers between devices, pz(): return lax.ppermute(value, 'grp', [(s, s ^ k) for s in range(4)])  39.6 us
    ppermute x47, starting transfers between devices, pc(): return lax.ppermute(value, 'ctx', [(s, s ^ k) for s in range(8)])  37.5 us
    ppermute x47, waiting for transfers between devices, pc(): return lax.ppermute(value, 'ctx', [(s, s ^ k) for s in range(8)])  30.4 us
    ppermute x18, starting transfers between devices, pz(): return lax.ppermute(value, 'grp', [(s, s ^ k) for s in range(4)])  22.5 us
    unnamed x148, local copies, waits for them, and re-layouts  6.01 us
    all_to_all x1, starting transfers between devices, fast_local(): packed = lax.all_to_all(packed, 'ctx', 0, 0, tiled=True)  5.42 us
  transfers between devices with their start and end apart: 68, of which 33 were waited for; matrix products, arithmetic and copies ran while one was open for 5% of the time, Pallas kernels for 18%

profile of v3, /device:TPU:0, one launch (start us, length us, event | category | flops | bytes accessed | tf_op | source)
XLA Modules:
  0.0 232.3 jit_solution(13608889509070937913)
XLA Ops:
  1.5 2.4 %pack.1 = bf16[8,40,1152]{2,1,0:T(8,128)(2,1)} custom-call(bf16[324,128]{1,0:T(8,128)(2,1)} %bitcast.66, bf16[108,128]{1,0:T(8,128)(2,1)} %bitcast.73, bf16[108,128]{1,0:T(8,128)(2,1)} %bitcast.74, bf16[864,128]{1,0:T(8,128)(2,1)} %bitcast.64, bf16[864,128]{1,0:T(8,128)(2,1)} %bitcast.65, bf16[1,1152]{1,0:T(2,128)(2,1)S(1)} %dynamic_update_slice.3.gain), custom_call_target="tpu_custom_call" | custom-call | bytes 1 | tf_op jit(solution)/shard_map/pack/pallas_call | solution.py:632
  4.0 5.4 %all-to-all-start = ((bf16[8,40,1152]{2,1,0:T(8,128)(2,1)}), bf16[8,40,1152]{2,1,0:T(8,128)(2,1)S(1)}, u32[]{:S(2)}, u32[]{:S(2)}) async-start(bf16[8,40,1152]{2,1,0:T(8,128)(2,1)} %pack.1), calls=%async_computation | async-start | bytes 1474560 | tf_op jit(solution)/shard_map/all_to_all | solution.py:1106
  9.4 2.7 %collective-permute-start.1 = (bf16[324,128]{1,0:T(8,128)(2,1)S(1)}, bf16[324,128]{1,0:T(8,128)(2,1)S(1)}, u32[]{:S(2)}, u32[]{:S(2)}) collective-permute-start(bf16[324,128]{1,0:T(8,128)(2,1)S(1)} %bitcast.67), channel_id=1, source_target_pairs={{0,16},{8,24},{16,0},{24,8},{1,17},{9,25},{17,1},{25,9},{2,18},{10... | collective-permute-start | bytes 248840 | tf_op jit(solution)/shard_map/ppermute | solution.py:560
  12.0 1.6 collective-permute-start
  13.6 2.0 collective-permute-start.8
  17.6 4.4 %all-to-all-done.src = bf16[8,40,1152]{2,1,0:T(8,128)(2,1)S(1)} async-done(((bf16[8,40,1152]{2,1,0:T(8,128)(2,1)}), bf16[8,40,1152]{2,1,0:T(8,128)(2,1)S(1)}, u32[]{:S(2)}, u32[]{:S(2)}) %all-to-all-start) | async-done | bytes 737312 | tf_op jit(solution)/shard_map/all_to_all | solution.py:1106
  24.4 2.6 %collective-permute-start.5 = (bf16[8,40,384]{2,1,0:T(8,128)(2,1)S(1)}, bf16[8,40,384]{2,1,0:T(8,128)(2,1)S(1)}, u32[]{:S(2)}, u32[]{:S(2)}) collective-permute-start(bf16[8,40,384]{2,1,0:T(8,128)(2,1)S(1)} %get-tuple-element.239.w0), channel_id=1, source_target_pairs={{0,16},{8,24},{16,0},{24,8},{1,17},{9,25},{17,1},{25,9},{2,18},{10... | collective-permute-start | bytes 737288 | tf_op jit(solution)/shard_map/ppermute | solution.py:560
  28.6 2.0 collective-permute-start.2
  30.7 1.8 collective-permute-done.6.w1
  33.8 2.4 %collective-permute-start.9 = (bf16[8,40,384]{2,1,0:T(8,128)(2,1)S(1)}, bf16[8,40,384]{2,1,0:T(8,128)(2,1)S(1)}, u32[]{:S(2)}, u32[]{:S(2)}) collective-permute-start(bf16[8,40,384]{2,1,0:T(8,128)(2,1)S(1)} %collective-permute-done.5.w2), channel_id=1, source_target_pairs={{0,8},{8,0},{16,24},{24,16},{1,9},{9,1},{17,25},{25,17},{2,10},{10... | collective-permute-start | bytes 737288 | tf_op jit(solution)/shard_map/ppermute | solution.py:560
  36.2 5.0 %collective-permute-done.10 = bf16[324,128]{1,0:T(8,128)(2,1)S(1)} collective-permute-done((bf16[324,128]{1,0:T(8,128)(2,1)S(1)}, bf16[324,128]{1,0:T(8,128)(2,1)S(1)}, u32[]{:S(2)}, u32[]{:S(2)}) %collective-permute-start.10) | collective-permute-done | bytes 82976 | tf_op jit(solution)/shard_map/ppermute | solution.py:560
  43.0 2.6 %collective-permute-start.16 = (bf16[96,1152]{1,0:T(8,128)(2,1)S(1)}, bf16[96,1152]{1,0:T(8,128)(2,1)}, u32[]{:S(2)}, u32[]{:S(2)}) collective-permute-start(bf16[96,1152]{1,0:T(8,128)(2,1)S(1)} %reshape.202.d0), channel_id=1, source_target_pairs={{0,16},{8,24},{16,0},{24,8},{1,17},{9,25},{17,1},{25,9},{2,18},{10... | collective-permute-start | bytes 663560 | tf_op jit(solution)/shard_map/ppermute | solution.py:560
  45.6 1.6 collective-permute-start.15
  47.2 2.4 %collective-permute-start.22 = (bf16[4,324,128]{2,1,0:T(8,128)(2,1)S(1)}, bf16[4,324,128]{2,1,0:T(8,128)(2,1)}, u32[]{:S(2)}, u32[]{:S(2)}) collective-permute-start(bf16[4,324,128]{2,1,0:T(8,128)(2,1)S(1)} %pad_maximum_fusion.b0), channel_id=1, source_target_pairs={{0,6},{1,7},{2,4},{3,5},{4,2},{5,3},{6,0},{7,1},{8,14},{9,15},{10,... | collective-permute-start | bytes 995336 | tf_op jit(solution)/shard_map/ppermute | solution.py:556
  49.6 3.3 %collective-permute-start.21 = (bf16[4,324,128]{2,1,0:T(8,128)(2,1)S(1)}, bf16[4,324,128]{2,1,0:T(8,128)(2,1)}, u32[]{:S(2)}, u32[]{:S(2)}) collective-permute-start(bf16[4,324,128]{2,1,0:T(8,128)(2,1)S(1)} %pad_maximum_fusion.b0), channel_id=1, source_target_pairs={{0,4},{1,5},{2,6},{3,7},{4,0},{5,1},{6,2},{7,3},{8,12},{9,13},{10,... | collective-permute-start | bytes 995336 | tf_op jit(solution)/shard_map/ppermute | solution.py:556
  54.8 11.0 %attend.1 = (bf16[512,384]{1,0:T(8,128)(2,1)S(1)}, f32[8,1152]{1,0:T(8,128)S(1)}, bf16[1152,384]{1,0:T(8,128)(2,1)S(1)}, bf16[2,512,256]{2,1,0:T(8,128)(2,1)}, b...) custom-call(s32[2]{0:T(128)S(1)} %pad_add_fusion.sc, ...), custom_call_target="tpu_custom_call" | custom-call | bytes 1 | tf_op jit(solution)/shard_map/attend/pallas_call | solution.py:632
  68.3 1.7 collective-permute-start.17
  73.8 2.6 %output_weight.1.wo = bf16[1152,1152]{1,0:T(8,128)(2,1)S(1)} custom-call(s32[2]{0:T(128)S(1)} %pad_add_fusion.sc, bf16[4,324,128]{2,1,0:T(8,128)(2,1)} %copy-done.26, bf16[4,324,128]{2,1,0:T(8,128)(2,1)} %collective-permute-done.20.b1, bf16[4,324,128]{2,1,0:T(8,128)(2,1)} %collective-permute-done.21.b2, bf16[4,324,128]{2,1,0:T(8,128)(2,1)} %collective-permute-done.22.b3, ...), custom_call_target="tpu_custom_call" | custom-call | bytes 1 | tf_op jit(solution)/shard_map/output_weight/pallas_call | solution.py:632
  76.3 5.5 %collective-permute-done.19.d3 = bf16[96,1152]{1,0:T(8,128)(2,1)S(1)} collective-permute-done((bf16[96,1152]{1,0:T(8,128)(2,1)}, bf16[96,1152]{1,0:T(8,128)(2,1)S(1)}, u32[]{:S(2)}, u32[]{:S(2)}) %collective-permute-start.19) | collective-permute-done | bytes 221216 | tf_op jit(solution)/shard_map/ppermute | solution.py:560
  84.0 4.7 %collective-permute-done.27.a3 = bf16[512,384]{1,0:T(8,128)(2,1)S(1)} collective-permute-done((bf16[512,384]{1,0:T(8,128)(2,1)S(1)}, bf16[512,384]{1,0:T(8,128)(2,1)S(1)}, u32[]{:S(2)}, u32[]{:S(2)}) %collective-permute-start.27) | collective-permute-done | bytes 393248 | tf_op jit(solution)/shard_map/ppermute | solution.py:556
  92.1 3.8 %collective-permute-done.32.g2 = bf16[288,768]{1,0:T(8,128)(2,1)} collective-permute-done((bf16[288,768]{1,0:T(8,128)(2,1)}, bf16[288,768]{1,0:T(8,128)(2,1)}, u32[]{:S(2)}, u32[]{:S(2)}) %collective-permute-start.32) | collective-permute-done | bytes 442400 | tf_op jit(solution)/shard_map/ppermute | solution.py:560
  95.9 2.0 collective-permute-start.33
  97.9 2.0 collective-permute-start.38
  100.7 9.1 %project.1 = (bf16[1024,1152]{1,0:T(8,128)(2,1)}, bf16[1024,1152]{1,0:T(8,128)(2,1)S(1)}, f32[128,1152]{1,0:T(8,128)}) custom-call(s32[2]{0:T(128)S(1)} %pad_add_fusion.sc, bf16[1024,1152]{1,0:T(8,128)(2,1)} %get-tuple-element.243.x, bf16[512,384]{1,0:T(8,128)(2,1)} %copy-done.16, bf16[512,384]{1,0:T(8,128)(2,1)} %copy-done.32, bf16[512,384]{1,0:T(8,128)(2,1)} %copy-done.31, ...), custom_call_target="tpu_custom_call" | custom-call | bytes 1 | tf_op jit(solution)/shard_map/project/pallas_call | solution.py:632
  114.2 1.8 join.1.c
  117.0 8.3 %feed.1 = (bf16[1024,384]{1,0:T(8,128)(2,1)S(1)}, bf16[1024,768]{1,0:T(8,128)(2,1)S(1)}, bf16[4,128,1152]{2,1,0:T(8,128)(2,1)S(1)}, bf16[4,128,1152]{2,1,0:T(8,1...) custom-call(s32[2]{0:T(128)S(1)} %pad_add_fusion.sc, ...), custom_call_target="tpu_custom_call" | custom-call | bytes 1 | tf_op jit(solution)/shard_map/feed/pallas_call | solution.py:632
  125.3 2.1 convolution_convert_fusion.grad_gu
  129.7 2.3 grads.1
  133.0 1.7 collective-permute-start.41
  136.4 12.7 %collective-permute-done.44 = bf16[432,768]{1,0:T(8,128)(2,1)S(1)} collective-permute-done((bf16[432,768]{1,0:T(8,128)(2,1)}, bf16[432,768]{1,0:T(8,128)(2,1)S(1)}, u32[]{:S(2)}, u32[]{:S(2)}) %collective-permute-start.44) | collective-permute-done | bytes 663584 | tf_op jit(solution)/shard_map/ppermute | solution.py:560
  149.3 2.6 %mid.1 = (f32[128,1152]{1,0:T(8,128)}, bf16[128,1152]{1,0:T(8,128)(2,1)}) custom-call(bf16[128,1152]{1,0:T(8,128)(2,1)S(1)} %get-tuple-element.322.a, bf16[128,1152]{1,0:T(8,128)(2,1)S(1)} %collective-permute-done.41.b, bf16[128,1152]{1,0:T(8,128)(2,1)S(1)} %collective-permute-done.42.d, bf16[128,1152]{1,0:T(8,128)(2,1)S(1)} %collective-permute-done.43.f, ...), custom_call_target="tpu_custom_call" | custom-call | bytes 1 | tf_op jit(solution)/shard_map/mid/pallas_call | solution.py:632
  153.5 2.0 collective-permute-start.51
  159.9 4.4 %collective-permute-done.51.l3 = bf16[128,1152]{1,0:T(8,128)(2,1)S(1)} collective-permute-done((bf16[128,1152]{1,0:T(8,128)(2,1)S(1)}, bf16[128,1152]{1,0:T(8,128)(2,1)S(1)}, u32[]{:S(2)}, u32[]{:S(2)}) %collective-permute-start.51) | collective-permute-done | bytes 294944 | tf_op jit(solution)/shard_map/ppermute | solution.py:556
  164.3 5.8 %collective-permute-done.50.l2 = bf16[128,1152]{1,0:T(8,128)(2,1)S(1)} collective-permute-done((bf16[128,1152]{1,0:T(8,128)(2,1)S(1)}, bf16[128,1152]{1,0:T(8,128)(2,1)S(1)}, u32[]{:S(2)}, u32[]{:S(2)}) %collective-permute-start.50) | collective-permute-done | bytes 294944 | tf_op jit(solution)/shard_map/ppermute | solution.py:556
  174.1 11.6 %back.1 = (bf16[1024,384]{1,0:T(8,128)(2,1)S(1)}, bf16[304,512]{1,0:T(8,128)(2,1)S(1)}, bf16[304,512]{1,0:T(8,128)(2,1)S(1)}, bf16[304,512]{1,0:T(8,128)(2,1)S(1)}, bf16[304,512]{1,0:T(8,128)(2,1)}) custom-call(s32[2]{0:T(128)S(1)} %pad_add_fusion.sc, bf16[128,1152]{1,0:T(8,128)(2,1)} %get-tuple-element.336.l0, bf16[128,1152]{1,0:T(8,128)(2,1)} %copy-done.54, ...), custom_call_target="tpu_custom_call" | custom-call | bytes 1 | tf_op jit(solution)/shard_map/back/pallas_call | solution.py:632
  185.7 2.9 %collective-permute-done.57.d = bf16[432,768]{1,0:T(8,128)(2,1)S(1)} collective-permute-done((bf16[432,768]{1,0:T(8,128)(2,1)S(1)}, bf16[432,768]{1,0:T(8,128)(2,1)S(1)}, u32[]{:S(2)}, u32[]{:S(2)}) %collective-permute-start.57) | collective-permute-done | bytes 663584 | tf_op jit(solution)/shard_map/ppermute | solution.py:560
  189.7 2.6 %inward.1 = (bf16[4,128,1152]{2,1,0:T(8,128)(2,1)S(1)}, bf16[4,128,1152]{2,1,0:T(8,128)(2,1)}) custom-call(bf16[1024,384]{1,0:T(8,128)(2,1)S(1)} %get-tuple-element.357.rows, bf16[1152,384]{1,0:T(8,128)(2,1)S(1)} %get-tuple-element.347.w_slab.weight), custom_call_target="tpu_custom_call" | custom-call | bytes 1 | tf_op jit(solution)/shard_map/inward/pallas_call | solution.py:632
  192.4 2.0 collective-permute-start.48
  196.0 3.5 %all-to-all-start.1 = ((bf16[8,36,768]{2,1,0:T(8,128)(2,1)}), bf16[8,36,768]{2,1,0:T(8,128)(2,1)S(1)}, u32[]{:S(2)}, u32[]{:S(2)}) async-start(bf16[8,36,768]{2,1,0:T(8,128)(2,1)} %get-tuple-element.370), calls=%async_computation.1 | async-start | bytes 983040 | tf_op jit(solution)/shard_map/all_to_all | solution.py:1240
  199.5 2.8 %collective-permute-done.59 = bf16[304,512]{1,0:T(8,128)(2,1)S(1)} collective-permute-done((bf16[304,512]{1,0:T(8,128)(2,1)}, bf16[304,512]{1,0:T(8,128)(2,1)S(1)}, u32[]{:S(2)}, u32[]{:S(2)}) %collective-permute-start.59) | collective-permute-done | bytes 311328 | tf_op jit(solution)/shard_map/ppermute | solution.py:560
  204.7 2.5 %fusion.11 = (bf16[128,1152]{1,0:T(8,128)(2,1)}, bf16[128,1152]{1,0:T(8,128)(2,1)}, bf16[128,1152]{1,0:T(8,128)(2,1)}, bf16[128,1152]{1,0:T(8,128)(2,1)}) fusion(bf16[4,128,1152]{2,1,0:T(8,128)(2,1)} %collective-permute-done.58, bf16[4,128,1152]{2,1,0:T(8,128)(2,1)S(1)} %get-tuple-element.358), kind=kLoop, calls=%fused_computation.32 | loop fusion | flops 2359296 | bytes 3538944 | tf_op jit(solution)/shard_map/convert_element_type | solution.py:587
  207.3 2.1 collective-permute-done.47
  209.4 2.5 %collective-permute-start.62 = (bf16[128,1152]{1,0:T(8,128)(2,1)}, bf16[128,1152]{1,0:T(8,128)(2,1)S(1)}, u32[]{:S(2)}, u32[]{:S(2)}) collective-permute-start(bf16[128,1152]{1,0:T(8,128)(2,1)} %get-tuple-element.421), channel_id=1, source_target_pairs={{0,6},{1,7},{2,4},{3,5},{4,2},{5,3},{6,0},{7,1},{8,14},{9,15},{10,... | collective-permute-start | bytes 884744 | tf_op jit(solution)/shard_map/ppermute | solution.py:556
  213.2 2.1 add_convert_fusion.5
  216.7 2.3 collective-permute-done.64.d
  219.9 3.4 %all-to-all-start.2 = ((bf16[8,40,512]{2,1,0:T(8,128)(2,1)}), bf16[8,40,512]{2,1,0:T(8,128)(2,1)S(1)}, u32[]{:S(2)}, u32[]{:S(2)}) async-start(bf16[8,40,512]{2,1,0:T(8,128)(2,1)} %split_back.1), calls=%async_computation.2 | async-start | bytes 655360 | tf_op jit(solution)/shard_map/all_to_all | solution.py:1252
  223.3 3.9 %collective-permute-done.61.d = bf16[128,1152]{1,0:T(8,128)(2,1)S(1)} collective-permute-done((bf16[128,1152]{1,0:T(8,128)(2,1)}, bf16[128,1152]{1,0:T(8,128)(2,1)S(1)}, u32[]{:S(2)}, u32[]{:S(2)}) %collective-permute-start.61) | collective-permute-done | bytes 294944 | tf_op jit(solution)/shard_map/ppermute | solution.py:556
  228.1 2.6 %last.1 = bf16[128,1152]{1,0:T(8,128)(2,1)} custom-call(bf16[128,1152]{1,0:T(8,128)(2,1)} %get-tuple-element.376.a, bf16[128,1152]{1,0:T(8,128)(2,1)} %copy-done.57, bf16[128,1152]{1,0:T(8,128)(2,1)} %copy-done.56, bf16[128,1152]{1,0:T(8,128)(2,1)} %copy-done.55, bf16[128,1152]{1,0:T(8,128)(2,1)} %bitcast.59, f32[128,1152]{1,0:T(8,128)} %get-tuple-element.380.dres, ...), custom_call_target="tpu_custom_call" | custom-call | bytes 1 | tf_op jit(solution)/shard_map/last/pallas_call | solution.py:632
  (285 shorter events, 56.0 us)
Async XLA Ops:
  4.0 18.0 %all-to-all-start = ((bf16[8,40,1152]{2,1,0:T(8,128)(2,1)}), bf16[8,40,1152]{2,1,0:T(8,128)(2,1)S(1)}, u32[]{:S(2)}, u32[]{:S(2)}) async-start(bf16[8,40,1152]{2,1,0:T(8,128)(2,1)} %pack.1), calls=%async_computation | async-start | bytes 1474560 | tf_op jit(solution)/shard_map/all_to_all | solution.py:1106
  9.4 8.2 %collective-permute-start.1 = (bf16[324,128]{1,0:T(8,128)(2,1)S(1)}, bf16[324,128]{1,0:T(8,128)(2,1)S(1)}, u32[]{:S(2)}, u32[]{:S(2)}) collective-permute-start(bf16[324,128]{1,0:T(8,128)(2,1)S(1)} %bitcast.67), channel_id=1, source_target_pairs={{0,16},{8,24},{16,0},{24,8},{1,17},{9,25},{17,1},{25,9},{2,18},{10... | collective-permute-start | bytes 248840 | tf_op jit(solution)/shard_map/ppermute | solution.py:560
  12.0 5.6 %collective-permute-start = (bf16[324,128]{1,0:T(8,128)(2,1)S(1)}, bf16[324,128]{1,0:T(8,128)(2,1)S(1)}, u32[]{:S(2)}, u32[]{:S(2)}) collective-permute-start(bf16[324,128]{1,0:T(8,128)(2,1)S(1)} %bitcast.68), channel_id=1, source_target_pairs={{0,8},{8,0},{16,24},{24,16},{1,9},{9,1},{17,25},{25,17},{2,10},{10... | collective-permute-start | bytes 248840 | tf_op jit(solution)/shard_map/ppermute | solution.py:560
  13.6 13.9 %collective-permute-start.8 = (bf16[128,1152]{1,0:T(8,128)(2,1)}, bf16[128,1152]{1,0:T(8,128)(2,1)S(1)}, u32[]{:S(2)}, u32[]{:S(2)}) collective-permute-start(bf16[128,1152]{1,0:T(8,128)(2,1)} %bitcast.3.refs_0_.c), channel_id=1, source_target_pairs={{0,4},{1,5},{2,6},{3,7},{4,0},{5,1},{6,2},{7,3},{8,12},{9,13},{10,... | collective-permute-start | bytes 884744 | tf_op jit(solution)/shard_map/ppermute | solution.py:556
  15.6 13.0 %collective-permute-start.7 = (bf16[128,1152]{1,0:T(8,128)(2,1)}, bf16[128,1152]{1,0:T(8,128)(2,1)}, u32[]{:S(2)}, u32[]{:S(2)}) collective-permute-start(bf16[128,1152]{1,0:T(8,128)(2,1)} %bitcast.3.refs_0_.c), channel_id=1, source_target_pairs={{0,2},{1,3},{2,0},{3,1},{4,6},{5,7},{6,4},{7,5},{8,10},{9,11},{10,... | collective-permute-start | bytes 884744 | tf_op jit(solution)/shard_map/ppermute | solution.py:556
  22.8 9.7 %collective-permute-start.6 = (bf16[8,40,384]{2,1,0:T(8,128)(2,1)S(1)}, bf16[8,40,384]{2,1,0:T(8,128)(2,1)S(1)}, u32[]{:S(2)}, u32[]{:S(2)}) collective-permute-start(bf16[8,40,384]{2,1,0:T(8,128)(2,1)S(1)} %get-tuple-element.239.w0), channel_id=1, source_target_pairs={{0,8},{8,0},{16,24},{24,16},{1,9},{9,1},{17,25},{25,17},{2,10},{10... | collective-permute-start | bytes 737288 | tf_op jit(solution)/shard_map/ppermute | solution.py:560
  24.4 9.5 %collective-permute-start.5 = (bf16[8,40,384]{2,1,0:T(8,128)(2,1)S(1)}, bf16[8,40,384]{2,1,0:T(8,128)(2,1)S(1)}, u32[]{:S(2)}, u32[]{:S(2)}) collective-permute-start(bf16[8,40,384]{2,1,0:T(8,128)(2,1)S(1)} %get-tuple-element.239.w0), channel_id=1, source_target_pairs={{0,16},{8,24},{16,0},{24,8},{1,17},{9,25},{17,1},{25,9},{2,18},{10... | collective-permute-start | bytes 737288 | tf_op jit(solution)/shard_map/ppermute | solution.py:560
  27.0 14.4 %collective-permute-start.4 = (bf16[128,1280]{1,0:T(8,128)(2,1)S(1)}, bf16[128,1280]{1,0:T(8,128)(2,1)S(1)}, u32[]{:S(2)}, u32[]{:S(2)}) collective-permute-start(bf16[128,1280]{1,0:T(8,128)(2,1)S(1)} %pad_maximum_fusion.1.x0), channel_id=1, source_target_pairs={{0,6},{1,7},{2,4},{3,5},{4,2},{5,3},{6,0},{7,1},{8,14},{9,15},{10,... | collective-permute-start | bytes 983048 | tf_op jit(solution)/shard_map/ppermute | solution.py:556
  27.5 14.3 %collective-permute-start.3 = (bf16[128,1280]{1,0:T(8,128)(2,1)S(1)}, bf16[128,1280]{1,0:T(8,128)(2,1)S(1)}, u32[]{:S(2)}, u32[]{:S(2)}) collective-permute-start(bf16[128,1280]{1,0:T(8,128)(2,1)S(1)} %pad_maximum_fusion.1.x0), channel_id=1, source_target_pairs={{0,4},{1,5},{2,6},{3,7},{4,0},{5,1},{6,2},{7,3},{8,12},{9,13},{10,... | collective-permute-start | bytes 983048 | tf_op jit(solution)/shard_map/ppermute | solution.py:556
  28.6 13.3 %collective-permute-start.2 = (bf16[128,1280]{1,0:T(8,128)(2,1)S(1)}, bf16[128,1280]{1,0:T(8,128)(2,1)S(1)}, u32[]{:S(2)}, u32[]{:S(2)}) collective-permute-start(bf16[128,1280]{1,0:T(8,128)(2,1)S(1)} %pad_maximum_fusion.1.x0), channel_id=1, source_target_pairs={{0,2},{1,3},{2,0},{3,1},{4,6},{5,7},{6,4},{7,5},{8,10},{9,11},{10,... | collective-permute-start | bytes 983048 | tf_op jit(solution)/shard_map/ppermute | solution.py:556
  33.8 7.5 %collective-permute-start.9 = (bf16[8,40,384]{2,1,0:T(8,128)(2,1)S(1)}, bf16[8,40,384]{2,1,0:T(8,128)(2,1)S(1)}, u32[]{:S(2)}, u32[]{:S(2)}) collective-permute-start(bf16[8,40,384]{2,1,0:T(8,128)(2,1)S(1)} %collective-permute-done.5.w2), channel_id=1, source_target_pairs={{0,8},{8,0},{16,24},{24,16},{1,9},{9,1},{17,25},{25,17},{2,10},{10... | collective-permute-start | bytes 737288 | tf_op jit(solution)/shard_map/ppermute | solution.py:560
  42.0 5.3 %collective-permute-start.12 = (bf16[128,1280]{1,0:T(8,128)(2,1)S(1)}, bf16[128,1280]{1,0:T(8,128)(2,1)S(1)}, u32[]{:S(2)}, u32[]{:S(2)}) collective-permute-start(bf16[128,1280]{1,0:T(8,128)(2,1)S(1)} %collective-permute-done.2.x1), channel_id=1, source_target_pairs={{0,1},{1,0},{2,3},{3,2},{4,5},{5,4},{6,7},{7,6},{8,9},{9,8},{10,11... | collective-permute-start | bytes 983048 | tf_op jit(solution)/shard_map/ppermute | solution.py:556
  42.5 7.2 %collective-permute-start.13 = (bf16[128,1280]{1,0:T(8,128)(2,1)S(1)}, bf16[128,1280]{1,0:T(8,128)(2,1)S(1)}, u32[]{:S(2)}, u32[]{:S(2)}) collective-permute-start(bf16[128,1280]{1,0:T(8,128)(2,1)S(1)} %collective-permute-done.3.x2), channel_id=1, source_target_pairs={{0,1},{1,0},{2,3},{3,2},{4,5},{5,4},{6,7},{7,6},{8,9},{9,8},{10,11... | collective-permute-start | bytes 983048 | tf_op jit(solution)/shard_map/ppermute | solution.py:556
  42.5 10.3 %collective-permute-start.14 = (bf16[128,1280]{1,0:T(8,128)(2,1)S(1)}, bf16[128,1280]{1,0:T(8,128)(2,1)S(1)}, u32[]{:S(2)}, u32[]{:S(2)}) collective-permute-start(bf16[128,1280]{1,0:T(8,128)(2,1)S(1)} %collective-permute-done.4.x3), channel_id=1, source_target_pairs={{0,1},{1,0},{2,3},{3,2},{4,5},{5,4},{6,7},{7,6},{8,9},{9,8},{10,11... | collective-permute-start | bytes 983048 | tf_op jit(solution)/shard_map/ppermute | solution.py:556
  43.0 22.8 %collective-permute-start.16 = (bf16[96,1152]{1,0:T(8,128)(2,1)S(1)}, bf16[96,1152]{1,0:T(8,128)(2,1)}, u32[]{:S(2)}, u32[]{:S(2)}) collective-permute-start(bf16[96,1152]{1,0:T(8,128)(2,1)S(1)} %reshape.202.d0), channel_id=1, source_target_pairs={{0,16},{8,24},{16,0},{24,8},{1,17},{9,25},{17,1},{25,9},{2,18},{10... | collective-permute-start | bytes 663560 | tf_op jit(solution)/shard_map/ppermute | solution.py:560
  45.6 20.2 %collective-permute-start.15 = (bf16[96,1152]{1,0:T(8,128)(2,1)S(1)}, bf16[96,1152]{1,0:T(8,128)(2,1)S(1)}, u32[]{:S(2)}, u32[]{:S(2)}) collective-permute-start(bf16[96,1152]{1,0:T(8,128)(2,1)S(1)} %reshape.202.d0), channel_id=1, source_target_pairs={{0,8},{8,0},{16,24},{24,16},{1,9},{9,1},{17,25},{25,17},{2,10},{10... | collective-permute-start | bytes 663560 | tf_op jit(solution)/shard_map/ppermute | solution.py:560
  47.2 19.4 %collective-permute-start.22 = (bf16[4,324,128]{2,1,0:T(8,128)(2,1)S(1)}, bf16[4,324,128]{2,1,0:T(8,128)(2,1)}, u32[]{:S(2)}, u32[]{:S(2)}) collective-permute-start(bf16[4,324,128]{2,1,0:T(8,128)(2,1)S(1)} %pad_maximum_fusion.b0), channel_id=1, source_target_pairs={{0,6},{1,7},{2,4},{3,5},{4,2},{5,3},{6,0},{7,1},{8,14},{9,15},{10,... | collective-permute-start | bytes 995336 | tf_op jit(solution)/shard_map/ppermute | solution.py:556
  49.6 17.0 %collective-permute-start.21 = (bf16[4,324,128]{2,1,0:T(8,128)(2,1)S(1)}, bf16[4,324,128]{2,1,0:T(8,128)(2,1)}, u32[]{:S(2)}, u32[]{:S(2)}) collective-permute-start(bf16[4,324,128]{2,1,0:T(8,128)(2,1)S(1)} %pad_maximum_fusion.b0), channel_id=1, source_target_pairs={{0,4},{1,5},{2,6},{3,7},{4,0},{5,1},{6,2},{7,3},{8,12},{9,13},{10,... | collective-permute-start | bytes 995336 | tf_op jit(solution)/shard_map/ppermute | solution.py:556
  52.9 13.7 %collective-permute-start.20 = (bf16[4,324,128]{2,1,0:T(8,128)(2,1)S(1)}, bf16[4,324,128]{2,1,0:T(8,128)(2,1)}, u32[]{:S(2)}, u32[]{:S(2)}) collective-permute-start(bf16[4,324,128]{2,1,0:T(8,128)(2,1)S(1)} %pad_maximum_fusion.b0), channel_id=1, source_target_pairs={{0,2},{1,3},{2,0},{3,1},{4,6},{5,7},{6,4},{7,5},{8,10},{9,11},{10,... | collective-permute-start | bytes 995336 | tf_op jit(solution)/shard_map/ppermute | solution.py:556
  67.3 16.6 %collective-permute-start.18 = (bf16[512,384]{1,0:T(8,128)(2,1)S(1)}, bf16[512,384]{1,0:T(8,128)(2,1)S(1)}, u32[]{:S(2)}, u32[]{:S(2)}) collective-permute-start(bf16[512,384]{1,0:T(8,128)(2,1)S(1)} %get-tuple-element.270.a0), channel_id=1, source_target_pairs={{0,4},{1,5},{2,6},{3,7},{4,0},{5,1},{6,2},{7,3},{8,12},{9,13},{10,... | collective-permute-start | bytes 1179656 | tf_op jit(solution)/shard_map/ppermute | solution.py:556
  68.3 15.6 %collective-permute-start.17 = (bf16[512,384]{1,0:T(8,128)(2,1)S(1)}, bf16[512,384]{1,0:T(8,128)(2,1)S(1)}, u32[]{:S(2)}, u32[]{:S(2)}) collective-permute-start(bf16[512,384]{1,0:T(8,128)(2,1)S(1)} %get-tuple-element.270.a0), channel_id=1, source_target_pairs={{0,2},{1,3},{2,0},{3,1},{4,6},{5,7},{6,4},{7,5},{8,10},{9,11},{10,... | collective-permute-start | bytes 1179656 | tf_op jit(solution)/shard_map/ppermute | solution.py:556
  70.1 18.6 %collective-permute-start.27 = (bf16[512,384]{1,0:T(8,128)(2,1)S(1)}, bf16[512,384]{1,0:T(8,128)(2,1)S(1)}, u32[]{:S(2)}, u32[]{:S(2)}) collective-permute-start(bf16[512,384]{1,0:T(8,128)(2,1)S(1)} %get-tuple-element.270.a0), channel_id=1, source_target_pairs={{0,6},{1,7},{2,4},{3,5},{4,2},{5,3},{6,0},{7,1},{8,14},{9,15},{10,... | collective-permute-start | bytes 1179656 | tf_op jit(solution)/shard_map/ppermute | solution.py:556
  71.1 10.8 %collective-permute-start.19 = (bf16[96,1152]{1,0:T(8,128)(2,1)}, bf16[96,1152]{1,0:T(8,128)(2,1)S(1)}, u32[]{:S(2)}, u32[]{:S(2)}) collective-permute-start(bf16[96,1152]{1,0:T(8,128)(2,1)} %collective-permute-done.16.d2), channel_id=1, source_target_pairs={{0,8},{8,0},{16,24},{24,16},{1,9},{9,1},{17,25},{25,17},{2,10},{10... | collective-permute-start | bytes 663560 | tf_op jit(solution)/shard_map/ppermute | solution.py:560
  72.9 23.0 %collective-permute-start.32 = (bf16[288,768]{1,0:T(8,128)(2,1)}, bf16[288,768]{1,0:T(8,128)(2,1)}, u32[]{:S(2)}, u32[]{:S(2)}) collective-permute-start(bf16[288,768]{1,0:T(8,128)(2,1)} %get-tuple-element.301.g0), channel_id=1, source_target_pairs={{0,16},{8,24},{16,0},{24,8},{1,17},{9,25},{17,1},{25,9},{2,18},{10... | collective-permute-start | bytes 1327112 | tf_op jit(solution)/shard_map/ppermute | solution.py:560
  95.9 14.6 %collective-permute-start.39 = (bf16[288,768]{1,0:T(8,128)(2,1)}, bf16[288,768]{1,0:T(8,128)(2,1)}, u32[]{:S(2)}, u32[]{:S(2)}) collective-permute-start(bf16[288,768]{1,0:T(8,128)(2,1)} %collective-permute-done.32.g2), channel_id=1, source_target_pairs={{0,8},{8,0},{16,24},{24,16},{1,9},{9,1},{17,25},{25,17},{2,10},{10... | collective-permute-start | bytes 1327112 | tf_op jit(solution)/shard_map/ppermute | solution.py:560
  95.9 13.9 %collective-permute-start.33 = (bf16[128,1152]{1,0:T(8,128)(2,1)}, bf16[128,1152]{1,0:T(8,128)(2,1)}, u32[]{:S(2)}, u32[]{:S(2)}) collective-permute-start(bf16[128,1152]{1,0:T(8,128)(2,1)} %bitcast.3.refs_0_.c), channel_id=1, source_target_pairs={{0,6},{1,7},{2,4},{3,5},{4,2},{5,3},{6,0},{7,1},{8,14},{9,15},{10,... | collective-permute-start | bytes 884744 | tf_op jit(solution)/shard_map/ppermute | solution.py:556
  97.9 19.1 %collective-permute-start.38 = (bf16[288,768]{1,0:T(8,128)(2,1)}, bf16[288,768]{1,0:T(8,128)(2,1)S(1)}, u32[]{:S(2)}, u32[]{:S(2)}) collective-permute-start(bf16[288,768]{1,0:T(8,128)(2,1)} %get-tuple-element.301.g0), channel_id=1, source_target_pairs={{0,8},{8,0},{16,24},{24,16},{1,9},{9,1},{17,25},{25,17},{2,10},{10... | collective-permute-start | bytes 1327112 | tf_op jit(solution)/shard_map/ppermute | solution.py:560
  131.9 17.2 %collective-permute-start.44 = (bf16[432,768]{1,0:T(8,128)(2,1)}, bf16[432,768]{1,0:T(8,128)(2,1)S(1)}, u32[]{:S(2)}, u32[]{:S(2)}) collective-permute-start(bf16[432,768]{1,0:T(8,128)(2,1)} %get-tuple-element.318), channel_id=1, source_target_pairs={{0,8},{8,0},{16,24},{24,16},{1,9},{9,1},{17,25},{25,17},{2,10},{10... | collective-permute-start | bytes 1990664 | tf_op jit(solution)/shard_map/ppermute | solution.py:560
  132.2 17.1 %collective-permute-start.42 = (bf16[128,1152]{1,0:T(8,128)(2,1)S(1)}, bf16[128,1152]{1,0:T(8,128)(2,1)S(1)}, u32[]{:S(2)}, u32[]{:S(2)}) collective-permute-start(bf16[128,1152]{1,0:T(8,128)(2,1)S(1)} %get-tuple-element.427), channel_id=1, source_target_pairs={{0,4},{1,5},{2,6},{3,7},{4,0},{5,1},{6,2},{7,3},{8,12},{9,13},{10,... | collective-permute-start | bytes 884744 | tf_op jit(solution)/shard_map/ppermute | solution.py:556
  133.0 16.3 %collective-permute-start.41 = (bf16[128,1152]{1,0:T(8,128)(2,1)S(1)}, bf16[128,1152]{1,0:T(8,128)(2,1)S(1)}, u32[]{:S(2)}, u32[]{:S(2)}) collective-permute-start(bf16[128,1152]{1,0:T(8,128)(2,1)S(1)} %get-tuple-element.428), channel_id=1, source_target_pairs={{0,2},{1,3},{2,0},{3,1},{4,6},{5,7},{6,4},{7,5},{8,10},{9,11},{10,... | collective-permute-start | bytes 884744 | tf_op jit(solution)/shard_map/ppermute | solution.py:556
  134.7 14.6 %collective-permute-start.43 = (bf16[128,1152]{1,0:T(8,128)(2,1)S(1)}, bf16[128,1152]{1,0:T(8,128)(2,1)S(1)}, u32[]{:S(2)}, u32[]{:S(2)}) collective-permute-start(bf16[128,1152]{1,0:T(8,128)(2,1)S(1)} %get-tuple-element.426), channel_id=1, source_target_pairs={{0,6},{1,7},{2,4},{3,5},{4,2},{5,3},{6,0},{7,1},{8,14},{9,15},{10,... | collective-permute-start | bytes 884744 | tf_op jit(solution)/shard_map/ppermute | solution.py:556
  153.5 10.8 %collective-permute-start.51 = (bf16[128,1152]{1,0:T(8,128)(2,1)S(1)}, bf16[128,1152]{1,0:T(8,128)(2,1)S(1)}, u32[]{:S(2)}, u32[]{:S(2)}) collective-permute-start(bf16[128,1152]{1,0:T(8,128)(2,1)S(1)} %copy-done.51), channel_id=1, source_target_pairs={{0,6},{1,7},{2,4},{3,5},{4,2},{5,3},{6,0},{7,1},{8,14},{9,15},{10,... | collective-permute-start | bytes 884744 | tf_op jit(solution)/shard_map/ppermute | solution.py:556
  155.5 14.6 %collective-permute-start.50 = (bf16[128,1152]{1,0:T(8,128)(2,1)S(1)}, bf16[128,1152]{1,0:T(8,128)(2,1)S(1)}, u32[]{:S(2)}, u32[]{:S(2)}) collective-permute-start(bf16[128,1152]{1,0:T(8,128)(2,1)S(1)} %copy-done.51), channel_id=1, source_target_pairs={{0,4},{1,5},{2,6},{3,7},{4,0},{5,1},{6,2},{7,3},{8,12},{9,13},{10,... | collective-permute-start | bytes 884744 | tf_op jit(solution)/shard_map/ppermute | solution.py:556
  156.8 13.3 %collective-permute-start.49 = (bf16[128,1152]{1,0:T(8,128)(2,1)S(1)}, bf16[128,1152]{1,0:T(8,128)(2,1)S(1)}, u32[]{:S(2)}, u32[]{:S(2)}) collective-permute-start(bf16[128,1152]{1,0:T(8,128)(2,1)S(1)} %copy-done.51), channel_id=1, source_target_pairs={{0,2},{1,3},{2,0},{3,1},{4,6},{5,7},{6,4},{7,5},{8,10},{9,11},{10,... | collective-permute-start | bytes 884744 | tf_op jit(solution)/shard_map/ppermute | solution.py:556
  157.0 31.6 %collective-permute-start.57 = (bf16[432,768]{1,0:T(8,128)(2,1)S(1)}, bf16[432,768]{1,0:T(8,128)(2,1)S(1)}, u32[]{:S(2)}, u32[]{:S(2)}) collective-permute-start(bf16[432,768]{1,0:T(8,128)(2,1)S(1)} %add_convert_fusion), channel_id=1, source_target_pairs={{0,16},{8,24},{16,0},{24,8},{1,17},{9,25},{17,1},{25,9},{2,18},{10... | collective-permute-start | bytes 1990664 | tf_op jit(solution)/shard_map/ppermute | solution.py:560
  157.5 28.2 %collective-permute-start.56 = (bf16[432,768]{1,0:T(8,128)(2,1)S(1)}, bf16[432,768]{1,0:T(8,128)(2,1)S(1)}, u32[]{:S(2)}, u32[]{:S(2)}) collective-permute-start(bf16[432,768]{1,0:T(8,128)(2,1)S(1)} %copy-done.71), channel_id=1, source_target_pairs={{0,8},{8,0},{16,24},{24,16},{1,9},{9,1},{17,25},{25,17},{2,10},{10... | collective-permute-start | bytes 1990664 | tf_op jit(solution)/shard_map/ppermute | solution.py:560
  192.4 11.1 %collective-permute-start.58 = (bf16[4,128,1152]{2,1,0:T(8,128)(2,1)}, bf16[4,128,1152]{2,1,0:T(8,128)(2,1)}, u32[]{:S(2)}, u32[]{:S(2)}) collective-permute-start(bf16[4,128,1152]{2,1,0:T(8,128)(2,1)} %get-tuple-element.359), channel_id=1, source_target_pairs={{0,1},{1,0},{2,3},{3,2},{4,5},{5,4},{6,7},{7,6},{8,9},{9,8},{10,11... | collective-permute-start | bytes 3538952 | tf_op jit(solution)/shard_map/ppermute | solution.py:556
  192.4 10.0 %collective-permute-start.59 = (bf16[304,512]{1,0:T(8,128)(2,1)}, bf16[304,512]{1,0:T(8,128)(2,1)S(1)}, u32[]{:S(2)}, u32[]{:S(2)}) collective-permute-start(bf16[304,512]{1,0:T(8,128)(2,1)} %get-tuple-element.352), channel_id=1, source_target_pairs={{0,8},{8,0},{16,24},{24,16},{1,9},{9,1},{17,25},{25,17},{2,10},{10... | collective-permute-start | bytes 933896 | tf_op jit(solution)/shard_map/ppermute | solution.py:560
  192.4 19.4 %collective-permute-start.48 = (bf16[128,1152]{1,0:T(8,128)(2,1)}, bf16[128,1152]{1,0:T(8,128)(2,1)}, u32[]{:S(2)}, u32[]{:S(2)}) collective-permute-start(bf16[128,1152]{1,0:T(8,128)(2,1)} %get-tuple-element.422), channel_id=1, source_target_pairs={{0,6},{1,7},{2,4},{3,5},{4,2},{5,3},{6,0},{7,1},{8,14},{9,15},{10,... | collective-permute-start | bytes 884744 | tf_op jit(solution)/shard_map/ppermute | solution.py:556
  194.4 15.0 %collective-permute-start.47 = (bf16[128,1152]{1,0:T(8,128)(2,1)}, bf16[128,1152]{1,0:T(8,128)(2,1)}, u32[]{:S(2)}, u32[]{:S(2)}) collective-permute-start(bf16[128,1152]{1,0:T(8,128)(2,1)} %get-tuple-element.423), channel_id=1, source_target_pairs={{0,4},{1,5},{2,6},{3,7},{4,0},{5,1},{6,2},{7,3},{8,12},{9,13},{10,... | collective-permute-start | bytes 884744 | tf_op jit(solution)/shard_map/ppermute | solution.py:556
  195.7 16.2 %collective-permute-start.46 = (bf16[128,1152]{1,0:T(8,128)(2,1)}, bf16[128,1152]{1,0:T(8,128)(2,1)}, u32[]{:S(2)}, u32[]{:S(2)}) collective-permute-start(bf16[128,1152]{1,0:T(8,128)(2,1)} %get-tuple-element.424), channel_id=1, source_target_pairs={{0,2},{1,3},{2,0},{3,1},{4,6},{5,7},{6,4},{7,5},{8,10},{9,11},{10,... | collective-permute-start | bytes 884744 | tf_op jit(solution)/shard_map/ppermute | solution.py:556
  196.0 19.2 %all-to-all-start.1 = ((bf16[8,36,768]{2,1,0:T(8,128)(2,1)}), bf16[8,36,768]{2,1,0:T(8,128)(2,1)S(1)}, u32[]{:S(2)}, u32[]{:S(2)}) async-start(bf16[8,36,768]{2,1,0:T(8,128)(2,1)} %get-tuple-element.370), calls=%async_computation.1 | async-start | bytes 983040 | tf_op jit(solution)/shard_map/all_to_all | solution.py:1240
  202.4 16.6 %collective-permute-start.64 = (bf16[304,512]{1,0:T(8,128)(2,1)S(1)}, bf16[304,512]{1,0:T(8,128)(2,1)S(1)}, u32[]{:S(2)}, u32[]{:S(2)}) collective-permute-start(bf16[304,512]{1,0:T(8,128)(2,1)S(1)} %add_convert_fusion.1), channel_id=1, source_target_pairs={{0,16},{8,24},{16,0},{24,8},{1,17},{9,25},{17,1},{25,9},{2,18},{10... | collective-permute-start | bytes 933896 | tf_op jit(solution)/shard_map/ppermute | solution.py:560
  203.4 13.3 %collective-permute-start.63 = (bf16[304,512]{1,0:T(8,128)(2,1)S(1)}, bf16[304,512]{1,0:T(8,128)(2,1)S(1)}, u32[]{:S(2)}, u32[]{:S(2)}) collective-permute-start(bf16[304,512]{1,0:T(8,128)(2,1)S(1)} %copy-done.24), channel_id=1, source_target_pairs={{0,8},{8,0},{16,24},{24,16},{1,9},{9,1},{17,25},{25,17},{2,10},{10... | collective-permute-start | bytes 933896 | tf_op jit(solution)/shard_map/ppermute | solution.py:560
  209.4 17.8 %collective-permute-start.62 = (bf16[128,1152]{1,0:T(8,128)(2,1)}, bf16[128,1152]{1,0:T(8,128)(2,1)S(1)}, u32[]{:S(2)}, u32[]{:S(2)}) collective-permute-start(bf16[128,1152]{1,0:T(8,128)(2,1)} %get-tuple-element.421), channel_id=1, source_target_pairs={{0,6},{1,7},{2,4},{3,5},{4,2},{5,3},{6,0},{7,1},{8,14},{9,15},{10,... | collective-permute-start | bytes 884744 | tf_op jit(solution)/shard_map/ppermute | solution.py:556
  211.9 15.3 %collective-permute-start.61 = (bf16[128,1152]{1,0:T(8,128)(2,1)}, bf16[128,1152]{1,0:T(8,128)(2,1)S(1)}, u32[]{:S(2)}, u32[]{:S(2)}) collective-permute-start(bf16[128,1152]{1,0:T(8,128)(2,1)} %get-tuple-element.418), channel_id=1, source_target_pairs={{0,4},{1,5},{2,6},{3,7},{4,0},{5,1},{6,2},{7,3},{8,12},{9,13},{10,... | collective-permute-start | bytes 884744 | tf_op jit(solution)/shard_map/ppermute | solution.py:556
  213.2 14.0 %collective-permute-start.60 = (bf16[128,1152]{1,0:T(8,128)(2,1)}, bf16[128,1152]{1,0:T(8,128)(2,1)S(1)}, u32[]{:S(2)}, u32[]{:S(2)}) collective-permute-start(bf16[128,1152]{1,0:T(8,128)(2,1)} %get-tuple-element.419), channel_id=1, source_target_pairs={{0,2},{1,3},{2,0},{3,1},{4,6},{5,7},{6,4},{7,5},{8,10},{9,11},{10,... | collective-permute-start | bytes 884744 | tf_op jit(solution)/shard_map/ppermute | solution.py:556
  219.9 11.0 %all-to-all-start.2 = ((bf16[8,40,512]{2,1,0:T(8,128)(2,1)}), bf16[8,40,512]{2,1,0:T(8,128)(2,1)S(1)}, u32[]{:S(2)}, u32[]{:S(2)}) async-start(bf16[8,40,512]{2,1,0:T(8,128)(2,1)} %split_back.1), calls=%async_computation.2 | async-start | bytes 655360 | tf_op jit(solution)/shard_map/all_to_all | solution.py:1252
  (94 other events, 753.3 us)
